TPU v7x, 32 devices: a whole 2x2x4 slice. The times are simulated.
32 devices in a mesh: expert: 8 (over z, y), etp: 4 (over x, core).
Axes of the slice: x: 2, y: 2, z: 4, core: 2. Of those that a mesh axis runs over, the one named last changes fastest.
Arguments:
- tokens: bfloat16 [1024, 2048], P('expert'), may hold values from -6 to 6
- grad_out: bfloat16 [1024, 2048], P('expert'), may hold values from -6 to 6
- routes: int32 [1024, 8], P('expert'), may hold values from 0 to 15, all different within a row; in each aligned block of 128 rows (0 to 127, 128 to 255, ...) at most 80 rows name the same one
- probs: bfloat16 [1024, 8], P('expert'), may hold values from 0.049804688 to 0.3984375
- w_gate: bfloat16 [16, 768, 2048], P('expert', 'etp'), may hold values from -0.125 to 0.125
- w_up: bfloat16 [16, 768, 2048], P('expert', 'etp'), may hold values from -0.125 to 0.125
- w_down: bfloat16 [16, 768, 2048], P('expert', 'etp'), may hold values from -0.21875 to 0.21875
Outputs:
- grad_tokens: bfloat16 [1024, 2048], P('expert')
- grad_probs: bfloat16 [1024, 8], P('expert')
- grad_gate: bfloat16 [16, 768, 2048], P('expert', 'etp')
- grad_up: bfloat16 [16, 768, 2048], P('expert', 'etp')
- grad_down: bfloat16 [16, 768, 2048], P('expert', 'etp')
Inputs may be any that keep to these rules, and one draw needn't show every extreme that they name: `routes`: each row names 8 different experts. Among the 128 rows of one device no expert is named by more than 80 rows, a bound that some block reaches.
All inputs are finite; a program needn't handle non-finite values.
Results may differ from a plain program's by a relative error of at most 0.018.
Values may be sent and summed in bfloat16 or wider, within the bound.
No kernel may reach another device: no remote copies, remote signals or barrier semaphores. Data moves between devices by JAX's collectives and lax.ppermute only.
A program may use at most 128 MiB of HBM per device.

v0:
```python
import jax
import jax.numpy as jnp
from jax import lax
from jax.sharding import PartitionSpec as P


def token_sum(slot_rows, target, tok_rows, top_count):
    columns = slot_rows.shape[-1]
    picked = slot_rows.reshape(-1, columns)[target]
    return jnp.sum(picked.reshape(tok_rows, top_count, columns).astype(jnp.float32), axis=1).astype(
        jnp.bfloat16
    )


def expert_major(values, sources, local_experts, capacity):
    tail = values.shape[2:]
    shaped = values.reshape((sources, local_experts, capacity) + tail)
    order = (1, 0, 2) + tuple(range(3, 3 + len(tail)))
    return jnp.transpose(shaped, order).reshape((local_experts, sources * capacity) + tail)


def source_major(values, sources, local_experts, capacity):
    tail = values.shape[2:]
    shaped = values.reshape((local_experts, sources, capacity) + tail)
    order = (1, 0, 2) + tuple(range(3, 3 + len(tail)))
    return jnp.transpose(shaped, order).reshape((sources, local_experts * capacity) + tail)


def body(tokens, grad_out, routes, probs, w_gate, w_up, w_down):
    sources = lax.axis_size("expert")
    local_experts = w_gate.shape[0]
    hid_units = w_gate.shape[1]
    expert_count = sources * local_experts
    tok_rows, top_count = routes.shape
    model_width = tokens.shape[1]
    capacity = max(2, 5 * tok_rows * top_count // (4 * expert_count))
    pair_count = tok_rows * top_count
    flat_routes = routes.reshape(-1)
    one_hot = (flat_routes[:, None] == jnp.arange(expert_count, dtype=jnp.int32)[None, :]).astype(
        jnp.int32
    )
    slot_rank = jnp.sum(jnp.cumsum(one_hot, axis=0) * one_hot, axis=1) - 1
    target = flat_routes * capacity + slot_rank
    slot_table = (
        jnp.full((expert_count * capacity,), pair_count, jnp.int32)
        .at[target]
        .set(jnp.arange(pair_count, dtype=jnp.int32))
    )
    filled = slot_table < pair_count
    safe_index = jnp.where(filled, slot_table, 0)
    token_of = safe_index // top_count
    block_rows = local_experts * capacity
    send_prob = jnp.where(filled, probs.reshape(-1)[safe_index], 0).reshape(sources, block_rows)
    send_rows = jnp.where(filled[:, None], tokens[token_of], 0).reshape(
        sources, block_rows, model_width
    )
    send_grad = jnp.where(filled[:, None], grad_out[token_of], 0).reshape(
        sources, block_rows, model_width
    )
    recv_rows, recv_grad, recv_prob = (
        lax.all_to_all(send_rows, "expert", split_axis=0, concat_axis=0, tiled=True),
        lax.all_to_all(send_grad, "expert", split_axis=0, concat_axis=0, tiled=True),
        lax.all_to_all(send_prob, "expert", split_axis=0, concat_axis=0, tiled=True),
    )
    in_rows = expert_major(recv_rows, sources, local_experts, capacity)
    in_grad = expert_major(recv_grad, sources, local_experts, capacity)
    weight = expert_major(recv_prob, sources, local_experts, capacity).astype(jnp.float32)[
        ..., None
    ]
    gate_up = jnp.concatenate([w_gate, w_up], axis=1)
    both_pre = jnp.einsum("end,ehd->enh", in_rows, gate_up, preferred_element_type=jnp.float32)
    pre_gate = both_pre[..., :hid_units]
    pre_up = both_pre[..., hid_units:]
    back_grad = jnp.einsum("end,ehd->enh", in_grad, w_down, preferred_element_type=jnp.float32)
    sigma_gate = jax.nn.sigmoid(pre_gate)
    activated = pre_gate * sigma_gate
    hidden = (activated * pre_up).astype(jnp.bfloat16)
    prob_local = jnp.sum(hidden.astype(jnp.float32) * back_grad, axis=-1)
    prob_part = source_major(prob_local, sources, local_experts, capacity)
    scaled = (weight * in_grad.astype(jnp.float32)).astype(jnp.bfloat16)
    grad_down = jnp.einsum(
        "enh,end->ehd", hidden, scaled, preferred_element_type=jnp.float32
    ).astype(jnp.bfloat16)
    hidden_grad = weight * back_grad
    d_gate = (hidden_grad * pre_up * sigma_gate * (1.0 + pre_gate * (1.0 - sigma_gate))).astype(
        jnp.bfloat16
    )
    d_up = (hidden_grad * activated).astype(jnp.bfloat16)
    d_both = jnp.concatenate([d_gate, d_up], axis=-1)
    grad_both = jnp.einsum(
        "enh,end->ehd", d_both, in_rows, preferred_element_type=jnp.float32
    ).astype(jnp.bfloat16)
    grad_gate = grad_both[:, :hid_units]
    grad_up = grad_both[:, hid_units:]
    local_part = jnp.einsum(
        "enh,ehd->end", d_both, gate_up, preferred_element_type=jnp.float32
    ).astype(jnp.bfloat16)
    partial_sum = source_major(local_part, sources, local_experts, capacity).astype(jnp.float32)
    totals, prob_total = (
        lax.psum(partial_sum.astype(jnp.bfloat16), "etp").astype(jnp.float32),
        lax.psum(prob_part.astype(jnp.bfloat16), "etp").astype(jnp.float32),
    )
    back_rows, back_prob = (
        lax.all_to_all(
            totals.astype(jnp.bfloat16), "expert", split_axis=0, concat_axis=0, tiled=True
        ),
        lax.all_to_all(
            prob_total.astype(jnp.bfloat16), "expert", split_axis=0, concat_axis=0, tiled=True
        ),
    )
    grad_tokens = token_sum(back_rows, target, tok_rows, top_count)
    grad_probs = back_prob.reshape(-1)[target].reshape(tok_rows, top_count)
    return (grad_tokens, grad_probs, grad_gate, grad_up, grad_down)


def solution(mesh):
    return jax.shard_map(
        body,
        mesh=mesh,
        in_specs=(
            P("expert", None),
            P("expert", None),
            P("expert", None),
            P("expert", None),
            P("expert", "etp", None),
            P("expert", "etp", None),
            P("expert", "etp", None),
        ),
        out_specs=(
            P("expert", None),
            P("expert", None),
            P("expert", "etp", None),
            P("expert", "etp", None),
            P("expert", "etp", None),
        ),
        check_vma=False,
    )
```

profile of v0, /device:TPU:0, one launch (start us, length us, event | category | flops | bytes accessed | tf_op | source)
XLA Modules:
  0.0 562.9 jit_solution(11726583092587561487)
XLA Ops:
  9.0 4.5 reduce-window.6
  14.2 4.3 scatter_custom_fusion
  19.5 8.0 %gather_fusion = bf16[1280]{0:T(1024)(128)(2,1)S(1)} fusion(bf16[1024]{0:T(1024)(128)(2,1)S(1)} %reshape.132, s32[2048]{0:T(1024)S(1)} %pad_clamp_fusion.1), kind=kCustom, calls=%fused_computation | custom fusion | bytes 10240 | tf_op jit(solution)/shard_map/gather | solution.py:53
  28.2 7.3 %all-to-all-start = ((bf16[8,1,160]{2,1,0:T(2,128)(2,1)}), bf16[8,1,160]{2,1,0:T(2,128)(2,1)S(1)}, u32[]{:S(2)}, u32[]{:S(2)}) async-start(bf16[8,1,160]{2,1,0:T(2,128)(2,1)} %all_to_all.28), calls=%async_computation | async-start | bytes 16384 | tf_op jit(solution)/shard_map/all_to_all | solution.py:63
  35.6 6.2 %gather_fusion.1 = bf16[1280,2048]{1,0:T(8,128)(2,1)} fusion(bf16[128,2048]{1,0:T(8,128)(2,1)S(1)} %copy-done.1, s32[2048]{0:T(1024)S(1)} %pad_clamp_fusion), kind=kCustom, calls=%fused_computation.1 | custom fusion | bytes 10490880 | tf_op jit(solution)/shard_map/gather | solution.py:57
  41.8 6.2 %gather_fusion.2 = bf16[1280,2048]{1,0:T(8,128)(2,1)} fusion(bf16[128,2048]{1,0:T(8,128)(2,1)S(1)} %copy-done.2, s32[2048]{0:T(1024)S(1)} %pad_clamp_fusion), kind=kCustom, calls=%fused_computation.2 | custom fusion | bytes 10490880 | tf_op jit(solution)/shard_map/gather | solution.py:54
  47.9 8.8 %broadcast_select_fusion = (bf16[8,160,2048]{2,1,0:T(8,128)(2,1)}, bf16[8,160,2048]{2,1,0:T(8,128)(2,1)}) fusion(bf16[8,160,2048]{2,1,0:T(8,128)(2,1)} %bitcast.45, pred[8,160]{1,0:T(8,128)(4,1)S(1)} %broadcast_in_dim.43, bf16[8,160,2048]{2,1,0:T(8,128)(2,1)} %bitcast.44), kind=kLoop, calls=%fused_computation.9 | loop fusion | flops 5242880 | bytes 20972800 | tf_op jit(solution)/shard_map/jit(_where)/select_n | solution.py:54
  56.7 121.4 %all_to_all.34 = bf16[8,160,2048]{2,1,0:T(8,128)(2,1)} all-to-all(bf16[8,160,2048]{2,1,0:T(8,128)(2,1)} %get-tuple-element.30), channel_id=1, replica_groups=mesh['expert'=8,'etp'=4] {'expert'}, dimensions={0} | all-to-all | bytes 10485760 | tf_op jit(solution)/shard_map/all_to_all | solution.py:61
  178.2 4.8 all-to-all-start.1
  186.7 5.7 %copy.48 = bf16[2,8,80,2048]{3,2,1,0:T(8,128)(2,1)} copy(bf16[2,8,80,2048]{3,2,0,1:T(8,128)(2,1)} %bitcast.42) | data formatting | bytes 10485760 | tf_op jit(solution)/shard_map/transpose | solution.py:19
  192.4 105.2 %all-to-all-done.1 = bf16[8,160,2048]{2,1,0:T(8,128)(2,1)} async-done(((bf16[8,160,2048]{2,1,0:T(8,128)(2,1)}), bf16[8,160,2048]{2,1,0:T(8,128)(2,1)}, u32[]{:S(2)}, u32[]{:S(2)}) %all-to-all-start.1) | async-done | bytes 5242912 | tf_op jit(solution)/shard_map/all_to_all | solution.py:62
  297.6 3.1 copy.47
  301.6 2.9 copy-done.8
  309.4 3.2 convolution_convert_fusion
  315.6 5.6 %psum.15 = bf16[8,1,160]{2,0,1:T(8,128)(2,1)S(1)} all-reduce(bf16[8,1,160]{2,0,1:T(8,128)(2,1)S(1)} %all_to_all.26), channel_id=1, replica_groups=mesh['expert'=8,'etp'=4] {'etp'}, use_global_device_ids=true, to_apply=%region_7.8 | all-reduce | flops 1280 | bytes 5120 | tf_op jit(solution)/shard_map/psum | solution.py:101
  321.3 11.1 %all_to_all.35 = bf16[8,1,160]{2,1,0:T(2,128)(2,1)S(1)} all-to-all(bf16[8,1,160]{2,1,0:T(2,128)(2,1)S(1)} %copy.52), channel_id=1, replica_groups=mesh['expert'=8,'etp'=4] {'expert'}, dimensions={0} | all-to-all | bytes 5120 | tf_op jit(solution)/shard_map/all_to_all | solution.py:107
  332.4 84.8 %all-reduce.2.cloned.1.call-done = bf16[8,160,2048]{2,1,0:T(8,128)(2,1)} async-done(((bf16[8,160,2048]{2,1,0:T(8,128)(2,1)}), bf16[8,160,2048]{2,1,0:T(8,128)(2,1)}) %all-reduce.2.cloned.1.call-update) | async-done | bytes 5242896 | tf_op jit(solution)/shard_map/psum | solution.py:100
  417.1 5.5 all-to-all-start.3
  422.7 5.2 fusion.2
  427.9 5.6 convolution_convert_fusion.1
  435.5 6.8 %gather_fusion.4 = bf16[1024]{0:T(1024)(128)(2,1)S(1)} fusion(bf16[1280]{0:T(1024)(128)(2,1)S(1)} %reshape.141, s32[1024]{0:T(1024)S(1)} %broadcast_clamp_fusion), kind=kCustom, calls=%fused_computation.4 | custom fusion | bytes 8192 | tf_op jit(solution)/shard_map/gather | solution.py:112
  443.0 95.2 %all-to-all-done.3 = bf16[8,160,2048]{2,1,0:T(8,128)(2,1)} async-done(((bf16[8,160,2048]{2,1,0:T(8,128)(2,1)}), bf16[8,160,2048]{2,1,0:T(8,128)(2,1)}, u32[]{:S(2)}, u32[]{:S(2)}) %all-to-all-start.3) | async-done | bytes 5242912 | tf_op jit(solution)/shard_map/all_to_all | solution.py:104
  538.2 12.0 %gather_fusion.3 = bf16[1024,2048]{1,0:T(8,128)(2,1)} fusion(bf16[1280,2048]{1,0:T(8,128)(2,1)} %bitcast.16, s32[1024]{0:T(1024)S(1)} %broadcast_clamp_fusion), kind=kCustom, calls=%fused_computation.3 | custom fusion | bytes 8392704 | tf_op jit(solution)/shard_map/gather | solution.py:9
  550.2 5.9 %bitcast_reduce_fusion = bf16[128,2048]{1,0:T(8,128)(2,1)} fusion(bf16[1024,2048]{1,0:T(8,128)(2,1)} %gather_fusion.3), kind=kLoop, calls=%fused_computation.11 | loop fusion | flops 1835008 | bytes 4718592 | tf_op jit(solution)/shard_map/reduce_sum | solution.py:10
  (65 shorter events, 19.4 us)
Async XLA Ops:
  7.2 300.0 %copy-start = (bf16[2,192,2048]{2,1,0:T(8,128)(2,1)S(1)}, bf16[2,192,2048]{2,1,0:T(8,128)(2,1)}, u32[]{:S(2)}) copy-start(bf16[2,192,2048]{2,1,0:T(8,128)(2,1)} %param.13) | copy-start | bytes 4718596
  7.2 28.4 %copy-start.1 = (bf16[128,2048]{1,0:T(8,128)(2,1)S(1)}, bf16[128,2048]{1,0:T(8,128)(2,1)}, u32[]{:S(2)}) copy-start(bf16[128,2048]{1,0:T(8,128)(2,1)} %param.8) | copy-start | bytes 1572868
  28.2 28.6 %all-to-all-start = ((bf16[8,1,160]{2,1,0:T(2,128)(2,1)}), bf16[8,1,160]{2,1,0:T(2,128)(2,1)S(1)}, u32[]{:S(2)}, u32[]{:S(2)}) async-start(bf16[8,1,160]{2,1,0:T(2,128)(2,1)} %all_to_all.28), calls=%async_computation | async-start | bytes 16384 | tf_op jit(solution)/shard_map/all_to_all | solution.py:63
  35.6 6.2 %copy-start.2 = (bf16[128,2048]{1,0:T(8,128)(2,1)S(1)}, bf16[128,2048]{1,0:T(8,128)(2,1)}, u32[]{:S(2)}) copy-start(bf16[128,2048]{1,0:T(8,128)(2,1)} %param.7) | copy-start | bytes 1572868
  178.2 5.0 copy-start.5
  178.2 119.4 %all-to-all-start.1 = ((bf16[8,160,2048]{2,1,0:T(8,128)(2,1)}), bf16[8,160,2048]{2,1,0:T(8,128)(2,1)}, u32[]{:S(2)}, u32[]{:S(2)}) async-start(bf16[8,160,2048]{2,1,0:T(8,128)(2,1)} %get-tuple-element.31), calls=%async_computation.1 | async-start | bytes 10485760 | tf_op jit(solution)/shard_map/all_to_all | solution.py:62
  183.0 234.2 %all-reduce.2.cloned.1.call-start = ((), (), s32[]{:S(2)}) async-start(), calls=%async_computation.5 | async-start | bytes 10485760 | tf_op jit(solution)/shard_map/psum | solution.py:100
  183.2 1.4 copy-start.6
  184.8 1.7 copy-start.7
  297.6 4.0 copy-start.3
  297.6 6.9 %copy-start.8 = (bf16[2,384,2048]{2,1,0:T(8,128)(2,1)S(1)}, bf16[2,384,2048]{2,1,0:T(8,128)(2,1)}, u32[]{:S(2)}) copy-start(bf16[2,384,2048]{2,1,0:T(8,128)(2,1)} %copy-done.7) | copy-start | bytes 9437188
  300.7 6.4 %copy-start.4 = (bf16[2,8,80,2048]{3,2,1,0:T(8,128)(2,1)}, bf16[2,8,80,2048]{3,2,1,0:T(8,128)(2,1)S(1)}, u32[]{:S(2)}) copy-start(bf16[2,8,80,2048]{3,2,1,0:T(8,128)(2,1)S(1)} %copy.47) | copy-start | bytes 15728644
  417.1 121.1 %all-to-all-start.3 = ((bf16[8,160,2048]{2,1,0:T(8,128)(2,1)}), bf16[8,160,2048]{2,1,0:T(8,128)(2,1)}, u32[]{:S(2)}, u32[]{:S(2)}) async-start(bf16[8,160,2048]{2,1,0:T(8,128)(2,1)} %all-reduce.2.cloned.1.call-done), calls=%async_computation.3 | async-start | bytes 10485760 | tf_op jit(solution)/shard_map/all_to_all | solution.py:104
Sparse Core Ops, SparseCore 0:
  315.5 101.5 all-reduce.1
where the time goes:
time: 564 us; the launch traced here: 563 us
  waiting for transfers between devices  285 us (51%)
  blocking collectives  138 us (24%)
  local copies, waits for them, and re-layouts  68.4 us (12%)
  other arithmetic  20.2 us (4%)
  matrix products  18.9 us (3%)
  starting transfers between devices  17.8 us (3%)
  between operations  14.3 us (3%)
    all_to_all x1, blocking collectives, body(): lax.all_to_all(send_rows, 'expert', split_axis=0, concat_axis=0, tiled=True)  121 us
    all_to_all x1, waiting for transfers between devices, body(): lax.all_to_all(send_grad, 'expert', split_axis=0, concat_axis=0, tiled=True)  105 us
    all_to_all x1, waiting for transfers between devices, body(): lax.all_to_all(totals.astype(jnp.bfloat16), 'expert', split_axis=0, conca...  95.2 us
    psum x1, waiting for transfers between devices, body(): lax.psum(partial_sum.astype(jnp.bfloat16), 'etp').astype(jnp.float32)  84.8 us
    gather x1, local copies, waits for them, and re-layouts, token_sum(): picked = slot_rows.reshape(-1, columns)[target]  12 us
  transfers between devices with their start and end apart: 4, of which 3 were waited for; matrix products, arithmetic and copies ran while one was open for 9% of the time, Pallas kernels for 0%

commit v1 on v0

v1 whole, which is shorter than its diff:
```python
import functools

import jax
import jax.numpy as jnp
from jax import lax
from jax.experimental import pallas as pl
from jax.experimental.pallas import tpu as pltpu
from jax.sharding import PartitionSpec as P

BF16 = jnp.bfloat16
F32 = jnp.float32
LANES = 128
VMEM_BYTES = 48 * 1024 * 1024


def token_sum(slot_rows, target, tok_rows, top_count):
    columns = slot_rows.shape[-1]
    picked = slot_rows.reshape(-1, columns)[target]
    return jnp.sum(picked.reshape(tok_rows, top_count, columns).astype(F32), axis=1).astype(BF16)


def expert_major(values, sources, local_experts, capacity):
    tail = values.shape[2:]
    shaped = values.reshape((sources, local_experts, capacity) + tail)
    order = (1, 0, 2) + tuple(range(3, 3 + len(tail)))
    return jnp.transpose(shaped, order).reshape((local_experts, sources * capacity) + tail)


def source_major(values, sources, local_experts, capacity):
    tail = values.shape[2:]
    shaped = values.reshape((local_experts, sources, capacity) + tail)
    order = (1, 0, 2) + tuple(range(3, 3 + len(tail)))
    return jnp.transpose(shaped, order).reshape((sources, local_experts * capacity) + tail)


def slots_of(tok_rows, top_count, expert_count):
    return max(2, 5 * tok_rows * top_count // (4 * expert_count))


def routed_body(tokens, grad_out, routes, probs, w_gate, w_up, w_down):
    sources = lax.axis_size("expert")
    local_experts = w_gate.shape[0]
    hid_units = w_gate.shape[1]
    expert_count = sources * local_experts
    tok_rows, top_count = routes.shape
    model_width = tokens.shape[1]
    capacity = slots_of(tok_rows, top_count, expert_count)
    pair_count = tok_rows * top_count
    flat_routes = routes.reshape(-1)
    one_hot = (flat_routes[:, None] == jnp.arange(expert_count, dtype=jnp.int32)[None, :]).astype(
        jnp.int32
    )
    slot_rank = jnp.sum(jnp.cumsum(one_hot, axis=0) * one_hot, axis=1) - 1
    target = flat_routes * capacity + slot_rank
    slot_table = (
        jnp.full((expert_count * capacity,), pair_count, jnp.int32)
        .at[target]
        .set(jnp.arange(pair_count, dtype=jnp.int32))
    )
    filled = slot_table < pair_count
    safe_index = jnp.where(filled, slot_table, 0)
    token_of = safe_index // top_count
    block_rows = local_experts * capacity
    send_prob = jnp.where(filled, probs.reshape(-1)[safe_index], 0).reshape(sources, block_rows)
    send_rows = jnp.where(filled[:, None], tokens[token_of], 0).reshape(
        sources, block_rows, model_width
    )
    send_grad = jnp.where(filled[:, None], grad_out[token_of], 0).reshape(
        sources, block_rows, model_width
    )
    recv_rows, recv_grad, recv_prob = (
        lax.all_to_all(send_rows, "expert", split_axis=0, concat_axis=0, tiled=True),
        lax.all_to_all(send_grad, "expert", split_axis=0, concat_axis=0, tiled=True),
        lax.all_to_all(send_prob, "expert", split_axis=0, concat_axis=0, tiled=True),
    )
    in_rows = expert_major(recv_rows, sources, local_experts, capacity)
    in_grad = expert_major(recv_grad, sources, local_experts, capacity)
    weight = expert_major(recv_prob, sources, local_experts, capacity).astype(F32)[..., None]
    gate_up = jnp.concatenate([w_gate, w_up], axis=1)
    both_pre = jnp.einsum("end,ehd->enh", in_rows, gate_up, preferred_element_type=F32)
    pre_gate = both_pre[..., :hid_units]
    pre_up = both_pre[..., hid_units:]
    back_grad = jnp.einsum("end,ehd->enh", in_grad, w_down, preferred_element_type=F32)
    sigma_gate = jax.nn.sigmoid(pre_gate)
    activated = pre_gate * sigma_gate
    hidden = (activated * pre_up).astype(BF16)
    prob_local = jnp.sum(hidden.astype(F32) * back_grad, axis=-1)
    prob_part = source_major(prob_local, sources, local_experts, capacity)
    scaled = (weight * in_grad.astype(F32)).astype(BF16)
    grad_down = jnp.einsum("enh,end->ehd", hidden, scaled, preferred_element_type=F32).astype(BF16)
    hidden_grad = weight * back_grad
    d_gate = (hidden_grad * pre_up * sigma_gate * (1.0 + pre_gate * (1.0 - sigma_gate))).astype(
        BF16
    )
    d_up = (hidden_grad * activated).astype(BF16)
    d_both = jnp.concatenate([d_gate, d_up], axis=-1)
    grad_both = jnp.einsum("enh,end->ehd", d_both, in_rows, preferred_element_type=F32).astype(BF16)
    grad_gate = grad_both[:, :hid_units]
    grad_up = grad_both[:, hid_units:]
    local_part = jnp.einsum("enh,ehd->end", d_both, gate_up, preferred_element_type=F32).astype(
        BF16
    )
    partial_sum = source_major(local_part, sources, local_experts, capacity).astype(F32)
    totals, prob_total = (
        lax.psum(partial_sum.astype(BF16), "etp").astype(F32),
        lax.psum(prob_part.astype(BF16), "etp").astype(F32),
    )
    back_rows, back_prob = (
        lax.all_to_all(totals.astype(BF16), "expert", split_axis=0, concat_axis=0, tiled=True),
        lax.all_to_all(prob_total.astype(BF16), "expert", split_axis=0, concat_axis=0, tiled=True),
    )
    grad_tokens = token_sum(back_rows, target, tok_rows, top_count)
    grad_probs = back_prob.reshape(-1)[target].reshape(tok_rows, top_count)
    return (grad_tokens, grad_probs, grad_gate, grad_up, grad_down)


def stage_kernel(local_experts, base_ref, *refs):
    (*chunks, gate_up, down, keep, send, rows, d_both, hid) = refs
    width = down.shape[1]
    units = down.shape[0]
    each = units // local_experts
    step = chunks[0].shape[0]
    for i, chunk in enumerate(chunks):
        rows[i * step : (i + 1) * step, :] = chunk[...]
    count = rows.shape[0]
    nt = (((1,), (1,)), ((), ()))
    pre = lax.dot_general(rows[:, :width], gate_up[...], nt, preferred_element_type=F32)
    back = lax.dot_general(rows[:, width : 2 * width], down[...], nt, preferred_element_type=F32)
    extra = rows[:, 2 * width :].astype(F32)
    lane = lax.broadcasted_iota(jnp.int32, extra.shape, 1)
    unit = lax.broadcasted_iota(jnp.int32, (count, units), 1)
    weight = jnp.zeros((count, units), F32)
    for e in range(local_experts):
        own = jnp.sum(jnp.where(lane == base_ref[0] + e, extra, 0.0), axis=1, keepdims=True)
        weight = jnp.where((unit >= e * each) & (unit < (e + 1) * each), own, weight)
    pre_gate = pre[:, :units]
    pre_up = pre[:, units:]
    sigma = 1.0 / (1.0 + jnp.exp(-pre_gate))
    activated = pre_gate * sigma
    hidden = (activated * pre_up).astype(BF16).astype(F32)
    product = hidden * back
    found = jnp.zeros(extra.shape, F32)
    for e in range(local_experts):
        mine = (unit >= e * each) & (unit < (e + 1) * each)
        own = jnp.sum(jnp.where(mine, product, 0.0), axis=1, keepdims=True)
        found = jnp.where(lane == base_ref[0] + e, own, found)
    hid[...] = (hidden * weight).astype(BF16)
    hidden_grad = weight * back
    d_both[:, :units] = (
        hidden_grad * pre_up * sigma * (1.0 + pre_gate * (1.0 - sigma))
    ).astype(BF16)
    d_both[:, units:] = (hidden_grad * activated).astype(BF16)
    part = jnp.dot(d_both[...], gate_up[...], preferred_element_type=F32).astype(BF16)
    half = count // 2
    keep[:, :width] = part[:half]
    send[:, :width] = part[half:]
    keep[:, width:] = found[:half].astype(BF16)
    send[:, width:] = found[half:].astype(BF16)


def stage(base, chunks, gate_up, down, local_experts):
    units, width = down.shape
    step, columns = chunks[0].shape
    count = step * len(chunks)
    extra = columns - 2 * width
    flops = 2 * count * width * (2 * units + units + 2 * units)
    return pl.pallas_call(
        functools.partial(stage_kernel, local_experts),
        out_shape=(
            jax.ShapeDtypeStruct((count // 2, width + extra), BF16),
            jax.ShapeDtypeStruct((count // 2, width + extra), BF16),
            jax.ShapeDtypeStruct((count, columns), BF16),
            jax.ShapeDtypeStruct((count, 2 * units), BF16),
            jax.ShapeDtypeStruct((count, units), BF16),
        ),
        in_specs=[pl.BlockSpec(memory_space=pltpu.SMEM)]
        + [pl.BlockSpec(memory_space=pltpu.VMEM)] * (len(chunks) + 2),
        out_specs=(pl.BlockSpec(memory_space=pltpu.VMEM),) * 5,
        compiler_params=pltpu.CompilerParams(vmem_limit_bytes=VMEM_BYTES),
        cost_estimate=pl.CostEstimate(
            flops=flops, bytes_accessed=4 * count * columns, transcendentals=count * units
        ),
        name="stage",
    )(base, *chunks, gate_up, down)


def weights_kernel(stages, *refs):
    ins = refs[: 4 * stages]
    gate, up, down = refs[4 * stages :]
    units = gate.shape[0]
    tn = (((0,), (0,)), ((), ()))
    both = 0.0
    below = 0.0
    for s in range(stages):
        x, o, d_both, hid = ins[4 * s : 4 * s + 4]
        both = both + lax.dot_general(d_both[...], x[...], tn, preferred_element_type=F32)
        below = below + lax.dot_general(hid[...], o[...], tn, preferred_element_type=F32)
    gate[...] = both[:units].astype(BF16)
    up[...] = both[units:].astype(BF16)
    down[...] = below.astype(BF16)


def weight_grads(parts, width, units):
    tile = 256
    tiles = width // tile
    specs, operands, total = [], [], 0
    for rows, d_both, hid in parts:
        count = rows.shape[0]
        total += count
        specs += [
            pl.BlockSpec((count, tile), lambda j: (0, j)),
            pl.BlockSpec((count, tile), lambda j: (0, j + tiles)),
            pl.BlockSpec(d_both.shape, lambda j: (0, 0)),
            pl.BlockSpec(hid.shape, lambda j: (0, 0)),
        ]
        operands += [rows, rows, d_both, hid]
    return pl.pallas_call(
        functools.partial(weights_kernel, len(parts)),
        grid=(tiles,),
        out_shape=(jax.ShapeDtypeStruct((units, width), BF16),) * 3,
        in_specs=specs,
        out_specs=(pl.BlockSpec((units, tile), lambda j: (0, j)),) * 3,
        compiler_params=pltpu.CompilerParams(vmem_limit_bytes=VMEM_BYTES),
        cost_estimate=pl.CostEstimate(
            flops=2 * total * width * 3 * units,
            bytes_accessed=4 * total * width + 6 * units * width,
            transcendentals=0,
        ),
        name="weight_grads",
    )(*operands)


def gathered_body(lines, tokens, grad_out, routes, probs, w_gate, w_up, w_down):
    axes = ("expert", "etp")
    local_experts, hid_units, width = w_gate.shape
    expert_count = 2 * lines * local_experts
    units = local_experts * hid_units
    tok_rows, top_count = routes.shape
    step = tok_rows // 4
    expert, etp = lax.axis_index("expert"), lax.axis_index("etp")
    side, core = etp // 2, etp % 2

    order = list(range(0, lines, 2)) + list(range(1, lines, 2))[::-1]
    after = {order[i]: order[(i + 1) % lines] for i in range(lines)}
    places = [
        (z, y, x, c) for z in range(lines) for y in range(2) for x in range(2) for c in range(2)
    ]

    def number(z, y, x, c):
        return ((z * 2 + y) * 2 + x) * 2 + c

    ring = [(number(z, y, x, c), number(after[z], y, x, c)) for z, y, x, c in places]
    over_y = [(number(z, y, x, c), number(z, 1 - y, x, c)) for z, y, x, c in places]
    over_x = [(number(z, y, x, c), number(z, y, 1 - x, c)) for z, y, x, c in places]
    over_c = [(number(z, y, x, c), number(z, y, x, 1 - c)) for z, y, x, c in places]

    def move(value, pairs):
        return lax.ppermute(value, axes, pairs)

    extra = -(-expert_count // LANES) * LANES
    named = routes[:, :, None] == jnp.arange(extra, dtype=jnp.int32)
    dense = jnp.sum(jnp.where(named, probs[:, :, None], 0).astype(F32), axis=1).astype(BF16)
    block = jnp.concatenate([tokens, grad_out, dense], axis=1).reshape(4, step, -1)

    def quarter(x, c):
        return lax.dynamic_index_in_dim(block, 2 * x + c, 0, keepdims=False)

    here = quarter(side, core)
    gate_up = jnp.concatenate([w_gate.reshape(units, width), w_up.reshape(units, width)], axis=0)
    down = w_down.reshape(units, width)
    base = (expert * local_experts).astype(jnp.int32).reshape(1)

    line = [here]
    for s in range(1, lines):
        line.append(move(line[-1], ring))
    other = [move(v, over_y) for v in line]
    line_x = [quarter(1 - side, core)] + [move(v, over_x) for v in line[1:]]
    other_x = [move(v, over_x) for v in other]
    parts, sums = [], []
    for s in range(lines):
        mine = [line[s], line_x[s], other[s], other_x[s]]
        if s == 0:
            theirs = [quarter(side, 1 - core), quarter(1 - side, 1 - core)] + [
                move(v, over_c) for v in mine[2:]
            ]
        else:
            theirs = [move(v, over_c) for v in mine]
        keep, send, rows, d_both, hid = stage(base, mine + theirs, gate_up, down, local_experts)
        parts.append((rows, d_both, hid))
        chip = keep.astype(F32) + move(send, over_c).astype(F32)
        far = move(chip[2 * step :].astype(BF16), over_y)
        sums.append(chip[: 2 * step] + far.astype(F32))
    total = sums[1]
    for s in list(range(2, lines)) + [0]:
        total = sums[s] + move(total.astype(BF16), ring).astype(F32)
    total = total.astype(BF16)
    cross = move(total, over_x)
    final = (
        total.astype(F32) + jnp.concatenate([cross[step:], cross[:step]], axis=0).astype(F32)
    ).astype(BF16)
    beside = move(final, over_c)
    grad_gate, grad_up, grad_down = weight_grads(parts, width, units)

    pair = jnp.stack([final, beside]).reshape(2, 2, step, -1)
    pair = jnp.where(core == 0, pair, pair[::-1])
    pair = jnp.where(side == 0, pair, pair[:, ::-1])
    whole = jnp.transpose(pair, (1, 0, 2, 3)).reshape(tok_rows, -1)
    grad_tokens = whole[:, :width]
    found = whole[:, None, width:]
    grad_probs = jnp.sum(jnp.where(named, found, 0).astype(F32), axis=2).astype(BF16)
    shape = w_gate.shape
    return (
        grad_tokens,
        grad_probs,
        grad_gate.reshape(shape),
        grad_up.reshape(shape),
        grad_down.reshape(shape),
    )


def body(sources, splits, tokens, grad_out, routes, probs, w_gate, w_up, w_down):
    tok_rows, top_count = routes.shape
    local_experts = w_gate.shape[0]
    slots = local_experts * slots_of(tok_rows, top_count, sources * local_experts)
    fits = splits == 4 and sources % 2 == 0 and sources >= 4 and tok_rows % 64 == 0
    args = (tokens, grad_out, routes, probs, w_gate, w_up, w_down)
    if fits and slots >= tok_rows:
        return gathered_body(sources // 2, *args)
    return routed_body(*args)


def solution(mesh):
    return jax.shard_map(
        functools.partial(body, mesh.shape["expert"], mesh.shape["etp"]),
        mesh=mesh,
        in_specs=(
            P("expert", None),
            P("expert", None),
            P("expert", None),
            P("expert", None),
            P("expert", "etp", None),
            P("expert", "etp", None),
            P("expert", "etp", None),
        ),
        out_specs=(
            P("expert", None),
            P("expert", None),
            P("expert", "etp", None),
            P("expert", "etp", None),
            P("expert", "etp", None),
        ),
        check_vma=False,
    )
```

time: 564 us -> 149 us (0.26)
  waiting for transfers between devices: 285 us -> 41.4 us
  blocking collectives: 138 us -> 0 us
  local copies, waits for them, and re-layouts: 68.4 us -> 21.8 us
  Pallas kernels: 0 us -> 35.1 us
  starting transfers between devices: 17.8 us -> 41.9 us
  matrix products: 18.9 us -> 0 us
  other arithmetic: 20.2 us -> 6.93 us
  between operations: 14.3 us -> 1.05 us
    all_to_all x3 -> x0, waiting for transfers between devices: 200 us -> none  [the longest x1 105 us: body(): lax.all_to_all(send_grad, 'expert', split_axis=0, concat_axis=0, tiled=True)]
    all_to_all x2 -> x0, blocking collectives: 133 us -> none  [the longest x1 121 us: body(): lax.all_to_all(send_rows, 'expert', split_axis=0, concat_axis=0, tiled=True)]
    psum x1 -> x0, waiting for transfers between devices: 84.8 us -> none  [body(): lax.psum(partial_sum.astype(jnp.bfloat16), 'etp').astype(jnp.float32)]
    ppermute x0 -> x41, starting transfers between devices: none -> 41.9 us  [move(): return lax.ppermute(value, axes, pairs)]
    ppermute x0 -> x41, waiting for transfers between devices: none -> 41.4 us  [move(): return lax.ppermute(value, axes, pairs)]
    gather x5 -> x0, local copies, waits for them, and re-layouts: 39.1 us -> none  [the longest x1 12 us: token_sum(): picked = slot_rows.reshape(-1, columns)[target]]
    pallas_call x0 -> x5, Pallas kernels: none -> 35.1 us  [the longest x4 24.8 us: stage(): pl.pallas_call(functools.partial(stage_kernel, local_experts), out_shape=...]
    dot_general x5 -> x0, matrix products: 18.9 us -> none  [the longest x1 5.6 us: body(): jnp.einsum('enh,end->ehd', d_both, in_rows, preferred_element_type=jnp.fl...]
  transfers between devices with their start and end apart: 4 -> 41, of which waited for: 3 -> 13; matrix products, arithmetic and copies ran while one was open for 9% -> 2% of each run, Pallas kernels for 0% -> 24%
where the time goes in v1:
time: 149 us; the launch traced here: 148 us
  starting transfers between devices  41.9 us (28%)
  waiting for transfers between devices  41.4 us (28%)
  Pallas kernels  35.1 us (24%)
  local copies, waits for them, and re-layouts  21.8 us (15%)
  other arithmetic  6.93 us (5%)
    ppermute x41, starting transfers between devices, move(): return lax.ppermute(value, axes, pairs)  41.9 us
    ppermute x41, waiting for transfers between devices, move(): return lax.ppermute(value, axes, pairs)  41.4 us
    pallas_call x4, Pallas kernels, stage(): pl.pallas_call(functools.partial(stage_kernel, local_experts), out_shape=...  24.8 us
    unnamed x85, local copies, waits for them, and re-layouts  19.7 us
    pallas_call x1, Pallas kernels, weight_grads(): pl.pallas_call(functools.partial(weights_kernel, len(parts)), grid=(tiles...  10.2 us
  transfers between devices with their start and end apart: 41, of which 13 were waited for; matrix products, arithmetic and copies ran while one was open for 2% of the time, Pallas kernels for 24%

profile of v1, /device:TPU:0, one launch (start us, length us, event | category | flops | bytes accessed | tf_op | source)
XLA Modules:
  0.0 148.2 jit_solution(7843672856939347096)
XLA Ops:
  4.2 4.1 %collective-permute-start.6 = (bf16[32,4224]{1,0:T(8,128)(2,1)S(1)}, bf16[32,4224]{1,0:T(8,128)(2,1)S(1)}, u32[]{:S(2)}, u32[]{:S(2)}) collective-permute-start(bf16[32,4224]{1,0:T(8,128)(2,1)S(1)} %get-tuple-element.59.refs_0_), channel_id=1, source_target_pairs={{0,16},{1,17},{2,18},{3,19},{4,20},{5,21},{6,22},{7,23},{8,0},{9,1... | collective-permute-start | bytes 811016 | tf_op jit(solution)/shard_map/ppermute | solution.py:258
  8.3 1.5 %collective-permute-start = (bf16[32,4224]{1,0:T(8,128)(2,1)S(1)}, bf16[32,4224]{1,0:T(8,128)(2,1)S(1)}, u32[]{:S(2)}, u32[]{:S(2)}) collective-permute-start(bf16[32,4224]{1,0:T(8,128)(2,1)S(1)} %get-tuple-element.59.refs_0_), channel_id=1, source_target_pairs={{0,4},{1,5},{2,6},{3,7},{4,0},{5,1},{6,2},{7,3},{8,12},{9,13},{10,... | collective-permute-start | bytes 811016 | tf_op jit(solution)/shard_map/ppermute | solution.py:258
  9.8 4.2 %collective-permute-done.6.refs_0_ = bf16[32,4224]{1,0:T(8,128)(2,1)S(1)} collective-permute-done((bf16[32,4224]{1,0:T(8,128)(2,1)S(1)}, bf16[32,4224]{1,0:T(8,128)(2,1)S(1)}, u32[]{:S(2)}, u32[]{:S(2)}) %collective-permute-start.6) | collective-permute-done | bytes 270368 | tf_op jit(solution)/shard_map/ppermute | solution.py:258
  14.0 1.5 %collective-permute-start.28 = (bf16[32,4224]{1,0:T(8,128)(2,1)S(1)}, bf16[32,4224]{1,0:T(8,128)(2,1)S(1)}, u32[]{:S(2)}, u32[]{:S(2)}) collective-permute-start(bf16[32,4224]{1,0:T(8,128)(2,1)S(1)} %collective-permute-done.6.refs_0_), channel_id=1, source_target_pairs={{0,4},{1,5},{2,6},{3,7},{4,0},{5,1},{6,2},{7,3},{8,12},{9,13},{10,... | collective-permute-start | bytes 811016 | tf_op jit(solution)/shard_map/ppermute | solution.py:258
  17.0 3.4 %collective-permute-start.7 = (bf16[32,4224]{1,0:T(8,128)(2,1)S(1)}, bf16[32,4224]{1,0:T(8,128)(2,1)S(1)}, u32[]{:S(2)}, u32[]{:S(2)}) collective-permute-start(bf16[32,4224]{1,0:T(8,128)(2,1)S(1)} %collective-permute-done.6.refs_0_), channel_id=1, source_target_pairs={{0,16},{1,17},{2,18},{3,19},{4,20},{5,21},{6,22},{7,23},{8,0},{9,1... | collective-permute-start | bytes 811016 | tf_op jit(solution)/shard_map/ppermute | solution.py:258
  24.2 2.2 %collective-permute-start.29 = (bf16[32,4224]{1,0:T(8,128)(2,1)S(1)}, bf16[32,4224]{1,0:T(8,128)(2,1)S(1)}, u32[]{:S(2)}, u32[]{:S(2)}) collective-permute-start(bf16[32,4224]{1,0:T(8,128)(2,1)S(1)} %collective-permute-done.28.refs_2_), channel_id=1, source_target_pairs={{0,2},{1,3},{2,0},{3,1},{4,6},{5,7},{6,4},{7,5},{8,10},{9,11},{10,... | collective-permute-start | bytes 811016 | tf_op jit(solution)/shard_map/ppermute | solution.py:258
  28.3 2.1 %collective-permute-done.1.refs_3_ = bf16[32,4224]{1,0:T(8,128)(2,1)S(1)} collective-permute-done((bf16[32,4224]{1,0:T(8,128)(2,1)S(1)}, bf16[32,4224]{1,0:T(8,128)(2,1)S(1)}, u32[]{:S(2)}, u32[]{:S(2)}) %collective-permute-start.1) | collective-permute-done | bytes 270368 | tf_op jit(solution)/shard_map/ppermute | solution.py:258
  31.6 3.6 %collective-permute-start.8 = (bf16[32,4224]{1,0:T(8,128)(2,1)S(1)}, bf16[32,4224]{1,0:T(8,128)(2,1)}, u32[]{:S(2)}, u32[]{:S(2)}) collective-permute-start(bf16[32,4224]{1,0:T(8,128)(2,1)S(1)} %collective-permute-done.7.refs_0_), channel_id=1, source_target_pairs={{0,16},{1,17},{2,18},{3,19},{4,20},{5,21},{6,22},{7,23},{8,0},{9,1... | collective-permute-start | bytes 811016 | tf_op jit(solution)/shard_map/ppermute | solution.py:258
  41.5 3.9 %collective-permute-done.18.refs_1_ = bf16[32,4224]{1,0:T(8,128)(2,1)} collective-permute-done((bf16[32,4224]{1,0:T(8,128)(2,1)S(1)}, bf16[32,4224]{1,0:T(8,128)(2,1)}, u32[]{:S(2)}, u32[]{:S(2)}) %collective-permute-start.18) | collective-permute-done | bytes 270368 | tf_op jit(solution)/shard_map/ppermute | solution.py:258
  47.7 3.2 %collective-permute-done.20.refs_3_ = bf16[32,4224]{1,0:T(8,128)(2,1)} collective-permute-done((bf16[32,4224]{1,0:T(8,128)(2,1)S(1)}, bf16[32,4224]{1,0:T(8,128)(2,1)}, u32[]{:S(2)}, u32[]{:S(2)}) %collective-permute-start.20) | collective-permute-done | bytes 270368 | tf_op jit(solution)/shard_map/ppermute | solution.py:258
  51.6 2.0 %pad_maximum_fusion.refs_8_ = bf16[768,2048]{1,0:T(8,128)(2,1)} fusion(bf16[384,2048]{1,0:T(8,128)(2,1)S(1)} %bitcast.28, bf16[384,2048]{1,0:T(8,128)(2,1)S(1)} %bitcast.29), kind=kLoop, calls=%fused_computation | loop fusion | flops 6291456 | bytes 6291456 | tf_op jit(solution)/shard_map/concatenate | solution.py:269
  61.8 6.1 %stage.7 = (bf16[128,2176]{1,0:T(8,128)(2,1)S(1)}, bf16[128,2176]{1,0:T(8,128)(2,1)S(1)}, bf16[256,4224]{1,0:T(8,128)(2,1)}, bf16[256,768]{1,0:T(8,128)(2,1)S(1)}, bf16[256,384]{1,0:T(8,128)(2,1)S(1)}) custom-call(s32[1]{0:T(128)} %bitcast.base_ref, bf16[32,4224]{1,0:T(8,128)(2,1)S(1)} %collective-permute-done.6.refs_0_, bf16[32,4224]{1,0:T(8,128)(2,1)S(1)} %copy-done.26, ...), custom_call_target="tpu_custom_call" | custom-call | flops 2013265920 | bytes 4325376 | tf_op jit(solution)/shard_map/stage/pallas_call | solution.py:167
  69.1 6.0 %stage.4 = (bf16[128,2176]{1,0:T(8,128)(2,1)S(1)}, bf16[128,2176]{1,0:T(8,128)(2,1)S(1)}, bf16[256,4224]{1,0:T(8,128)(2,1)}, bf16[256,768]{1,0:T(8,128)(2,1)S(1)}, bf16[256,384]{1,0:T(8,128)(2,1)S(1)}) custom-call(s32[1]{0:T(128)} %bitcast.base_ref, bf16[32,4224]{1,0:T(8,128)(2,1)S(1)} %get-tuple-element.59.refs_0_, ...), custom_call_target="tpu_custom_call" | custom-call | flops 2013265920 | bytes 4325376 | tf_op jit(solution)/shard_map/stage/pallas_call | solution.py:167
  75.9 6.4 %stage.6 = (bf16[128,2176]{1,0:T(8,128)(2,1)S(1)}, bf16[128,2176]{1,0:T(8,128)(2,1)S(1)}, bf16[256,4224]{1,0:T(8,128)(2,1)}, bf16[256,768]{1,0:T(8,128)(2,1)S(1)}, bf16[256,384]{1,0:T(8,128)(2,1)S(1)}) custom-call(s32[1]{0:T(128)} %bitcast.base_ref, bf16[32,4224]{1,0:T(8,128)(2,1)S(1)} %copy-done.12, bf16[32,4224]{1,0:T(8,128)(2,1)} %collective-permute-done.18.refs_1_, ...), custom_call_target="tpu_custom_call" | custom-call | flops 2013265920 | bytes 4325376 | tf_op jit(solution)/shard_map/stage/pallas_call | solution.py:167
  83.5 6.3 %stage.5 = (bf16[128,2176]{1,0:T(8,128)(2,1)S(1)}, bf16[128,2176]{1,0:T(8,128)(2,1)S(1)}, bf16[256,4224]{1,0:T(8,128)(2,1)}, bf16[256,768]{1,0:T(8,128)(2,1)S(1)}, bf16[256,384]{1,0:T(8,128)(2,1)S(1)}) custom-call(s32[1]{0:T(128)} %bitcast.base_ref, bf16[32,4224]{1,0:T(8,128)(2,1)} %collective-permute-done.8.refs_0_, ...), custom_call_target="tpu_custom_call" | custom-call | flops 2013265920 | bytes 4325376 | tf_op jit(solution)/shard_map/stage/pallas_call | solution.py:167
  93.0 7.2 %collective-permute-done.35 = bf16[64,2176]{1,0:T(8,128)(2,1)S(1)} collective-permute-done((bf16[64,2176]{1,0:T(8,128)(2,1)S(1)}, bf16[64,2176]{1,0:T(8,128)(2,1)S(1)}, u32[]{:S(2)}, u32[]{:S(2)}) %collective-permute-start.35) | collective-permute-done | bytes 278560 | tf_op jit(solution)/shard_map/ppermute | solution.py:258
  100.3 3.6 %collective-permute-start.36 = (bf16[64,2176]{1,0:T(8,128)(2,1)S(1)}, bf16[64,2176]{1,0:T(8,128)(2,1)S(1)}, u32[]{:S(2)}, u32[]{:S(2)}) collective-permute-start(bf16[64,2176]{1,0:T(8,128)(2,1)S(1)} %fusion.1), channel_id=1, source_target_pairs={{0,16},{1,17},{2,18},{3,19},{4,20},{5,21},{6,22},{7,23},{8,0},{9,1... | collective-permute-start | bytes 835592 | tf_op jit(solution)/shard_map/ppermute | solution.py:258
  105.8 3.0 %collective-permute-done.36 = bf16[64,2176]{1,0:T(8,128)(2,1)S(1)} collective-permute-done((bf16[64,2176]{1,0:T(8,128)(2,1)S(1)}, bf16[64,2176]{1,0:T(8,128)(2,1)S(1)}, u32[]{:S(2)}, u32[]{:S(2)}) %collective-permute-start.36) | collective-permute-done | bytes 278560 | tf_op jit(solution)/shard_map/ppermute | solution.py:258
  108.9 3.4 %collective-permute-start.37 = (bf16[64,2176]{1,0:T(8,128)(2,1)S(1)}, bf16[64,2176]{1,0:T(8,128)(2,1)S(1)}, u32[]{:S(2)}, u32[]{:S(2)}) collective-permute-start(bf16[64,2176]{1,0:T(8,128)(2,1)S(1)} %fusion.3), channel_id=1, source_target_pairs={{0,16},{1,17},{2,18},{3,19},{4,20},{5,21},{6,22},{7,23},{8,0},{9,1... | collective-permute-start | bytes 835592 | tf_op jit(solution)/shard_map/ppermute | solution.py:258
  113.0 3.4 %collective-permute-done.37 = bf16[64,2176]{1,0:T(8,128)(2,1)S(1)} collective-permute-done((bf16[64,2176]{1,0:T(8,128)(2,1)S(1)}, bf16[64,2176]{1,0:T(8,128)(2,1)S(1)}, u32[]{:S(2)}, u32[]{:S(2)}) %collective-permute-start.37) | collective-permute-done | bytes 278560 | tf_op jit(solution)/shard_map/ppermute | solution.py:258
  116.5 3.4 %collective-permute-start.38 = (bf16[64,2176]{1,0:T(8,128)(2,1)S(1)}, bf16[64,2176]{1,0:T(8,128)(2,1)S(1)}, u32[]{:S(2)}, u32[]{:S(2)}) collective-permute-start(bf16[64,2176]{1,0:T(8,128)(2,1)S(1)} %fusion.5), channel_id=1, source_target_pairs={{0,16},{1,17},{2,18},{3,19},{4,20},{5,21},{6,22},{7,23},{8,0},{9,1... | collective-permute-start | bytes 835592 | tf_op jit(solution)/shard_map/ppermute | solution.py:258
  119.9 4.1 %collective-permute-done.38 = bf16[64,2176]{1,0:T(8,128)(2,1)S(1)} collective-permute-done((bf16[64,2176]{1,0:T(8,128)(2,1)S(1)}, bf16[64,2176]{1,0:T(8,128)(2,1)S(1)}, u32[]{:S(2)}, u32[]{:S(2)}) %collective-permute-start.38) | collective-permute-done | bytes 278560 | tf_op jit(solution)/shard_map/ppermute | solution.py:258
  125.6 6.1 %collective-permute-done.39 = bf16[64,2176]{1,0:T(8,128)(2,1)} collective-permute-done((bf16[64,2176]{1,0:T(8,128)(2,1)}, bf16[64,2176]{1,0:T(8,128)(2,1)}, u32[]{:S(2)}, u32[]{:S(2)}) %collective-permute-start.39) | collective-permute-done | bytes 278560 | tf_op jit(solution)/shard_map/ppermute | solution.py:258
  135.7 10.2 %weight_grads.1 = (bf16[384,2048]{1,0:T(8,128)(2,1)}, bf16[384,2048]{1,0:T(8,128)(2,1)}, bf16[384,2048]{1,0:T(8,128)(2,1)}) custom-call(bf16[256,4224]{1,0:T(8,128)(2,1)S(1)} %copy-done, bf16[256,4224]{1,0:T(8,128)(2,1)S(1)} %copy-done, bf16[256,768]{1,0:T(8,128)(2,1)S(1)} %get-tuple-element.37.refs_2_, bf16[256,384]{1,0:T(8,128)(2,1)S(1)} %copy-done.4, ...), custom_call_target="tpu_custom_call" | custom-call | flops 4831838208 | bytes 13107200 | tf_op jit(solution)/shard_map/weight_grads/pallas_call | solution.py:217
  (173 shorter events, 46.1 us)
Async XLA Ops:
  4.2 9.8 %collective-permute-start.6 = (bf16[32,4224]{1,0:T(8,128)(2,1)S(1)}, bf16[32,4224]{1,0:T(8,128)(2,1)S(1)}, u32[]{:S(2)}, u32[]{:S(2)}) collective-permute-start(bf16[32,4224]{1,0:T(8,128)(2,1)S(1)} %get-tuple-element.59.refs_0_), channel_id=1, source_target_pairs={{0,16},{1,17},{2,18},{3,19},{4,20},{5,21},{6,22},{7,23},{8,0},{9,1... | collective-permute-start | bytes 811016 | tf_op jit(solution)/shard_map/ppermute | solution.py:258
  8.3 12.1 %collective-permute-start = (bf16[32,4224]{1,0:T(8,128)(2,1)S(1)}, bf16[32,4224]{1,0:T(8,128)(2,1)S(1)}, u32[]{:S(2)}, u32[]{:S(2)}) collective-permute-start(bf16[32,4224]{1,0:T(8,128)(2,1)S(1)} %get-tuple-element.59.refs_0_), channel_id=1, source_target_pairs={{0,4},{1,5},{2,6},{3,7},{4,0},{5,1},{6,2},{7,3},{8,12},{9,13},{10,... | collective-permute-start | bytes 811016 | tf_op jit(solution)/shard_map/ppermute | solution.py:258
  17.0 10.0 %collective-permute-start.7 = (bf16[32,4224]{1,0:T(8,128)(2,1)S(1)}, bf16[32,4224]{1,0:T(8,128)(2,1)S(1)}, u32[]{:S(2)}, u32[]{:S(2)}) collective-permute-start(bf16[32,4224]{1,0:T(8,128)(2,1)S(1)} %collective-permute-done.6.refs_0_), channel_id=1, source_target_pairs={{0,16},{1,17},{2,18},{3,19},{4,20},{5,21},{6,22},{7,23},{8,0},{9,1... | collective-permute-start | bytes 811016 | tf_op jit(solution)/shard_map/ppermute | solution.py:258
  24.2 11.7 %collective-permute-start.29 = (bf16[32,4224]{1,0:T(8,128)(2,1)S(1)}, bf16[32,4224]{1,0:T(8,128)(2,1)S(1)}, u32[]{:S(2)}, u32[]{:S(2)}) collective-permute-start(bf16[32,4224]{1,0:T(8,128)(2,1)S(1)} %collective-permute-done.28.refs_2_), channel_id=1, source_target_pairs={{0,2},{1,3},{2,0},{3,1},{4,6},{5,7},{6,4},{7,5},{8,10},{9,11},{10,... | collective-permute-start | bytes 811016 | tf_op jit(solution)/shard_map/ppermute | solution.py:258
  27.1 10.2 %collective-permute-start.31 = (bf16[32,4224]{1,0:T(8,128)(2,1)S(1)}, bf16[32,4224]{1,0:T(8,128)(2,1)S(1)}, u32[]{:S(2)}, u32[]{:S(2)}) collective-permute-start(bf16[32,4224]{1,0:T(8,128)(2,1)S(1)} %collective-permute-done.27.refs_1_), channel_id=1, source_target_pairs={{0,1},{1,0},{2,3},{3,2},{4,5},{5,4},{6,7},{7,6},{8,9},{9,8},{10,11... | collective-permute-start | bytes 811016 | tf_op jit(solution)/shard_map/ppermute | solution.py:258
  27.8 10.8 %collective-permute-start.21 = (bf16[32,4224]{1,0:T(8,128)(2,1)S(1)}, bf16[32,4224]{1,0:T(8,128)(2,1)S(1)}, u32[]{:S(2)}, u32[]{:S(2)}) collective-permute-start(bf16[32,4224]{1,0:T(8,128)(2,1)S(1)} %collective-permute-done.7.refs_0_), channel_id=1, source_target_pairs={{0,1},{1,0},{2,3},{3,2},{4,5},{5,4},{6,7},{7,6},{8,9},{9,8},{10,11... | collective-permute-start | bytes 811016 | tf_op jit(solution)/shard_map/ppermute | solution.py:258
  35.8 9.5 %collective-permute-start.18 = (bf16[32,4224]{1,0:T(8,128)(2,1)S(1)}, bf16[32,4224]{1,0:T(8,128)(2,1)}, u32[]{:S(2)}, u32[]{:S(2)}) collective-permute-start(bf16[32,4224]{1,0:T(8,128)(2,1)S(1)} %collective-permute-done.7.refs_0_), channel_id=1, source_target_pairs={{0,2},{1,3},{2,0},{3,1},{4,6},{5,7},{6,4},{7,5},{8,10},{9,11},{10,... | collective-permute-start | bytes 811016 | tf_op jit(solution)/shard_map/ppermute | solution.py:258
  39.9 11.0 %collective-permute-start.20 = (bf16[32,4224]{1,0:T(8,128)(2,1)S(1)}, bf16[32,4224]{1,0:T(8,128)(2,1)}, u32[]{:S(2)}, u32[]{:S(2)}) collective-permute-start(bf16[32,4224]{1,0:T(8,128)(2,1)S(1)} %collective-permute-done.19.refs_2_), channel_id=1, source_target_pairs={{0,2},{1,3},{2,0},{3,1},{4,6},{5,7},{6,4},{7,5},{8,10},{9,11},{10,... | collective-permute-start | bytes 811016 | tf_op jit(solution)/shard_map/ppermute | solution.py:258
  40.5 10.4 %collective-permute-start.10 = (bf16[32,4224]{1,0:T(8,128)(2,1)}, bf16[32,4224]{1,0:T(8,128)(2,1)}, u32[]{:S(2)}, u32[]{:S(2)}) collective-permute-start(bf16[32,4224]{1,0:T(8,128)(2,1)} %collective-permute-done.8.refs_0_), channel_id=1, source_target_pairs={{0,4},{1,5},{2,6},{3,7},{4,0},{5,1},{6,2},{7,3},{8,12},{9,13},{10,... | collective-permute-start | bytes 811016 | tf_op jit(solution)/shard_map/ppermute | solution.py:258
  45.3 22.5 %collective-permute-start.23 = (bf16[32,4224]{1,0:T(8,128)(2,1)S(1)}, bf16[32,4224]{1,0:T(8,128)(2,1)}, u32[]{:S(2)}, u32[]{:S(2)}) collective-permute-start(bf16[32,4224]{1,0:T(8,128)(2,1)S(1)} %collective-permute-done.19.refs_2_), channel_id=1, source_target_pairs={{0,1},{1,0},{2,3},{3,2},{4,5},{5,4},{6,7},{7,6},{8,9},{9,8},{10,11... | collective-permute-start | bytes 811016 | tf_op jit(solution)/shard_map/ppermute | solution.py:258
  45.3 23.0 %collective-permute-start.9 = (bf16[32,4224]{1,0:T(8,128)(2,1)}, bf16[32,4224]{1,0:T(8,128)(2,1)}, u32[]{:S(2)}, u32[]{:S(2)}) collective-permute-start(bf16[32,4224]{1,0:T(8,128)(2,1)} %collective-permute-done.8.refs_0_), channel_id=1, source_target_pairs={{0,2},{1,3},{2,0},{3,1},{4,6},{5,7},{6,4},{7,5},{8,10},{9,11},{10,... | collective-permute-start | bytes 811016 | tf_op jit(solution)/shard_map/ppermute | solution.py:258
  47.5 20.5 %collective-permute-start.22 = (bf16[32,4224]{1,0:T(8,128)(2,1)}, bf16[32,4224]{1,0:T(8,128)(2,1)}, u32[]{:S(2)}, u32[]{:S(2)}) collective-permute-start(bf16[32,4224]{1,0:T(8,128)(2,1)} %collective-permute-done.18.refs_1_), channel_id=1, source_target_pairs={{0,1},{1,0},{2,3},{3,2},{4,5},{5,4},{6,7},{7,6},{8,9},{9,8},{10,11... | collective-permute-start | bytes 811016 | tf_op jit(solution)/shard_map/ppermute | solution.py:258
  50.9 17.7 %collective-permute-start.24 = (bf16[32,4224]{1,0:T(8,128)(2,1)}, bf16[32,4224]{1,0:T(8,128)(2,1)}, u32[]{:S(2)}, u32[]{:S(2)}) collective-permute-start(bf16[32,4224]{1,0:T(8,128)(2,1)} %collective-permute-done.20.refs_3_), channel_id=1, source_target_pairs={{0,1},{1,0},{2,3},{3,2},{4,5},{5,4},{6,7},{7,6},{8,9},{9,8},{10,11... | collective-permute-start | bytes 811016 | tf_op jit(solution)/shard_map/ppermute | solution.py:258
  50.9 18.0 %collective-permute-start.11 = (bf16[32,4224]{1,0:T(8,128)(2,1)}, bf16[32,4224]{1,0:T(8,128)(2,1)}, u32[]{:S(2)}, u32[]{:S(2)}) collective-permute-start(bf16[32,4224]{1,0:T(8,128)(2,1)} %collective-permute-done.10.refs_2_), channel_id=1, source_target_pairs={{0,2},{1,3},{2,0},{3,1},{4,6},{5,7},{6,4},{7,5},{8,10},{9,11},{10,... | collective-permute-start | bytes 811016 | tf_op jit(solution)/shard_map/ppermute | solution.py:258
  67.8 15.1 %collective-permute-start.12 = (bf16[32,4224]{1,0:T(8,128)(2,1)}, bf16[32,4224]{1,0:T(8,128)(2,1)S(1)}, u32[]{:S(2)}, u32[]{:S(2)}) collective-permute-start(bf16[32,4224]{1,0:T(8,128)(2,1)} %collective-permute-done.8.refs_0_), channel_id=1, source_target_pairs={{0,1},{1,0},{2,3},{3,2},{4,5},{5,4},{6,7},{7,6},{8,9},{9,8},{10,11... | collective-permute-start | bytes 811016 | tf_op jit(solution)/shard_map/ppermute | solution.py:258
  68.1 22.0 %collective-permute-start.34 = (bf16[128,2176]{1,0:T(8,128)(2,1)S(1)}, bf16[128,2176]{1,0:T(8,128)(2,1)S(1)}, u32[]{:S(2)}, u32[]{:S(2)}) collective-permute-start(bf16[128,2176]{1,0:T(8,128)(2,1)S(1)} %get-tuple-element.35), channel_id=1, source_target_pairs={{0,1},{1,0},{2,3},{3,2},{4,5},{5,4},{6,7},{7,6},{8,9},{9,8},{10,11... | collective-permute-start | bytes 1671176 | tf_op jit(solution)/shard_map/ppermute | solution.py:258
  68.4 14.9 %collective-permute-start.14 = (bf16[32,4224]{1,0:T(8,128)(2,1)}, bf16[32,4224]{1,0:T(8,128)(2,1)S(1)}, u32[]{:S(2)}, u32[]{:S(2)}) collective-permute-start(bf16[32,4224]{1,0:T(8,128)(2,1)} %collective-permute-done.10.refs_2_), channel_id=1, source_target_pairs={{0,1},{1,0},{2,3},{3,2},{4,5},{5,4},{6,7},{7,6},{8,9},{9,8},{10,11... | collective-permute-start | bytes 811016 | tf_op jit(solution)/shard_map/ppermute | solution.py:258
  68.6 14.9 %collective-permute-start.13 = (bf16[32,4224]{1,0:T(8,128)(2,1)}, bf16[32,4224]{1,0:T(8,128)(2,1)S(1)}, u32[]{:S(2)}, u32[]{:S(2)}) collective-permute-start(bf16[32,4224]{1,0:T(8,128)(2,1)} %collective-permute-done.9.refs_1_), channel_id=1, source_target_pairs={{0,1},{1,0},{2,3},{3,2},{4,5},{5,4},{6,7},{7,6},{8,9},{9,8},{10,11... | collective-permute-start | bytes 811016 | tf_op jit(solution)/shard_map/ppermute | solution.py:258
  68.9 14.6 %collective-permute-start.15 = (bf16[32,4224]{1,0:T(8,128)(2,1)}, bf16[32,4224]{1,0:T(8,128)(2,1)S(1)}, u32[]{:S(2)}, u32[]{:S(2)}) collective-permute-start(bf16[32,4224]{1,0:T(8,128)(2,1)} %collective-permute-done.11.refs_3_), channel_id=1, source_target_pairs={{0,1},{1,0},{2,3},{3,2},{4,5},{5,4},{6,7},{7,6},{8,9},{9,8},{10,11... | collective-permute-start | bytes 811016 | tf_op jit(solution)/shard_map/ppermute | solution.py:258
  83.0 29.4 %collective-permute-start.4 = (bf16[128,2176]{1,0:T(8,128)(2,1)S(1)}, bf16[128,2176]{1,0:T(8,128)(2,1)S(1)}, u32[]{:S(2)}, u32[]{:S(2)}) collective-permute-start(bf16[128,2176]{1,0:T(8,128)(2,1)S(1)} %get-tuple-element.29), channel_id=1, source_target_pairs={{0,1},{1,0},{2,3},{3,2},{4,5},{5,4},{6,7},{7,6},{8,9},{9,8},{10,11... | collective-permute-start | bytes 1671176 | tf_op jit(solution)/shard_map/ppermute | solution.py:258
  89.8 14.1 %collective-permute-start.16 = (bf16[128,2176]{1,0:T(8,128)(2,1)S(1)}, bf16[128,2176]{1,0:T(8,128)(2,1)S(1)}, u32[]{:S(2)}, u32[]{:S(2)}) collective-permute-start(bf16[128,2176]{1,0:T(8,128)(2,1)S(1)} %get-tuple-element.31), channel_id=1, source_target_pairs={{0,1},{1,0},{2,3},{3,2},{4,5},{5,4},{6,7},{7,6},{8,9},{9,8},{10,11... | collective-permute-start | bytes 1671176 | tf_op jit(solution)/shard_map/ppermute | solution.py:258
  90.7 9.5 %collective-permute-start.35 = (bf16[64,2176]{1,0:T(8,128)(2,1)S(1)}, bf16[64,2176]{1,0:T(8,128)(2,1)S(1)}, u32[]{:S(2)}, u32[]{:S(2)}) collective-permute-start(bf16[64,2176]{1,0:T(8,128)(2,1)S(1)} %slice.86), channel_id=1, source_target_pairs={{0,4},{1,5},{2,6},{3,7},{4,0},{5,1},{6,2},{7,3},{8,12},{9,13},{10,... | collective-permute-start | bytes 835592 | tf_op jit(solution)/shard_map/ppermute | solution.py:258
  91.6 14.1 %collective-permute-start.26 = (bf16[64,2176]{1,0:T(8,128)(2,1)S(1)}, bf16[64,2176]{1,0:T(8,128)(2,1)S(1)}, u32[]{:S(2)}, u32[]{:S(2)}) collective-permute-start(bf16[64,2176]{1,0:T(8,128)(2,1)S(1)} %slice.87), channel_id=1, source_target_pairs={{0,4},{1,5},{2,6},{3,7},{4,0},{5,1},{6,2},{7,3},{8,12},{9,13},{10,... | collective-permute-start | bytes 835592 | tf_op jit(solution)/shard_map/ppermute | solution.py:258
  133.7 12.2 %collective-permute-start.40 = (bf16[64,2176]{1,0:T(8,128)(2,1)S(1)}, bf16[64,2176]{1,0:T(8,128)(2,1)S(1)}, u32[]{:S(2)}, u32[]{:S(2)}) collective-permute-start(bf16[64,2176]{1,0:T(8,128)(2,1)S(1)} %add_convert_fusion), channel_id=1, source_target_pairs={{0,1},{1,0},{2,3},{3,2},{4,5},{5,4},{6,7},{7,6},{8,9},{9,8},{10,11... | collective-permute-start | bytes 835592 | tf_op jit(solution)/shard_map/ppermute | solution.py:258
  (58 other events, 428.2 us)

commit v2 on v1

--- a/solution.py
+++ b/solution.py
@@ -10,7 +10,7 @@
 BF16 = jnp.bfloat16
 F32 = jnp.float32
 LANES = 128
-VMEM_BYTES = 48 * 1024 * 1024
+VMEM_BYTES = 16 * 1024 * 1024
 
 
 def token_sum(slot_rows, target, tok_rows, top_count):
@@ -114,19 +114,19 @@
     return (grad_tokens, grad_probs, grad_gate, grad_up, grad_down)
 
 
-def stage_kernel(local_experts, base_ref, *refs):
-    (*chunks, gate_up, down, keep, send, rows, d_both, hid) = refs
-    width = down.shape[1]
-    units = down.shape[0]
+def stage_kernel(local_experts, base_ref, mine, theirs, gate_up, down, keep, send, d_both, hid):
+    units, width = down.shape
     each = units // local_experts
-    step = chunks[0].shape[0]
-    for i, chunk in enumerate(chunks):
-        rows[i * step : (i + 1) * step, :] = chunk[...]
-    count = rows.shape[0]
+    half = mine.shape[0]
+    count = 2 * half
     nt = (((1,), (1,)), ((), ()))
-    pre = lax.dot_general(rows[:, :width], gate_up[...], nt, preferred_element_type=F32)
-    back = lax.dot_general(rows[:, width : 2 * width], down[...], nt, preferred_element_type=F32)
-    extra = rows[:, 2 * width :].astype(F32)
+
+    def both(start, stop):
+        return jnp.concatenate([mine[:, start:stop], theirs[:, start:stop]], axis=0)
+
+    pre = lax.dot_general(both(0, width), gate_up[...], nt, preferred_element_type=F32)
+    back = lax.dot_general(both(width, 2 * width), down[...], nt, preferred_element_type=F32)
+    extra = both(2 * width, mine.shape[1]).astype(F32)
     lane = lax.broadcasted_iota(jnp.int32, extra.shape, 1)
     unit = lax.broadcasted_iota(jnp.int32, (count, units), 1)
     weight = jnp.zeros((count, units), F32)
@@ -141,8 +141,8 @@
     product = hidden * back
     found = jnp.zeros(extra.shape, F32)
     for e in range(local_experts):
-        mine = (unit >= e * each) & (unit < (e + 1) * each)
-        own = jnp.sum(jnp.where(mine, product, 0.0), axis=1, keepdims=True)
+        covered = (unit >= e * each) & (unit < (e + 1) * each)
+        own = jnp.sum(jnp.where(covered, product, 0.0), axis=1, keepdims=True)
         found = jnp.where(lane == base_ref[0] + e, own, found)
     hid[...] = (hidden * weight).astype(BF16)
     hidden_grad = weight * back
@@ -151,86 +151,128 @@
     ).astype(BF16)
     d_both[:, units:] = (hidden_grad * activated).astype(BF16)
     part = jnp.dot(d_both[...], gate_up[...], preferred_element_type=F32).astype(BF16)
-    half = count // 2
     keep[:, :width] = part[:half]
     send[:, :width] = part[half:]
     keep[:, width:] = found[:half].astype(BF16)
     send[:, width:] = found[half:].astype(BF16)
 
 
-def stage(base, chunks, gate_up, down, local_experts):
+def stage(base, mine, theirs, gate_up, down, local_experts):
     units, width = down.shape
-    step, columns = chunks[0].shape
-    count = step * len(chunks)
+    half, columns = mine.shape
+    count = 2 * half
     extra = columns - 2 * width
     flops = 2 * count * width * (2 * units + units + 2 * units)
     return pl.pallas_call(
         functools.partial(stage_kernel, local_experts),
         out_shape=(
-            jax.ShapeDtypeStruct((count // 2, width + extra), BF16),
-            jax.ShapeDtypeStruct((count // 2, width + extra), BF16),
-            jax.ShapeDtypeStruct((count, columns), BF16),
+            jax.ShapeDtypeStruct((half, width + extra), BF16),
+            jax.ShapeDtypeStruct((half, width + extra), BF16),
             jax.ShapeDtypeStruct((count, 2 * units), BF16),
             jax.ShapeDtypeStruct((count, units), BF16),
         ),
         in_specs=[pl.BlockSpec(memory_space=pltpu.SMEM)]
-        + [pl.BlockSpec(memory_space=pltpu.VMEM)] * (len(chunks) + 2),
-        out_specs=(pl.BlockSpec(memory_space=pltpu.VMEM),) * 5,
+        + [pl.BlockSpec(memory_space=pltpu.VMEM)] * 4,
+        out_specs=(pl.BlockSpec(memory_space=pltpu.VMEM),) * 4,
         compiler_params=pltpu.CompilerParams(vmem_limit_bytes=VMEM_BYTES),
         cost_estimate=pl.CostEstimate(
             flops=flops, bytes_accessed=4 * count * columns, transcendentals=count * units
         ),
         name="stage",
-    )(base, *chunks, gate_up, down)
+    )(base, mine, theirs, gate_up, down)
 
 
 def weights_kernel(stages, *refs):
-    ins = refs[: 4 * stages]
-    gate, up, down = refs[4 * stages :]
-    units = gate.shape[0]
+    out = refs[-1]
     tn = (((0,), (0,)), ((), ()))
-    both = 0.0
-    below = 0.0
+    total = 0.0
     for s in range(stages):
-        x, o, d_both, hid = ins[4 * s : 4 * s + 4]
-        both = both + lax.dot_general(d_both[...], x[...], tn, preferred_element_type=F32)
-        below = below + lax.dot_general(hid[...], o[...], tn, preferred_element_type=F32)
-    gate[...] = both[:units].astype(BF16)
-    up[...] = both[units:].astype(BF16)
-    down[...] = below.astype(BF16)
-
-
-def weight_grads(parts, width, units):
-    tile = 256
+        mine, theirs, hid = refs[3 * s : 3 * s + 3]
+        rows = jnp.concatenate([mine[...], theirs[...]], axis=0)
+        total = total + lax.dot_general(hid[...], rows, tn, preferred_element_type=F32)
+    out[...] = total.astype(BF16)
+
+
+def weight_grads(parts, side, width, units, which=0):
+    tile = 512
     tiles = width // tile
     specs, operands, total = [], [], 0
-    for rows, d_both, hid in parts:
-        count = rows.shape[0]
-        total += count
-        specs += [
-            pl.BlockSpec((count, tile), lambda j: (0, j)),
-            pl.BlockSpec((count, tile), lambda j: (0, j + tiles)),
-            pl.BlockSpec(d_both.shape, lambda j: (0, 0)),
-            pl.BlockSpec(hid.shape, lambda j: (0, 0)),
-        ]
-        operands += [rows, rows, d_both, hid]
+    for mine, theirs, hid in parts:
+        half = mine.shape[0]
+        total += 2 * half
+        specs += [pl.BlockSpec((half, tile), lambda j: (0, j + side * tiles))] * 2
+        specs += [pl.BlockSpec((2 * half, units), lambda j: (0, which))]
+        operands += [pltpu.with_memory_space_constraint(v, pltpu.HBM) for v in (mine, theirs, hid)]
     return pl.pallas_call(
         functools.partial(weights_kernel, len(parts)),
         grid=(tiles,),
-        out_shape=(jax.ShapeDtypeStruct((units, width), BF16),) * 3,
+        out_shape=jax.ShapeDtypeStruct((units, width), BF16),
         in_specs=specs,
-        out_specs=(pl.BlockSpec((units, tile), lambda j: (0, j)),) * 3,
+        out_specs=pl.BlockSpec((units, tile), lambda j: (0, j)),
         compiler_params=pltpu.CompilerParams(vmem_limit_bytes=VMEM_BYTES),
         cost_estimate=pl.CostEstimate(
-            flops=2 * total * width * 3 * units,
-            bytes_accessed=4 * total * width + 6 * units * width,
+            flops=2 * total * width * units,
+            bytes_accessed=2 * total * width + 2 * units * width,
             transcendentals=0,
         ),
         name="weight_grads",
     )(*operands)
 
 
-def gathered_body(lines, tokens, grad_out, routes, probs, w_gate, w_up, w_down):
+def pack_kernel(
+    step, quarters, routes, probs, tokens, grad_out, *refs
+):
+    outs, (dense, sem) = refs[:4], refs[4:]
+    width = tokens.shape[1]
+    copies = []
+    for i, out in enumerate(outs):
+        place = pl.ds(pl.multiple_of(quarters[i] * step, step), step)
+        copies.append(
+            pltpu.make_async_copy(tokens.at[place, :], out.at[:, pl.ds(0, width)], sem.at[2 * i])
+        )
+        copies.append(
+            pltpu.make_async_copy(
+                grad_out.at[place, :], out.at[:, pl.ds(width, width)], sem.at[2 * i + 1]
+            )
+        )
+    for copy in copies:
+        copy.start()
+    named = routes[...]
+    given = probs[...].astype(F32)
+    lanes = dense.shape[1]
+    ids = lax.broadcasted_iota(jnp.int32, (lanes, named.shape[1]), 0)
+    spread = jnp.zeros(ids.shape, F32)
+    for k in range(named.shape[0]):
+        spread = spread + jnp.where(ids == named[k : k + 1, :], given[k : k + 1, :], 0.0)
+    dense[...] = spread.T
+    for copy in copies:
+        copy.wait()
+    for i, out in enumerate(outs):
+        place = pl.ds(pl.multiple_of(quarters[i] * step, step), step)
+        out[:, 2 * width :] = dense[place, :].astype(BF16)
+
+
+def pack(quarters, routes, probs, tokens, grad_out, lanes):
+    rows, width = tokens.shape
+    step = rows // 4
+    return pl.pallas_call(
+        functools.partial(pack_kernel, step),
+        out_shape=(jax.ShapeDtypeStruct((step, 2 * width + lanes), BF16),) * 4,
+        in_specs=[pl.BlockSpec(memory_space=pltpu.SMEM)]
+        + [pl.BlockSpec(memory_space=pltpu.VMEM)] * 2
+        + [pl.BlockSpec(memory_space=pltpu.HBM)] * 2,
+        out_specs=(pl.BlockSpec(memory_space=pltpu.VMEM),) * 4,
+        scratch_shapes=[pltpu.VMEM((rows, lanes), F32), pltpu.SemaphoreType.DMA((8,))],
+        name="pack",
+    )(quarters, routes.T, probs.T, tokens, grad_out)
+
+
+def after(value, *others):
+    return lax.optimization_barrier((value, *others))[0] if others else value
+
+
+def gathered_body(tokens, grad_out, routes, probs, w_gate, w_up, w_down):
+    lines = 4
     axes = ("expert", "etp")
     local_experts, hid_units, width = w_gate.shape
     expert_count = 2 * lines * local_experts
@@ -240,8 +282,7 @@
     expert, etp = lax.axis_index("expert"), lax.axis_index("etp")
     side, core = etp // 2, etp % 2
 
-    order = list(range(0, lines, 2)) + list(range(1, lines, 2))[::-1]
-    after = {order[i]: order[(i + 1) % lines] for i in range(lines)}
+    order = (0, 2, 3, 1)
     places = [
         (z, y, x, c) for z in range(lines) for y in range(2) for x in range(2) for c in range(2)
     ]
@@ -249,7 +290,10 @@
     def number(z, y, x, c):
         return ((z * 2 + y) * 2 + x) * 2 + c
 
-    ring = [(number(z, y, x, c), number(after[z], y, x, c)) for z, y, x, c in places]
+    def along(hops):
+        ahead = {order[i]: order[(i + hops) % lines] for i in range(lines)}
+        return [(number(z, y, x, c), number(ahead[z], y, x, c)) for z, y, x, c in places]
+
     over_y = [(number(z, y, x, c), number(z, 1 - y, x, c)) for z, y, x, c in places]
     over_x = [(number(z, y, x, c), number(z, y, 1 - x, c)) for z, y, x, c in places]
     over_c = [(number(z, y, x, c), number(z, y, x, 1 - c)) for z, y, x, c in places]
@@ -258,48 +302,80 @@
         return lax.ppermute(value, axes, pairs)
 
     extra = -(-expert_count // LANES) * LANES
-    named = routes[:, :, None] == jnp.arange(extra, dtype=jnp.int32)
-    dense = jnp.sum(jnp.where(named, probs[:, :, None], 0).astype(F32), axis=1).astype(BF16)
-    block = jnp.concatenate([tokens, grad_out, dense], axis=1).reshape(4, step, -1)
-
-    def quarter(x, c):
-        return lax.dynamic_index_in_dim(block, 2 * x + c, 0, keepdims=False)
-
-    here = quarter(side, core)
+    ids = jnp.arange(extra, dtype=jnp.int32)
+
+    quarters = jnp.stack(
+        [2 * x + c for x, c in ((side, core), (1 - side, core), (side, 1 - core), (1 - side, 1 - core))]
+    ).astype(jnp.int32)
+    here, near, *rest = pack(quarters, routes, probs, tokens, grad_out, extra)
     gate_up = jnp.concatenate([w_gate.reshape(units, width), w_up.reshape(units, width)], axis=0)
     down = w_down.reshape(units, width)
     base = (expert * local_experts).astype(jnp.int32).reshape(1)
 
-    line = [here]
-    for s in range(1, lines):
-        line.append(move(line[-1], ring))
-    other = [move(v, over_y) for v in line]
-    line_x = [quarter(1 - side, core)] + [move(v, over_x) for v in line[1:]]
-    other_x = [move(v, over_x) for v in other]
-    parts, sums = [], []
-    for s in range(lines):
-        mine = [line[s], line_x[s], other[s], other_x[s]]
+    line = {0: here, 1: move(here, along(1)), }
+    line[3] = move(after(here, line[1]), along(-1))
+    other, line_x, other_x = {0: move(here, over_y)}, {0: near}, {0: move(near, over_y)}
+    line_x[1] = move(line[1], over_x)
+    line[2] = move(line[1], along(1))
+    for s in (1, 3, 2):
+        other[s] = move(line[s], over_y)
+
+    pairs = [
+        move(jnp.concatenate(v, axis=0), over_x)
+        for v in ([other[1], line[3]], [line[2], other[2]])
+    ]
+    rows, grads, chips, fars, backs = {}, {}, {}, {}, {}
+    sequence = list(range(lines))
+    for s in sequence:
         if s == 0:
-            theirs = [quarter(side, 1 - core), quarter(1 - side, 1 - core)] + [
-                move(v, over_c) for v in mine[2:]
-            ]
+            other_x[0] = after(other_x[0], line[2])
+        mine = jnp.concatenate([line[s], line_x[s], other[s], other_x[s]], axis=0)
+        if s == 0:
+            theirs = jnp.concatenate(rest + [move(mine[2 * step :], over_c)], axis=0)
         else:
-            theirs = [move(v, over_c) for v in mine]
-        keep, send, rows, d_both, hid = stage(base, mine + theirs, gate_up, down, local_experts)
-        parts.append((rows, d_both, hid))
-        chip = keep.astype(F32) + move(send, over_c).astype(F32)
-        far = move(chip[2 * step :].astype(BF16), over_y)
-        sums.append(chip[: 2 * step] + far.astype(F32))
-    total = sums[1]
-    for s in list(range(2, lines)) + [0]:
-        total = sums[s] + move(total.astype(BF16), ring).astype(F32)
+            theirs = move(mine, over_c)
+        wait = [chips[s - 1]] if s else []
+        outs = stage(after(base, *wait), mine, theirs, gate_up, down, local_experts)
+        if s == 0:
+            outs, pair, other[3] = lax.optimization_barrier((outs, pairs[0], other[3]))
+            other_x[1], line_x[3] = pair[:step], pair[step:]
+        elif s == 1:
+            outs, pair, fars[0] = lax.optimization_barrier((outs, pairs[1], fars[0]))
+            line_x[2], other_x[2] = pair[:step], pair[step:]
+            other_x[3] = move(other[3], over_x)
+        elif s == 2:
+            outs, other_x[3], fars[1] = lax.optimization_barrier((outs, other_x[3], fars[1]))
+            backs[1] = move((chips[1][: 2 * step] + fars[1].astype(F32)).astype(BF16), along(-1))
+        else:
+            outs, fars[2], backs[1] = lax.optimization_barrier((outs, fars[2], backs[1]))
+        keep, send, d_both, hid = outs
+        rows[s], grads[s] = (mine, theirs), (d_both, hid)
+        chips[s] = keep.astype(F32) + move(send, over_c).astype(F32)
+        fars[s] = move(chips[s][2 * step :].astype(BF16), over_y)
+    hids = [rows[s] + (grads[s][1],) for s in sequence]
+    boths = [rows[s] + (grads[s][0],) for s in sequence]
+    held = chips[2][: 2 * step] + fars[2].astype(F32)
+    passed = move(held.astype(BF16), along(1))
+    hids[-1] = hids[-1][:2] + (after(hids[-1][2], held, chips[3]),)
+    grad_down = weight_grads(hids, 1, width, units)
+    grad_down, fars[3], passed = lax.optimization_barrier((grad_down, fars[3], passed))
+    held = chips[3][: 2 * step] + fars[3].astype(F32) + passed.astype(F32)
+    backs[3] = move(held.astype(BF16), along(1))
+    boths[-1] = boths[-1][:2] + (after(boths[-1][2], grad_down, held),)
+    grad_gate = weight_grads(boths, 0, width, units)
+    grad_gate, backs[3] = lax.optimization_barrier((grad_gate, backs[3]))
+    total = chips[0][: 2 * step] + fars[0].astype(F32)
+    for back in backs.values():
+        total = total + back.astype(F32)
     total = total.astype(BF16)
     cross = move(total, over_x)
+    boths[-1] = boths[-1][:2] + (after(boths[-1][2], total),)
+    grad_up = weight_grads(boths, 0, width, units, 1)
+    grad_up, cross = lax.optimization_barrier((grad_up, cross))
     final = (
         total.astype(F32) + jnp.concatenate([cross[step:], cross[:step]], axis=0).astype(F32)
     ).astype(BF16)
     beside = move(final, over_c)
-    grad_gate, grad_up, grad_down = weight_grads(parts, width, units)
 
     pair = jnp.stack([final, beside]).reshape(2, 2, step, -1)
     pair = jnp.where(core == 0, pair, pair[::-1])
@@ -307,6 +383,7 @@
     whole = jnp.transpose(pair, (1, 0, 2, 3)).reshape(tok_rows, -1)
     grad_tokens = whole[:, :width]
     found = whole[:, None, width:]
+    named = routes[:, :, None] == ids
     grad_probs = jnp.sum(jnp.where(named, found, 0).astype(F32), axis=2).astype(BF16)
     shape = w_gate.shape
     return (
@@ -322,10 +399,10 @@
     tok_rows, top_count = routes.shape
     local_experts = w_gate.shape[0]
     slots = local_experts * slots_of(tok_rows, top_count, sources * local_experts)
-    fits = splits == 4 and sources % 2 == 0 and sources >= 4 and tok_rows % 64 == 0
+    fits = splits == 4 and sources == 8 and tok_rows % 64 == 0
     args = (tokens, grad_out, routes, probs, w_gate, w_up, w_down)
     if fits and slots >= tok_rows:
-        return gathered_body(sources // 2, *args)
+        return gathered_body(*args)
     return routed_body(*args)
 
 

time: 149 us -> 113 us (0.76)
  local copies, waits for them, and re-layouts: 21.8 us -> 3.67 us
  starting transfers between devices: 41.9 us -> 31.1 us
  Pallas kernels: 35.1 us -> 31.7 us
  other arithmetic: 6.93 us -> 4.76 us
    unnamed x85 -> x48, local copies, waits for them, and re-layouts: 19.7 us -> 2.48 us
    pallas_call x4, Pallas kernels: 24.8 us -> 11.6 us  [stage(): pl.pallas_call(functools.partial(stage_kernel, local_experts), out_shape=...]
    ppermute x41 -> x29, starting transfers between devices: 41.9 us -> 31.1 us  [move(): return lax.ppermute(value, axes, pairs)]
    pallas_call x1 -> x3, Pallas kernels: 10.2 us -> 17 us  [weight_grads(): pl.pallas_call(functools.partial(weights_kernel, len(parts)), grid=(tiles...]
    pallas_call x0 -> x1, Pallas kernels: none -> 3.04 us  [pack(): pl.pallas_call(functools.partial(pack_kernel, step), out_shape=(jax.Shape...]
    ppermute x41 -> x29, waiting for transfers between devices: 41.4 us -> 40.2 us  [move(): return lax.ppermute(value, axes, pairs)]
  transfers between devices with their start and end apart: 41 -> 29, of which waited for: 13 -> 18; matrix products, arithmetic and copies ran while one was open for 2% -> 4% of each run, Pallas kernels for 24% -> 25%
where the time goes in v2:
time: 113 us
  waiting for transfers between devices  40.2 us (36%)
  Pallas kernels  31.7 us (28%)
  starting transfers between devices  31.1 us (28%)
  other arithmetic  4.76 us (4%)
  local copies, waits for them, and re-layouts  3.67 us (3%)
  between operations  1.23 us (1%)
    ppermute x29, waiting for transfers between devices, move(): return lax.ppermute(value, axes, pairs)  40.2 us
    ppermute x29, starting transfers between devices, move(): return lax.ppermute(value, axes, pairs)  31.1 us
    pallas_call x3, Pallas kernels, weight_grads(): pl.pallas_call(functools.partial(weights_kernel, len(parts)), grid=(tiles...  17 us
    pallas_call x4, Pallas kernels, stage(): pl.pallas_call(functools.partial(stage_kernel, local_experts), out_shape=...  11.6 us
    pallas_call x1, Pallas kernels, pack(): pl.pallas_call(functools.partial(pack_kernel, step), out_shape=(jax.Shape...  3.04 us
    unnamed x48, local copies, waits for them, and re-layouts  2.48 us
    concatenate x1, other arithmetic, gathered_body(): jnp.concatenate([w_gate.reshape(units, width), w_up.reshape(units, width)...  2.29 us
  transfers between devices with their start and end apart: 29, of which 18 were waited for; matrix products, arithmetic and copies ran while one was open for 4% of the time, Pallas kernels for 25%

profile of v2, /device:TPU:0, one launch (start us, length us, event | category | flops | bytes accessed | tf_op | source)
XLA Modules:
  0.0 112.7 jit_solution(12413131000335264089)
XLA Ops:
  1.3 3.0 %pack.1 = (bf16[32,4224]{1,0:T(8,128)(2,1)}, bf16[32,4224]{1,0:T(8,128)(2,1)}, bf16[32,4224]{1,0:T(8,128)(2,1)}, bf16[32,4224]{1,0:T(8,128)(2,1)}) custom-call(s32[4]{0:T(128)} %pad_add_fusion.quarters, s32[8,128]{1,0:T(8,128)} %bitcast.31, bf16[8,128]{1,0:T(8,128)(2,1)} %bitcast.32, bf16[128,2048]{1,0:T(8,128)(2,1)} %tokens.1, bf16[128,2048]{1,0:T(8,128)(2,1)} %grad_out.1), custom_call_target="tpu_custom_call" | custom-call | tf_op jit(solution)/shard_map/pack/pallas_call | solution.py:258
  4.4 4.1 %collective-permute-start.2 = (bf16[32,4224]{1,0:T(8,128)(2,1)}, bf16[32,4224]{1,0:T(8,128)(2,1)S(1)}, u32[]{:S(2)}, u32[]{:S(2)}) collective-permute-start(bf16[32,4224]{1,0:T(8,128)(2,1)} %get-tuple-element.73), channel_id=1, source_target_pairs={{0,16},{1,17},{2,18},{3,19},{4,20},{5,21},{6,22},{7,23},{8,0},{9,1... | collective-permute-start | bytes 811016 | tf_op jit(solution)/shard_map/ppermute | solution.py:302
  11.7 2.3 %pad_maximum_fusion.gate_up = bf16[768,2048]{1,0:T(8,128)(2,1)S(1)} fusion(bf16[384,2048]{1,0:T(8,128)(2,1)} %bitcast.24, bf16[384,2048]{1,0:T(8,128)(2,1)} %bitcast.25), kind=kLoop, calls=%fused_computation | loop fusion | flops 6291456 | bytes 6291456 | tf_op jit(solution)/shard_map/concatenate | solution.py:311
  14.5 2.3 %collective-permute-start.6 = (bf16[32,4224]{1,0:T(8,128)(2,1)S(1)}, bf16[32,4224]{1,0:T(8,128)(2,1)S(1)}, u32[]{:S(2)}, u32[]{:S(2)}) collective-permute-start(bf16[32,4224]{1,0:T(8,128)(2,1)S(1)} %copy-done.19), channel_id=1, source_target_pairs={{0,8},{1,9},{2,10},{3,11},{4,12},{5,13},{6,14},{7,15},{8,24},{9,25... | collective-permute-start | bytes 811016 | tf_op jit(solution)/shard_map/ppermute | solution.py:302
  20.8 3.0 %collective-permute-done.1 = bf16[32,4224]{1,0:T(8,128)(2,1)S(1)} collective-permute-done((bf16[32,4224]{1,0:T(8,128)(2,1)}, bf16[32,4224]{1,0:T(8,128)(2,1)S(1)}, u32[]{:S(2)}, u32[]{:S(2)}) %collective-permute-start.1) | collective-permute-done | bytes 270368 | tf_op jit(solution)/shard_map/ppermute | solution.py:302
  23.9 5.3 %collective-permute-done.3 = bf16[32,4224]{1,0:T(8,128)(2,1)S(1)} collective-permute-done((bf16[32,4224]{1,0:T(8,128)(2,1)S(1)}, bf16[32,4224]{1,0:T(8,128)(2,1)S(1)}, u32[]{:S(2)}, u32[]{:S(2)}) %collective-permute-start.3) | collective-permute-done | bytes 270368 | tf_op jit(solution)/shard_map/ppermute | solution.py:302
  29.4 1.6 %collective-permute-start.7 = (bf16[64,4224]{1,0:T(8,128)(2,1)S(1)}, bf16[64,4224]{1,0:T(8,128)(2,1)S(1)}, u32[]{:S(2)}, u32[]{:S(2)}) collective-permute-start(bf16[64,4224]{1,0:T(8,128)(2,1)S(1)} %pad_maximum_fusion.6), channel_id=1, source_target_pairs={{0,2},{1,3},{2,0},{3,1},{4,6},{5,7},{6,4},{7,5},{8,10},{9,11},{10,... | collective-permute-start | bytes 1622024 | tf_op jit(solution)/shard_map/ppermute | solution.py:302
  33.1 2.9 %stage.4 = (bf16[128,2176]{1,0:T(8,128)(2,1)S(1)}, bf16[128,2176]{1,0:T(8,128)(2,1)S(1)}, bf16[256,768]{1,0:T(8,128)(2,1)S(1)}, bf16[256,384]{1,0:T(8,128)(2,1)S(1)}) custom-call(s32[1]{0:T(128)} %bitcast.base_ref, bf16[128,4224]{1,0:T(8,128)(2,1)S(1)} %constant_dynamic-update-slice_fusion.mine.refs_0_, ...), custom_call_target="tpu_custom_call" | custom-call | flops 2013265920 | bytes 4325376 | tf_op jit(solution)/shard_map/stage/pallas_call | solution.py:166
  36.1 4.2 %collective-permute-done.8 = bf16[32,4224]{1,0:T(8,128)(2,1)S(1)} collective-permute-done((bf16[32,4224]{1,0:T(8,128)(2,1)S(1)}, bf16[32,4224]{1,0:T(8,128)(2,1)S(1)}, u32[]{:S(2)}, u32[]{:S(2)}) %collective-permute-start.8) | collective-permute-done | bytes 270368 | tf_op jit(solution)/shard_map/ppermute | solution.py:302
  40.3 3.8 %collective-permute-done.7 = bf16[64,4224]{1,0:T(8,128)(2,1)S(1)} collective-permute-done((bf16[64,4224]{1,0:T(8,128)(2,1)S(1)}, bf16[64,4224]{1,0:T(8,128)(2,1)S(1)}, u32[]{:S(2)}, u32[]{:S(2)}) %collective-permute-start.7) | collective-permute-done | bytes 540704 | tf_op jit(solution)/shard_map/ppermute | solution.py:302
  48.0 1.6 %collective-permute-start.14 = (bf16[64,2176]{1,0:T(8,128)(2,1)S(1)}, bf16[64,2176]{1,0:T(8,128)(2,1)S(1)}, u32[]{:S(2)}, u32[]{:S(2)}) collective-permute-start(bf16[64,2176]{1,0:T(8,128)(2,1)S(1)} %slice.101), channel_id=1, source_target_pairs={{0,4},{1,5},{2,6},{3,7},{4,0},{5,1},{6,2},{7,3},{8,12},{9,13},{10,... | collective-permute-start | bytes 835592 | tf_op jit(solution)/shard_map/ppermute | solution.py:302
  49.6 2.9 %stage.5 = (bf16[128,2176]{1,0:T(8,128)(2,1)S(1)}, bf16[128,2176]{1,0:T(8,128)(2,1)S(1)}, bf16[256,768]{1,0:T(8,128)(2,1)S(1)}, bf16[256,384]{1,0:T(8,128)(2,1)S(1)}) custom-call(s32[1]{0:T(128)} %bitcast.base_ref, bf16[128,4224]{1,0:T(8,128)(2,1)S(1)} %pad_maximum_fusion.1.mine.refs_3_, bf16[128,4224]{1,0:T(8,128)(2,1)S(1)} %collective-permute-done.11.theirs.refs_4_, ...), custom_call_target="tpu_custom_call" | custom-call | flops 2013265920 | bytes 4325376 | tf_op jit(solution)/shard_map/stage/pallas_call | solution.py:166
  52.6 6.7 %collective-permute-done.13 = bf16[64,4224]{1,0:T(8,128)(2,1)S(1)} collective-permute-done((bf16[64,4224]{1,0:T(8,128)(2,1)S(1)}, bf16[64,4224]{1,0:T(8,128)(2,1)S(1)}, u32[]{:S(2)}, u32[]{:S(2)}) %collective-permute-start.13) | collective-permute-done | bytes 540704 | tf_op jit(solution)/shard_map/ppermute | solution.py:302
  61.4 1.6 %collective-permute-start.18 = (bf16[64,2176]{1,0:T(8,128)(2,1)S(1)}, bf16[64,2176]{1,0:T(8,128)(2,1)S(1)}, u32[]{:S(2)}, u32[]{:S(2)}) collective-permute-start(bf16[64,2176]{1,0:T(8,128)(2,1)S(1)} %slice.100), channel_id=1, source_target_pairs={{0,4},{1,5},{2,6},{3,7},{4,0},{5,1},{6,2},{7,3},{8,12},{9,13},{10,... | collective-permute-start | bytes 835592 | tf_op jit(solution)/shard_map/ppermute | solution.py:302
  64.4 2.9 %stage.6 = (bf16[128,2176]{1,0:T(8,128)(2,1)S(1)}, bf16[128,2176]{1,0:T(8,128)(2,1)S(1)}, bf16[256,768]{1,0:T(8,128)(2,1)S(1)}, bf16[256,384]{1,0:T(8,128)(2,1)S(1)}) custom-call(s32[1]{0:T(128)} %bitcast.base_ref, bf16[128,4224]{1,0:T(8,128)(2,1)S(1)} %pad_maximum_fusion.2.mine.refs_6_, bf16[128,4224]{1,0:T(8,128)(2,1)S(1)} %collective-permute-done.16.theirs.refs_7_, ...), custom_call_target="tpu_custom_call" | custom-call | flops 2013265920 | bytes 4325376 | tf_op jit(solution)/shard_map/stage/pallas_call | solution.py:166
  67.4 3.8 %collective-permute-done.17 = bf16[32,4224]{1,0:T(8,128)(2,1)S(1)} collective-permute-done((bf16[32,4224]{1,0:T(8,128)(2,1)S(1)}, bf16[32,4224]{1,0:T(8,128)(2,1)S(1)}, u32[]{:S(2)}, u32[]{:S(2)}) %collective-permute-start.17) | collective-permute-done | bytes 270368 | tf_op jit(solution)/shard_map/ppermute | solution.py:302
  71.9 2.0 %collective-permute-start.22 = (bf16[64,2176]{1,0:T(8,128)(2,1)S(1)}, bf16[64,2176]{1,0:T(8,128)(2,1)S(1)}, u32[]{:S(2)}, u32[]{:S(2)}) collective-permute-start(bf16[64,2176]{1,0:T(8,128)(2,1)S(1)} %fusion.2), channel_id=1, source_target_pairs={{0,8},{1,9},{2,10},{3,11},{4,12},{5,13},{6,14},{7,15},{8,24},{9,25... | collective-permute-start | bytes 835592 | tf_op jit(solution)/shard_map/ppermute | solution.py:302
  74.7 2.9 %stage.7 = (bf16[128,2176]{1,0:T(8,128)(2,1)S(1)}, bf16[128,2176]{1,0:T(8,128)(2,1)S(1)}, bf16[256,768]{1,0:T(8,128)(2,1)S(1)}, bf16[256,384]{1,0:T(8,128)(2,1)S(1)}) custom-call(s32[1]{0:T(128)} %bitcast.base_ref, bf16[128,4224]{1,0:T(8,128)(2,1)S(1)} %pad_maximum_fusion.3.mine.refs_9_, bf16[128,4224]{1,0:T(8,128)(2,1)S(1)} %collective-permute-done.20.theirs.refs_10_, ...), custom_call_target="tpu_custom_call" | custom-call | flops 2013265920 | bytes 4325376 | tf_op jit(solution)/shard_map/stage/pallas_call | solution.py:166
  77.6 4.0 %collective-permute-done.22 = bf16[64,2176]{1,0:T(8,128)(2,1)S(1)} collective-permute-done((bf16[64,2176]{1,0:T(8,128)(2,1)S(1)}, bf16[64,2176]{1,0:T(8,128)(2,1)S(1)}, u32[]{:S(2)}, u32[]{:S(2)}) %collective-permute-start.22) | collective-permute-done | bytes 278560 | tf_op jit(solution)/shard_map/ppermute | solution.py:302
  85.1 5.7 %weight_grads.3 = bf16[384,2048]{1,0:T(8,128)(2,1)} custom-call(bf16[128,4224]{1,0:T(8,128)(2,1)} %copy-done.4, bf16[128,4224]{1,0:T(8,128)(2,1)} %copy-done.3, bf16[256,384]{1,0:T(8,128)(2,1)} %copy-done.12, bf16[128,4224]{1,0:T(8,128)(2,1)} %copy-done, bf16[128,4224]{1,0:T(8,128)(2,1)} %copy-done.5, bf16[256,384]{1,0:T(8,128)(2,1)} %copy-done.13, ...), custom_call_target="tpu_custom_call" | custom-call | flops 1610612736 | bytes 5767168 | tf_op jit(solution)/shard_map/weight_grads/pallas_call | solution.py:206
  91.6 1.7 %collective-permute-done.24 = bf16[64,2176]{1,0:T(8,128)(2,1)S(1)} collective-permute-done((bf16[64,2176]{1,0:T(8,128)(2,1)S(1)}, bf16[64,2176]{1,0:T(8,128)(2,1)S(1)}, u32[]{:S(2)}, u32[]{:S(2)}) %collective-permute-start.24) | collective-permute-done | bytes 278560 | tf_op jit(solution)/shard_map/ppermute | solution.py:302
  94.8 5.7 %weight_grads.4 = bf16[384,2048]{1,0:T(8,128)(2,1)} custom-call(bf16[128,4224]{1,0:T(8,128)(2,1)} %copy-done.4, bf16[128,4224]{1,0:T(8,128)(2,1)} %copy-done.3, bf16[256,768]{1,0:T(8,128)(2,1)} %copy-done.8, bf16[128,4224]{1,0:T(8,128)(2,1)} %copy-done, bf16[128,4224]{1,0:T(8,128)(2,1)} %copy-done.5, bf16[256,768]{1,0:T(8,128)(2,1)} %copy-done.9, ...), custom_call_target="tpu_custom_call" | custom-call | flops 1610612736 | bytes 5767168 | tf_op jit(solution)/shard_map/weight_grads/pallas_call | solution.py:206
  101.5 1.6 %collective-permute-start.27 = (bf16[64,2176]{1,0:T(8,128)(2,1)S(1)}, bf16[64,2176]{1,0:T(8,128)(2,1)S(1)}, u32[]{:S(2)}, u32[]{:S(2)}) collective-permute-start(bf16[64,2176]{1,0:T(8,128)(2,1)S(1)} %fusion.5), channel_id=1, source_target_pairs={{0,2},{1,3},{2,0},{3,1},{4,6},{5,7},{6,4},{7,5},{8,10},{9,11},{10,... | collective-permute-start | bytes 835592 | tf_op jit(solution)/shard_map/ppermute | solution.py:302
  103.0 5.7 %weight_grads.5 = bf16[384,2048]{1,0:T(8,128)(2,1)} custom-call(bf16[128,4224]{1,0:T(8,128)(2,1)} %copy-done.4, bf16[128,4224]{1,0:T(8,128)(2,1)} %copy-done.3, bf16[256,768]{1,0:T(8,128)(2,1)} %copy-done.8, bf16[128,4224]{1,0:T(8,128)(2,1)} %copy-done, bf16[128,4224]{1,0:T(8,128)(2,1)} %copy-done.5, bf16[256,768]{1,0:T(8,128)(2,1)} %copy-done.9, ...), custom_call_target="tpu_custom_call" | custom-call | flops 1610612736 | bytes 5767168 | tf_op jit(solution)/shard_map/weight_grads/pallas_call | solution.py:206
  (123 shorter events, 30.2 us)
Async XLA Ops:
  4.4 10.1 %collective-permute-start.2 = (bf16[32,4224]{1,0:T(8,128)(2,1)}, bf16[32,4224]{1,0:T(8,128)(2,1)S(1)}, u32[]{:S(2)}, u32[]{:S(2)}) collective-permute-start(bf16[32,4224]{1,0:T(8,128)(2,1)} %get-tuple-element.73), channel_id=1, source_target_pairs={{0,16},{1,17},{2,18},{3,19},{4,20},{5,21},{6,22},{7,23},{8,0},{9,1... | collective-permute-start | bytes 811016 | tf_op jit(solution)/shard_map/ppermute | solution.py:302
  8.5 10.9 %collective-permute-start = (bf16[32,4224]{1,0:T(8,128)(2,1)}, bf16[32,4224]{1,0:T(8,128)(2,1)S(1)}, u32[]{:S(2)}, u32[]{:S(2)}) collective-permute-start(bf16[32,4224]{1,0:T(8,128)(2,1)} %get-tuple-element.73), channel_id=1, source_target_pairs={{0,4},{1,5},{2,6},{3,7},{4,0},{5,1},{6,2},{7,3},{8,12},{9,13},{10,... | collective-permute-start | bytes 811016 | tf_op jit(solution)/shard_map/ppermute | solution.py:302
  10.0 13.9 %collective-permute-start.1 = (bf16[32,4224]{1,0:T(8,128)(2,1)}, bf16[32,4224]{1,0:T(8,128)(2,1)S(1)}, u32[]{:S(2)}, u32[]{:S(2)}) collective-permute-start(bf16[32,4224]{1,0:T(8,128)(2,1)} %get-tuple-element.65), channel_id=1, source_target_pairs={{0,4},{1,5},{2,6},{3,7},{4,0},{5,1},{6,2},{7,3},{8,12},{9,13},{10,... | collective-permute-start | bytes 811016 | tf_op jit(solution)/shard_map/ppermute | solution.py:302
  14.5 14.8 %collective-permute-start.6 = (bf16[32,4224]{1,0:T(8,128)(2,1)S(1)}, bf16[32,4224]{1,0:T(8,128)(2,1)S(1)}, u32[]{:S(2)}, u32[]{:S(2)}) collective-permute-start(bf16[32,4224]{1,0:T(8,128)(2,1)S(1)} %copy-done.19), channel_id=1, source_target_pairs={{0,8},{1,9},{2,10},{3,11},{4,12},{5,13},{6,14},{7,15},{8,24},{9,25... | collective-permute-start | bytes 811016 | tf_op jit(solution)/shard_map/ppermute | solution.py:302
  16.8 12.4 %collective-permute-start.3 = (bf16[32,4224]{1,0:T(8,128)(2,1)S(1)}, bf16[32,4224]{1,0:T(8,128)(2,1)S(1)}, u32[]{:S(2)}, u32[]{:S(2)}) collective-permute-start(bf16[32,4224]{1,0:T(8,128)(2,1)S(1)} %collective-permute-done.2), channel_id=1, source_target_pairs={{0,16},{1,17},{2,18},{3,19},{4,20},{5,21},{6,22},{7,23},{8,0},{9,1... | collective-permute-start | bytes 811016 | tf_op jit(solution)/shard_map/ppermute | solution.py:302
  17.8 11.5 %collective-permute-start.5 = (bf16[32,4224]{1,0:T(8,128)(2,1)S(1)}, bf16[32,4224]{1,0:T(8,128)(2,1)S(1)}, u32[]{:S(2)}, u32[]{:S(2)}) collective-permute-start(bf16[32,4224]{1,0:T(8,128)(2,1)S(1)} %collective-permute-done.2), channel_id=1, source_target_pairs={{0,4},{1,5},{2,6},{3,7},{4,0},{5,1},{6,2},{7,3},{8,12},{9,13},{10,... | collective-permute-start | bytes 811016 | tf_op jit(solution)/shard_map/ppermute | solution.py:302
  19.3 24.9 %collective-permute-start.10 = (bf16[32,4224]{1,0:T(8,128)(2,1)S(1)}, bf16[32,4224]{1,0:T(8,128)(2,1)S(1)}, u32[]{:S(2)}, u32[]{:S(2)}) collective-permute-start(bf16[32,4224]{1,0:T(8,128)(2,1)S(1)} %collective-permute-done.2), channel_id=1, source_target_pairs={{0,2},{1,3},{2,0},{3,1},{4,6},{5,7},{6,4},{7,5},{8,10},{9,11},{10,... | collective-permute-start | bytes 811016 | tf_op jit(solution)/shard_map/ppermute | solution.py:302
  29.3 3.8 %collective-permute-start.4 = (bf16[64,4224]{1,0:T(8,128)(2,1)S(1)}, bf16[64,4224]{1,0:T(8,128)(2,1)S(1)}, u32[]{:S(2)}, u32[]{:S(2)}) collective-permute-start(bf16[64,4224]{1,0:T(8,128)(2,1)S(1)} %pad_maximum_fusion.5), channel_id=1, source_target_pairs={{0,1},{1,0},{2,3},{3,2},{4,5},{5,4},{6,7},{7,6},{8,9},{9,8},{10,11... | collective-permute-start | bytes 1622024 | tf_op jit(solution)/shard_map/ppermute | solution.py:302
  29.4 14.7 %collective-permute-start.7 = (bf16[64,4224]{1,0:T(8,128)(2,1)S(1)}, bf16[64,4224]{1,0:T(8,128)(2,1)S(1)}, u32[]{:S(2)}, u32[]{:S(2)}) collective-permute-start(bf16[64,4224]{1,0:T(8,128)(2,1)S(1)} %pad_maximum_fusion.6), channel_id=1, source_target_pairs={{0,2},{1,3},{2,0},{3,1},{4,6},{5,7},{6,4},{7,5},{8,10},{9,11},{10,... | collective-permute-start | bytes 1622024 | tf_op jit(solution)/shard_map/ppermute | solution.py:302
  31.0 9.3 %collective-permute-start.8 = (bf16[32,4224]{1,0:T(8,128)(2,1)S(1)}, bf16[32,4224]{1,0:T(8,128)(2,1)S(1)}, u32[]{:S(2)}, u32[]{:S(2)}) collective-permute-start(bf16[32,4224]{1,0:T(8,128)(2,1)S(1)} %collective-permute-done.6), channel_id=1, source_target_pairs={{0,4},{1,5},{2,6},{3,7},{4,0},{5,1},{6,2},{7,3},{8,12},{9,13},{10,... | collective-permute-start | bytes 811016 | tf_op jit(solution)/shard_map/ppermute | solution.py:302
  32.5 12.9 %collective-permute-start.12 = (bf16[32,4224]{1,0:T(8,128)(2,1)S(1)}, bf16[32,4224]{1,0:T(8,128)(2,1)S(1)}, u32[]{:S(2)}, u32[]{:S(2)}) collective-permute-start(bf16[32,4224]{1,0:T(8,128)(2,1)S(1)} %collective-permute-done.3), channel_id=1, source_target_pairs={{0,4},{1,5},{2,6},{3,7},{4,0},{5,1},{6,2},{7,3},{8,12},{9,13},{10,... | collective-permute-start | bytes 811016 | tf_op jit(solution)/shard_map/ppermute | solution.py:302
  44.3 5.3 %collective-permute-start.11 = (bf16[128,4224]{1,0:T(8,128)(2,1)S(1)}, bf16[128,4224]{1,0:T(8,128)(2,1)S(1)}, u32[]{:S(2)}, u32[]{:S(2)}) collective-permute-start(bf16[128,4224]{1,0:T(8,128)(2,1)S(1)} %pad_maximum_fusion.1.mine.refs_3_), channel_id=1, source_target_pairs={{0,1},{1,0},{2,3},{3,2},{4,5},{5,4},{6,7},{7,6},{8,9},{9,8},{10,11... | collective-permute-start | bytes 3244040 | tf_op jit(solution)/shard_map/ppermute | solution.py:302
  44.4 3.5 %collective-permute-start.9 = (bf16[128,2176]{1,0:T(8,128)(2,1)S(1)}, bf16[128,2176]{1,0:T(8,128)(2,1)S(1)}, u32[]{:S(2)}, u32[]{:S(2)}) collective-permute-start(bf16[128,2176]{1,0:T(8,128)(2,1)S(1)} %get-tuple-element.75), channel_id=1, source_target_pairs={{0,1},{1,0},{2,3},{3,2},{4,5},{5,4},{6,7},{7,6},{8,9},{9,8},{10,11... | collective-permute-start | bytes 1671176 | tf_op jit(solution)/shard_map/ppermute | solution.py:302
  45.4 13.9 %collective-permute-start.13 = (bf16[64,4224]{1,0:T(8,128)(2,1)S(1)}, bf16[64,4224]{1,0:T(8,128)(2,1)S(1)}, u32[]{:S(2)}, u32[]{:S(2)}) collective-permute-start(bf16[64,4224]{1,0:T(8,128)(2,1)S(1)} %pad_maximum_fusion.7), channel_id=1, source_target_pairs={{0,2},{1,3},{2,0},{3,1},{4,6},{5,7},{6,4},{7,5},{8,10},{9,11},{10,... | collective-permute-start | bytes 1622024 | tf_op jit(solution)/shard_map/ppermute | solution.py:302
  48.0 11.2 %collective-permute-start.14 = (bf16[64,2176]{1,0:T(8,128)(2,1)S(1)}, bf16[64,2176]{1,0:T(8,128)(2,1)S(1)}, u32[]{:S(2)}, u32[]{:S(2)}) collective-permute-start(bf16[64,2176]{1,0:T(8,128)(2,1)S(1)} %slice.101), channel_id=1, source_target_pairs={{0,4},{1,5},{2,6},{3,7},{4,0},{5,1},{6,2},{7,3},{8,12},{9,13},{10,... | collective-permute-start | bytes 835592 | tf_op jit(solution)/shard_map/ppermute | solution.py:302
  59.4 5.0 %collective-permute-start.16 = (bf16[128,4224]{1,0:T(8,128)(2,1)S(1)}, bf16[128,4224]{1,0:T(8,128)(2,1)S(1)}, u32[]{:S(2)}, u32[]{:S(2)}) collective-permute-start(bf16[128,4224]{1,0:T(8,128)(2,1)S(1)} %pad_maximum_fusion.2.mine.refs_6_), channel_id=1, source_target_pairs={{0,1},{1,0},{2,3},{3,2},{4,5},{5,4},{6,7},{7,6},{8,9},{9,8},{10,11... | collective-permute-start | bytes 3244040 | tf_op jit(solution)/shard_map/ppermute | solution.py:302
  61.4 9.8 %collective-permute-start.18 = (bf16[64,2176]{1,0:T(8,128)(2,1)S(1)}, bf16[64,2176]{1,0:T(8,128)(2,1)S(1)}, u32[]{:S(2)}, u32[]{:S(2)}) collective-permute-start(bf16[64,2176]{1,0:T(8,128)(2,1)S(1)} %slice.100), channel_id=1, source_target_pairs={{0,4},{1,5},{2,6},{3,7},{4,0},{5,1},{6,2},{7,3},{8,12},{9,13},{10,... | collective-permute-start | bytes 835592 | tf_op jit(solution)/shard_map/ppermute | solution.py:302
  62.9 8.2 %collective-permute-start.17 = (bf16[32,4224]{1,0:T(8,128)(2,1)S(1)}, bf16[32,4224]{1,0:T(8,128)(2,1)S(1)}, u32[]{:S(2)}, u32[]{:S(2)}) collective-permute-start(bf16[32,4224]{1,0:T(8,128)(2,1)S(1)} %collective-permute-done.8), channel_id=1, source_target_pairs={{0,2},{1,3},{2,0},{3,1},{4,6},{5,7},{6,4},{7,5},{8,10},{9,11},{10,... | collective-permute-start | bytes 811016 | tf_op jit(solution)/shard_map/ppermute | solution.py:302
  71.9 9.7 %collective-permute-start.22 = (bf16[64,2176]{1,0:T(8,128)(2,1)S(1)}, bf16[64,2176]{1,0:T(8,128)(2,1)S(1)}, u32[]{:S(2)}, u32[]{:S(2)}) collective-permute-start(bf16[64,2176]{1,0:T(8,128)(2,1)S(1)} %fusion.2), channel_id=1, source_target_pairs={{0,8},{1,9},{2,10},{3,11},{4,12},{5,13},{6,14},{7,15},{8,24},{9,25... | collective-permute-start | bytes 835592 | tf_op jit(solution)/shard_map/ppermute | solution.py:302
  74.1 8.4 %collective-permute-start.21 = (bf16[64,2176]{1,0:T(8,128)(2,1)S(1)}, bf16[64,2176]{1,0:T(8,128)(2,1)S(1)}, u32[]{:S(2)}, u32[]{:S(2)}) collective-permute-start(bf16[64,2176]{1,0:T(8,128)(2,1)S(1)} %slice.99), channel_id=1, source_target_pairs={{0,4},{1,5},{2,6},{3,7},{4,0},{5,1},{6,2},{7,3},{8,12},{9,13},{10,... | collective-permute-start | bytes 835592 | tf_op jit(solution)/shard_map/ppermute | solution.py:302
  82.5 9.1 %collective-permute-start.25 = (bf16[64,2176]{1,0:T(8,128)(2,1)S(1)}, bf16[64,2176]{1,0:T(8,128)(2,1)S(1)}, u32[]{:S(2)}, u32[]{:S(2)}) collective-permute-start(bf16[64,2176]{1,0:T(8,128)(2,1)S(1)} %slice_add_fusion.1), channel_id=1, source_target_pairs={{0,16},{1,17},{2,18},{3,19},{4,20},{5,21},{6,22},{7,23},{8,0},{9,1... | collective-permute-start | bytes 835592 | tf_op jit(solution)/shard_map/ppermute | solution.py:302
  84.6 8.8 %collective-permute-start.24 = (bf16[64,2176]{1,0:T(8,128)(2,1)S(1)}, bf16[64,2176]{1,0:T(8,128)(2,1)S(1)}, u32[]{:S(2)}, u32[]{:S(2)}) collective-permute-start(bf16[64,2176]{1,0:T(8,128)(2,1)S(1)} %slice.98), channel_id=1, source_target_pairs={{0,4},{1,5},{2,6},{3,7},{4,0},{5,1},{6,2},{7,3},{8,12},{9,13},{10,... | collective-permute-start | bytes 835592 | tf_op jit(solution)/shard_map/ppermute | solution.py:302
  93.4 7.9 %collective-permute-start.26 = (bf16[64,2176]{1,0:T(8,128)(2,1)S(1)}, bf16[64,2176]{1,0:T(8,128)(2,1)S(1)}, u32[]{:S(2)}, u32[]{:S(2)}) collective-permute-start(bf16[64,2176]{1,0:T(8,128)(2,1)S(1)} %fusion.1), channel_id=1, source_target_pairs={{0,16},{1,17},{2,18},{3,19},{4,20},{5,21},{6,22},{7,23},{8,0},{9,1... | collective-permute-start | bytes 835592 | tf_op jit(solution)/shard_map/ppermute | solution.py:302
  101.5 7.2 %collective-permute-start.27 = (bf16[64,2176]{1,0:T(8,128)(2,1)S(1)}, bf16[64,2176]{1,0:T(8,128)(2,1)S(1)}, u32[]{:S(2)}, u32[]{:S(2)}) collective-permute-start(bf16[64,2176]{1,0:T(8,128)(2,1)S(1)} %fusion.5), channel_id=1, source_target_pairs={{0,2},{1,3},{2,0},{3,1},{4,6},{5,7},{6,4},{7,5},{8,10},{9,11},{10,... | collective-permute-start | bytes 835592 | tf_op jit(solution)/shard_map/ppermute | solution.py:302
  (26 other events, 115.0 us)

commit v3 on v2

--- a/solution.py
+++ b/solution.py
@@ -312,18 +312,14 @@
     down = w_down.reshape(units, width)
     base = (expert * local_experts).astype(jnp.int32).reshape(1)
 
-    line = {0: here, 1: move(here, along(1)), }
-    line[3] = move(after(here, line[1]), along(-1))
-    other, line_x, other_x = {0: move(here, over_y)}, {0: near}, {0: move(near, over_y)}
-    line_x[1] = move(line[1], over_x)
+    line = {0: here, 1: move(here, along(1))}
     line[2] = move(line[1], along(1))
-    for s in (1, 3, 2):
-        other[s] = move(line[s], over_y)
-
-    pairs = [
-        move(jnp.concatenate(v, axis=0), over_x)
-        for v in ([other[1], line[3]], [line[2], other[2]])
-    ]
+    line[3] = move(after(here, line[2]), along(-1))
+    other = {s: move(line[s], over_y) for s in range(lines)}
+    line_x = {0: near, 1: move(line[1], over_x), 3: move(after(near, line[3]), along(-1))}
+    other_x = {0: move(near, over_y)}
+    ready, line_x[1], gate_up = lax.optimization_barrier((other[1], line_x[1], gate_up))
+    first = move(jnp.concatenate([ready, line[2]], axis=0), over_x)
     rows, grads, chips, fars, backs = {}, {}, {}, {}, {}
     sequence = list(range(lines))
     for s in sequence:
@@ -334,31 +330,34 @@
             theirs = jnp.concatenate(rest + [move(mine[2 * step :], over_c)], axis=0)
         else:
             theirs = move(mine, over_c)
-        wait = [chips[s - 1]] if s else []
-        outs = stage(after(base, *wait), mine, theirs, gate_up, down, local_experts)
-        if s == 0:
-            outs, pair, other[3] = lax.optimization_barrier((outs, pairs[0], other[3]))
-            other_x[1], line_x[3] = pair[:step], pair[step:]
-        elif s == 1:
-            outs, pair, fars[0] = lax.optimization_barrier((outs, pairs[1], fars[0]))
-            line_x[2], other_x[2] = pair[:step], pair[step:]
-            other_x[3] = move(other[3], over_x)
-        elif s == 2:
-            outs, other_x[3], fars[1] = lax.optimization_barrier((outs, other_x[3], fars[1]))
-            backs[1] = move((chips[1][: 2 * step] + fars[1].astype(F32)).astype(BF16), along(-1))
-        else:
-            outs, fars[2], backs[1] = lax.optimization_barrier((outs, fars[2], backs[1]))
-        keep, send, d_both, hid = outs
+        wait = [chips[s - 1]] if s > 1 else []
+        keep, send, d_both, hid = stage(after(base, *wait), mine, theirs, gate_up, down, local_experts)
         rows[s], grads[s] = (mine, theirs), (d_both, hid)
         chips[s] = keep.astype(F32) + move(send, over_c).astype(F32)
         fars[s] = move(chips[s][2 * step :].astype(BF16), over_y)
+        if s == 0:
+            _, pair, other[2], other[3], line_x[3] = lax.optimization_barrier(
+                (hid, first, other[2], other[3], line_x[3])
+            )
+            other_x[1], line_x[2] = pair[:step], pair[step:]
+            second = move(jnp.concatenate([other[2], other[3]], axis=0), over_x)
+        elif s == 1:
+            _, pair, fars[0] = lax.optimization_barrier((hid, second, fars[0]))
+            other_x[2], other_x[3] = pair[:step], pair[step:]
+        elif s == 2:
+            _, fars[1] = lax.optimization_barrier((hid, fars[1]))
+            backs[1] = move((chips[1][: 2 * step] + fars[1].astype(F32)).astype(BF16), along(-1))
+        elif s == 3:
+            _, fars[2] = lax.optimization_barrier((hid, fars[2]))
     hids = [rows[s] + (grads[s][1],) for s in sequence]
     boths = [rows[s] + (grads[s][0],) for s in sequence]
     held = chips[2][: 2 * step] + fars[2].astype(F32)
     passed = move(held.astype(BF16), along(1))
     hids[-1] = hids[-1][:2] + (after(hids[-1][2], held, chips[3]),)
     grad_down = weight_grads(hids, 1, width, units)
-    grad_down, fars[3], passed = lax.optimization_barrier((grad_down, fars[3], passed))
+    grad_down, fars[3], passed, backs[1] = lax.optimization_barrier(
+        (grad_down, fars[3], passed, backs[1])
+    )
     held = chips[3][: 2 * step] + fars[3].astype(F32) + passed.astype(F32)
     backs[3] = move(held.astype(BF16), along(1))
     boths[-1] = boths[-1][:2] + (after(boths[-1][2], grad_down, held),)

time: 113 us -> 105 us (0.929)
  waiting for transfers between devices: 40.2 us -> 30.8 us
    ppermute x29, waiting for transfers between devices: 40.2 us -> 30.8 us  [move(): return lax.ppermute(value, axes, pairs)]
  transfers between devices with their start and end apart: 29 -> 29, of which waited for: 18 -> 13; matrix products, arithmetic and copies ran while one was open for 4% -> 4% of each run, Pallas kernels for 25% -> 27%
where the time goes in v3:
time: 105 us
  starting transfers between devices  32.2 us (31%)
  Pallas kernels  31.8 us (30%)
  waiting for transfers between devices  30.8 us (29%)
  other arithmetic  4.74 us (5%)
  local copies, waits for them, and re-layouts  3.67 us (3%)
  between operations  1.29 us (1%)
    ppermute x29, starting transfers between devices, move(): return lax.ppermute(value, axes, pairs)  32.2 us
    ppermute x29, waiting for transfers between devices, move(): return lax.ppermute(value, axes, pairs)  30.8 us
    pallas_call x3, Pallas kernels, weight_grads(): pl.pallas_call(functools.partial(weights_kernel, len(parts)), grid=(tiles...  17 us
    pallas_call x4, Pallas kernels, stage(): pl.pallas_call(functools.partial(stage_kernel, local_experts), out_shape=...  11.7 us
    pallas_call x1, Pallas kernels, pack(): pl.pallas_call(functools.partial(pack_kernel, step), out_shape=(jax.Shape...  3.04 us
    unnamed x48, local copies, waits for them, and re-layouts  2.48 us
    concatenate x1, other arithmetic, gathered_body(): jnp.concatenate([w_gate.reshape(units, width), w_up.reshape(units, width)...  2.25 us
  transfers between devices with their start and end apart: 29, of which 13 were waited for; matrix products, arithmetic and copies ran while one was open for 4% of the time, Pallas kernels for 27%

profile of v3, /device:TPU:0, one launch (start us, length us, event | category | flops | bytes accessed | tf_op | source)
XLA Modules:
  0.0 104.5 jit_solution(7213699706221512097)
XLA Ops:
  1.3 3.0 %pack.1 = (bf16[32,4224]{1,0:T(8,128)(2,1)}, bf16[32,4224]{1,0:T(8,128)(2,1)}, bf16[32,4224]{1,0:T(8,128)(2,1)}, bf16[32,4224]{1,0:T(8,128)(2,1)}) custom-call(s32[4]{0:T(128)} %pad_add_fusion.quarters, s32[8,128]{1,0:T(8,128)} %bitcast.31, bf16[8,128]{1,0:T(8,128)(2,1)} %bitcast.32, bf16[128,2048]{1,0:T(8,128)(2,1)} %tokens.1, bf16[128,2048]{1,0:T(8,128)(2,1)} %grad_out.1), custom_call_target="tpu_custom_call" | custom-call | tf_op jit(solution)/shard_map/pack/pallas_call | solution.py:258
  4.4 4.1 %collective-permute-start.2 = (bf16[32,4224]{1,0:T(8,128)(2,1)}, bf16[32,4224]{1,0:T(8,128)(2,1)S(1)}, u32[]{:S(2)}, u32[]{:S(2)}) collective-permute-start(bf16[32,4224]{1,0:T(8,128)(2,1)} %get-tuple-element.63), channel_id=1, source_target_pairs={{0,16},{1,17},{2,18},{3,19},{4,20},{5,21},{6,22},{7,23},{8,0},{9,1... | collective-permute-start | bytes 811016 | tf_op jit(solution)/shard_map/ppermute | solution.py:302
  11.7 2.3 %pad_maximum_fusion.gate_up = bf16[768,2048]{1,0:T(8,128)(2,1)S(1)} fusion(bf16[384,2048]{1,0:T(8,128)(2,1)} %bitcast.24, bf16[384,2048]{1,0:T(8,128)(2,1)} %bitcast.25), kind=kLoop, calls=%fused_computation | loop fusion | flops 6291456 | bytes 6291456 | tf_op jit(solution)/shard_map/concatenate | solution.py:311
  14.5 3.3 %collective-permute-start.3 = (bf16[32,4224]{1,0:T(8,128)(2,1)S(1)}, bf16[32,4224]{1,0:T(8,128)(2,1)S(1)}, u32[]{:S(2)}, u32[]{:S(2)}) collective-permute-start(bf16[32,4224]{1,0:T(8,128)(2,1)S(1)} %collective-permute-done.2), channel_id=1, source_target_pairs={{0,16},{1,17},{2,18},{3,19},{4,20},{5,21},{6,22},{7,23},{8,0},{9,1... | collective-permute-start | bytes 811016 | tf_op jit(solution)/shard_map/ppermute | solution.py:302
  20.8 3.0 %collective-permute-done.1 = bf16[32,4224]{1,0:T(8,128)(2,1)S(1)} collective-permute-done((bf16[32,4224]{1,0:T(8,128)(2,1)}, bf16[32,4224]{1,0:T(8,128)(2,1)S(1)}, u32[]{:S(2)}, u32[]{:S(2)}) %collective-permute-start.1) | collective-permute-done | bytes 270368 | tf_op jit(solution)/shard_map/ppermute | solution.py:302
  24.0 4.2 %collective-permute-done.5 = bf16[32,4224]{1,0:T(8,128)(2,1)S(1)} collective-permute-done((bf16[32,4224]{1,0:T(8,128)(2,1)S(1)}, bf16[32,4224]{1,0:T(8,128)(2,1)S(1)}, u32[]{:S(2)}, u32[]{:S(2)}) %collective-permute-start.5) | collective-permute-done | bytes 270368 | tf_op jit(solution)/shard_map/ppermute | solution.py:302
  31.4 4.8 %collective-permute-done.10 = bf16[32,4224]{1,0:T(8,128)(2,1)S(1)} collective-permute-done((bf16[32,4224]{1,0:T(8,128)(2,1)S(1)}, bf16[32,4224]{1,0:T(8,128)(2,1)S(1)}, u32[]{:S(2)}, u32[]{:S(2)}) %collective-permute-start.10) | collective-permute-done | bytes 270368 | tf_op jit(solution)/shard_map/ppermute | solution.py:302
  37.7 2.9 %stage.4 = (bf16[128,2176]{1,0:T(8,128)(2,1)S(1)}, bf16[128,2176]{1,0:T(8,128)(2,1)S(1)}, bf16[256,768]{1,0:T(8,128)(2,1)S(1)}, bf16[256,384]{1,0:T(8,128)(2,1)S(1)}) custom-call(s32[1]{0:T(128)} %bitcast.base_ref, bf16[128,4224]{1,0:T(8,128)(2,1)S(1)} %constant_dynamic-update-slice_fusion.mine.refs_0_, ...), custom_call_target="tpu_custom_call" | custom-call | flops 2013265920 | bytes 4325376 | tf_op jit(solution)/shard_map/stage/pallas_call | solution.py:166
  41.2 2.3 %collective-permute-done.12 = bf16[32,4224]{1,0:T(8,128)(2,1)S(1)} collective-permute-done((bf16[32,4224]{1,0:T(8,128)(2,1)S(1)}, bf16[32,4224]{1,0:T(8,128)(2,1)S(1)}, u32[]{:S(2)}, u32[]{:S(2)}) %collective-permute-start.12) | collective-permute-done | bytes 270368 | tf_op jit(solution)/shard_map/ppermute | solution.py:302
  47.4 1.6 %collective-permute-start.15 = (bf16[64,2176]{1,0:T(8,128)(2,1)S(1)}, bf16[64,2176]{1,0:T(8,128)(2,1)S(1)}, u32[]{:S(2)}, u32[]{:S(2)}) collective-permute-start(bf16[64,2176]{1,0:T(8,128)(2,1)S(1)} %slice.101), channel_id=1, source_target_pairs={{0,4},{1,5},{2,6},{3,7},{4,0},{5,1},{6,2},{7,3},{8,12},{9,13},{10,... | collective-permute-start | bytes 835592 | tf_op jit(solution)/shard_map/ppermute | solution.py:302
  49.0 2.9 %stage.5 = (bf16[128,2176]{1,0:T(8,128)(2,1)S(1)}, bf16[128,2176]{1,0:T(8,128)(2,1)S(1)}, bf16[256,768]{1,0:T(8,128)(2,1)S(1)}, bf16[256,384]{1,0:T(8,128)(2,1)S(1)}) custom-call(s32[1]{0:T(128)} %bitcast.base_ref, bf16[128,4224]{1,0:T(8,128)(2,1)S(1)} %pad_maximum_fusion.1.mine.refs_3_, bf16[128,4224]{1,0:T(8,128)(2,1)S(1)} %collective-permute-done.13.theirs.refs_4_, ...), custom_call_target="tpu_custom_call" | custom-call | flops 2013265920 | bytes 4325376 | tf_op jit(solution)/shard_map/stage/pallas_call | solution.py:166
  52.0 6.6 %collective-permute-done.14 = bf16[64,4224]{1,0:T(8,128)(2,1)S(1)} collective-permute-done((bf16[64,4224]{1,0:T(8,128)(2,1)S(1)}, bf16[64,4224]{1,0:T(8,128)(2,1)S(1)}, u32[]{:S(2)}, u32[]{:S(2)}) %collective-permute-start.14) | collective-permute-done | bytes 540704 | tf_op jit(solution)/shard_map/ppermute | solution.py:302
  59.0 1.6 %collective-permute-start.24 = (bf16[64,2176]{1,0:T(8,128)(2,1)S(1)}, bf16[64,2176]{1,0:T(8,128)(2,1)S(1)}, u32[]{:S(2)}, u32[]{:S(2)}) collective-permute-start(bf16[64,2176]{1,0:T(8,128)(2,1)S(1)} %slice.98), channel_id=1, source_target_pairs={{0,4},{1,5},{2,6},{3,7},{4,0},{5,1},{6,2},{7,3},{8,12},{9,13},{10,... | collective-permute-start | bytes 835592 | tf_op jit(solution)/shard_map/ppermute | solution.py:302
  61.5 2.9 %stage.6 = (bf16[128,2176]{1,0:T(8,128)(2,1)S(1)}, bf16[128,2176]{1,0:T(8,128)(2,1)S(1)}, bf16[256,768]{1,0:T(8,128)(2,1)S(1)}, bf16[256,384]{1,0:T(8,128)(2,1)S(1)}) custom-call(s32[1]{0:T(128)} %bitcast.base_ref, bf16[128,4224]{1,0:T(8,128)(2,1)S(1)} %pad_maximum_fusion.2.mine.refs_6_, bf16[128,4224]{1,0:T(8,128)(2,1)S(1)} %collective-permute-done.16.theirs.refs_7_, ...), custom_call_target="tpu_custom_call" | custom-call | flops 2013265920 | bytes 4325376 | tf_op jit(solution)/shard_map/stage/pallas_call | solution.py:166
  65.2 2.9 %collective-permute-done.24 = bf16[64,2176]{1,0:T(8,128)(2,1)S(1)} collective-permute-done((bf16[64,2176]{1,0:T(8,128)(2,1)S(1)}, bf16[64,2176]{1,0:T(8,128)(2,1)S(1)}, u32[]{:S(2)}, u32[]{:S(2)}) %collective-permute-start.24) | collective-permute-done | bytes 278560 | tf_op jit(solution)/shard_map/ppermute | solution.py:302
  68.3 1.6 %collective-permute-start.20 = (bf16[64,2176]{1,0:T(8,128)(2,1)S(1)}, bf16[64,2176]{1,0:T(8,128)(2,1)S(1)}, u32[]{:S(2)}, u32[]{:S(2)}) collective-permute-start(bf16[64,2176]{1,0:T(8,128)(2,1)S(1)} %slice.100), channel_id=1, source_target_pairs={{0,4},{1,5},{2,6},{3,7},{4,0},{5,1},{6,2},{7,3},{8,12},{9,13},{10,... | collective-permute-start | bytes 835592 | tf_op jit(solution)/shard_map/ppermute | solution.py:302
  71.3 2.9 %stage.7 = (bf16[128,2176]{1,0:T(8,128)(2,1)S(1)}, bf16[128,2176]{1,0:T(8,128)(2,1)S(1)}, bf16[256,768]{1,0:T(8,128)(2,1)S(1)}, bf16[256,384]{1,0:T(8,128)(2,1)S(1)}) custom-call(s32[1]{0:T(128)} %bitcast.base_ref, bf16[128,4224]{1,0:T(8,128)(2,1)S(1)} %pad_maximum_fusion.3.mine.refs_9_, bf16[128,4224]{1,0:T(8,128)(2,1)S(1)} %collective-permute-done.18.theirs.refs_10_, ...), custom_call_target="tpu_custom_call" | custom-call | flops 2013265920 | bytes 4325376 | tf_op jit(solution)/shard_map/stage/pallas_call | solution.py:166
  74.3 2.3 %collective-permute-done.20 = bf16[64,2176]{1,0:T(8,128)(2,1)S(1)} collective-permute-done((bf16[64,2176]{1,0:T(8,128)(2,1)S(1)}, bf16[64,2176]{1,0:T(8,128)(2,1)S(1)}, u32[]{:S(2)}, u32[]{:S(2)}) %collective-permute-start.20) | collective-permute-done | bytes 278560 | tf_op jit(solution)/shard_map/ppermute | solution.py:302
  76.7 2.1 %collective-permute-start.23 = (bf16[64,2176]{1,0:T(8,128)(2,1)S(1)}, bf16[64,2176]{1,0:T(8,128)(2,1)S(1)}, u32[]{:S(2)}, u32[]{:S(2)}) collective-permute-start(bf16[64,2176]{1,0:T(8,128)(2,1)S(1)} %slice_add_fusion.2), channel_id=1, source_target_pairs={{0,16},{1,17},{2,18},{3,19},{4,20},{5,21},{6,22},{7,23},{8,0},{9,1... | collective-permute-start | bytes 835592 | tf_op jit(solution)/shard_map/ppermute | solution.py:302
  79.0 1.6 %collective-permute-start.22 = (bf16[64,2176]{1,0:T(8,128)(2,1)S(1)}, bf16[64,2176]{1,0:T(8,128)(2,1)S(1)}, u32[]{:S(2)}, u32[]{:S(2)}) collective-permute-start(bf16[64,2176]{1,0:T(8,128)(2,1)S(1)} %slice.99), channel_id=1, source_target_pairs={{0,4},{1,5},{2,6},{3,7},{4,0},{5,1},{6,2},{7,3},{8,12},{9,13},{10,... | collective-permute-start | bytes 835592 | tf_op jit(solution)/shard_map/ppermute | solution.py:302
  80.5 5.7 %weight_grads.3 = bf16[384,2048]{1,0:T(8,128)(2,1)} custom-call(bf16[128,4224]{1,0:T(8,128)(2,1)} %copy-done.4, bf16[128,4224]{1,0:T(8,128)(2,1)} %copy-done.3, bf16[256,384]{1,0:T(8,128)(2,1)} %copy-done.12, bf16[128,4224]{1,0:T(8,128)(2,1)} %copy-done, bf16[128,4224]{1,0:T(8,128)(2,1)} %copy-done.5, bf16[256,384]{1,0:T(8,128)(2,1)} %copy-done.13, ...), custom_call_target="tpu_custom_call" | custom-call | flops 1610612736 | bytes 5767168 | tf_op jit(solution)/shard_map/weight_grads/pallas_call | solution.py:206
  87.2 5.7 %weight_grads.4 = bf16[384,2048]{1,0:T(8,128)(2,1)} custom-call(bf16[128,4224]{1,0:T(8,128)(2,1)} %copy-done.4, bf16[128,4224]{1,0:T(8,128)(2,1)} %copy-done.3, bf16[256,768]{1,0:T(8,128)(2,1)} %copy-done.8, bf16[128,4224]{1,0:T(8,128)(2,1)} %copy-done, bf16[128,4224]{1,0:T(8,128)(2,1)} %copy-done.5, bf16[256,768]{1,0:T(8,128)(2,1)} %copy-done.9, ...), custom_call_target="tpu_custom_call" | custom-call | flops 1610612736 | bytes 5767168 | tf_op jit(solution)/shard_map/weight_grads/pallas_call | solution.py:206
  93.3 1.6 %collective-permute-start.27 = (bf16[64,2176]{1,0:T(8,128)(2,1)S(1)}, bf16[64,2176]{1,0:T(8,128)(2,1)S(1)}, u32[]{:S(2)}, u32[]{:S(2)}) collective-permute-start(bf16[64,2176]{1,0:T(8,128)(2,1)S(1)} %fusion.5), channel_id=1, source_target_pairs={{0,2},{1,3},{2,0},{3,1},{4,6},{5,7},{6,4},{7,5},{8,10},{9,11},{10,... | collective-permute-start | bytes 835592 | tf_op jit(solution)/shard_map/ppermute | solution.py:302
  94.9 5.7 %weight_grads.5 = bf16[384,2048]{1,0:T(8,128)(2,1)} custom-call(bf16[128,4224]{1,0:T(8,128)(2,1)} %copy-done.4, bf16[128,4224]{1,0:T(8,128)(2,1)} %copy-done.3, bf16[256,768]{1,0:T(8,128)(2,1)} %copy-done.8, bf16[128,4224]{1,0:T(8,128)(2,1)} %copy-done, bf16[128,4224]{1,0:T(8,128)(2,1)} %copy-done.5, bf16[256,768]{1,0:T(8,128)(2,1)} %copy-done.9, ...), custom_call_target="tpu_custom_call" | custom-call | flops 1610612736 | bytes 5767168 | tf_op jit(solution)/shard_map/weight_grads/pallas_call | solution.py:206
  (123 shorter events, 25.8 us)
Async XLA Ops:
  4.4 10.1 %collective-permute-start.2 = (bf16[32,4224]{1,0:T(8,128)(2,1)}, bf16[32,4224]{1,0:T(8,128)(2,1)S(1)}, u32[]{:S(2)}, u32[]{:S(2)}) collective-permute-start(bf16[32,4224]{1,0:T(8,128)(2,1)} %get-tuple-element.63), channel_id=1, source_target_pairs={{0,16},{1,17},{2,18},{3,19},{4,20},{5,21},{6,22},{7,23},{8,0},{9,1... | collective-permute-start | bytes 811016 | tf_op jit(solution)/shard_map/ppermute | solution.py:302
  8.5 12.3 %collective-permute-start = (bf16[32,4224]{1,0:T(8,128)(2,1)}, bf16[32,4224]{1,0:T(8,128)(2,1)S(1)}, u32[]{:S(2)}, u32[]{:S(2)}) collective-permute-start(bf16[32,4224]{1,0:T(8,128)(2,1)} %get-tuple-element.63), channel_id=1, source_target_pairs={{0,4},{1,5},{2,6},{3,7},{4,0},{5,1},{6,2},{7,3},{8,12},{9,13},{10,... | collective-permute-start | bytes 811016 | tf_op jit(solution)/shard_map/ppermute | solution.py:302
  10.0 13.9 %collective-permute-start.1 = (bf16[32,4224]{1,0:T(8,128)(2,1)}, bf16[32,4224]{1,0:T(8,128)(2,1)S(1)}, u32[]{:S(2)}, u32[]{:S(2)}) collective-permute-start(bf16[32,4224]{1,0:T(8,128)(2,1)} %get-tuple-element.64), channel_id=1, source_target_pairs={{0,4},{1,5},{2,6},{3,7},{4,0},{5,1},{6,2},{7,3},{8,12},{9,13},{10,... | collective-permute-start | bytes 811016 | tf_op jit(solution)/shard_map/ppermute | solution.py:302
  14.5 9.4 %collective-permute-start.3 = (bf16[32,4224]{1,0:T(8,128)(2,1)S(1)}, bf16[32,4224]{1,0:T(8,128)(2,1)S(1)}, u32[]{:S(2)}, u32[]{:S(2)}) collective-permute-start(bf16[32,4224]{1,0:T(8,128)(2,1)S(1)} %collective-permute-done.2), channel_id=1, source_target_pairs={{0,16},{1,17},{2,18},{3,19},{4,20},{5,21},{6,22},{7,23},{8,0},{9,1... | collective-permute-start | bytes 811016 | tf_op jit(solution)/shard_map/ppermute | solution.py:302
  17.8 10.4 %collective-permute-start.5 = (bf16[32,4224]{1,0:T(8,128)(2,1)S(1)}, bf16[32,4224]{1,0:T(8,128)(2,1)S(1)}, u32[]{:S(2)}, u32[]{:S(2)}) collective-permute-start(bf16[32,4224]{1,0:T(8,128)(2,1)S(1)} %collective-permute-done.2), channel_id=1, source_target_pairs={{0,4},{1,5},{2,6},{3,7},{4,0},{5,1},{6,2},{7,3},{8,12},{9,13},{10,... | collective-permute-start | bytes 811016 | tf_op jit(solution)/shard_map/ppermute | solution.py:302
  19.3 8.9 %collective-permute-start.6 = (bf16[32,4224]{1,0:T(8,128)(2,1)S(1)}, bf16[32,4224]{1,0:T(8,128)(2,1)S(1)}, u32[]{:S(2)}, u32[]{:S(2)}) collective-permute-start(bf16[32,4224]{1,0:T(8,128)(2,1)S(1)} %collective-permute-done.2), channel_id=1, source_target_pairs={{0,2},{1,3},{2,0},{3,1},{4,6},{5,7},{6,4},{7,5},{8,10},{9,11},{10,... | collective-permute-start | bytes 811016 | tf_op jit(solution)/shard_map/ppermute | solution.py:302
  23.9 13.7 %collective-permute-start.4 = (bf16[64,4224]{1,0:T(8,128)(2,1)S(1)}, bf16[64,4224]{1,0:T(8,128)(2,1)S(1)}, u32[]{:S(2)}, u32[]{:S(2)}) collective-permute-start(bf16[64,4224]{1,0:T(8,128)(2,1)S(1)} %pad_maximum_fusion.5), channel_id=1, source_target_pairs={{0,1},{1,0},{2,3},{3,2},{4,5},{5,4},{6,7},{7,6},{8,9},{9,8},{10,11... | collective-permute-start | bytes 1622024 | tf_op jit(solution)/shard_map/ppermute | solution.py:302
  28.2 7.9 %collective-permute-start.10 = (bf16[32,4224]{1,0:T(8,128)(2,1)S(1)}, bf16[32,4224]{1,0:T(8,128)(2,1)S(1)}, u32[]{:S(2)}, u32[]{:S(2)}) collective-permute-start(bf16[32,4224]{1,0:T(8,128)(2,1)S(1)} %copy-done.19), channel_id=1, source_target_pairs={{0,8},{1,9},{2,10},{3,11},{4,12},{5,13},{6,14},{7,15},{8,24},{9,25... | collective-permute-start | bytes 811016 | tf_op jit(solution)/shard_map/ppermute | solution.py:302
  28.3 12.9 %collective-permute-start.8 = (bf16[64,4224]{1,0:T(8,128)(2,1)S(1)}, bf16[64,4224]{1,0:T(8,128)(2,1)S(1)}, u32[]{:S(2)}, u32[]{:S(2)}) collective-permute-start(bf16[64,4224]{1,0:T(8,128)(2,1)S(1)} %pad_maximum_fusion.6), channel_id=1, source_target_pairs={{0,2},{1,3},{2,0},{3,1},{4,6},{5,7},{6,4},{7,5},{8,10},{9,11},{10,... | collective-permute-start | bytes 1622024 | tf_op jit(solution)/shard_map/ppermute | solution.py:302
  29.9 10.8 %collective-permute-start.9 = (bf16[32,4224]{1,0:T(8,128)(2,1)S(1)}, bf16[32,4224]{1,0:T(8,128)(2,1)S(1)}, u32[]{:S(2)}, u32[]{:S(2)}) collective-permute-start(bf16[32,4224]{1,0:T(8,128)(2,1)S(1)} %collective-permute-done.3), channel_id=1, source_target_pairs={{0,4},{1,5},{2,6},{3,7},{4,0},{5,1},{6,2},{7,3},{8,12},{9,13},{10,... | collective-permute-start | bytes 811016 | tf_op jit(solution)/shard_map/ppermute | solution.py:302
  36.1 7.4 %collective-permute-start.12 = (bf16[32,4224]{1,0:T(8,128)(2,1)S(1)}, bf16[32,4224]{1,0:T(8,128)(2,1)S(1)}, u32[]{:S(2)}, u32[]{:S(2)}) collective-permute-start(bf16[32,4224]{1,0:T(8,128)(2,1)S(1)} %copy-done.17), channel_id=1, source_target_pairs={{0,8},{1,9},{2,10},{3,11},{4,12},{5,13},{6,14},{7,15},{8,24},{9,25... | collective-permute-start | bytes 811016 | tf_op jit(solution)/shard_map/ppermute | solution.py:302
  36.1 7.4 %collective-permute-start.11 = (bf16[32,4224]{1,0:T(8,128)(2,1)S(1)}, bf16[32,4224]{1,0:T(8,128)(2,1)S(1)}, u32[]{:S(2)}, u32[]{:S(2)}) collective-permute-start(bf16[32,4224]{1,0:T(8,128)(2,1)S(1)} %collective-permute-done.10), channel_id=1, source_target_pairs={{0,4},{1,5},{2,6},{3,7},{4,0},{5,1},{6,2},{7,3},{8,12},{9,13},{10,... | collective-permute-start | bytes 811016 | tf_op jit(solution)/shard_map/ppermute | solution.py:302
  43.7 5.3 %collective-permute-start.13 = (bf16[128,4224]{1,0:T(8,128)(2,1)S(1)}, bf16[128,4224]{1,0:T(8,128)(2,1)S(1)}, u32[]{:S(2)}, u32[]{:S(2)}) collective-permute-start(bf16[128,4224]{1,0:T(8,128)(2,1)S(1)} %pad_maximum_fusion.1.mine.refs_3_), channel_id=1, source_target_pairs={{0,1},{1,0},{2,3},{3,2},{4,5},{5,4},{6,7},{7,6},{8,9},{9,8},{10,11... | collective-permute-start | bytes 3244040 | tf_op jit(solution)/shard_map/ppermute | solution.py:302
  44.3 14.3 %collective-permute-start.14 = (bf16[64,4224]{1,0:T(8,128)(2,1)S(1)}, bf16[64,4224]{1,0:T(8,128)(2,1)S(1)}, u32[]{:S(2)}, u32[]{:S(2)}) collective-permute-start(bf16[64,4224]{1,0:T(8,128)(2,1)S(1)} %pad_maximum_fusion.7), channel_id=1, source_target_pairs={{0,2},{1,3},{2,0},{3,1},{4,6},{5,7},{6,4},{7,5},{8,10},{9,11},{10,... | collective-permute-start | bytes 1622024 | tf_op jit(solution)/shard_map/ppermute | solution.py:302
  47.4 11.2 %collective-permute-start.15 = (bf16[64,2176]{1,0:T(8,128)(2,1)S(1)}, bf16[64,2176]{1,0:T(8,128)(2,1)S(1)}, u32[]{:S(2)}, u32[]{:S(2)}) collective-permute-start(bf16[64,2176]{1,0:T(8,128)(2,1)S(1)} %slice.101), channel_id=1, source_target_pairs={{0,4},{1,5},{2,6},{3,7},{4,0},{5,1},{6,2},{7,3},{8,12},{9,13},{10,... | collective-permute-start | bytes 835592 | tf_op jit(solution)/shard_map/ppermute | solution.py:302
  51.9 6.9 %collective-permute-start.17 = (bf16[128,2176]{1,0:T(8,128)(2,1)S(1)}, bf16[128,2176]{1,0:T(8,128)(2,1)S(1)}, u32[]{:S(2)}, u32[]{:S(2)}) collective-permute-start(bf16[128,2176]{1,0:T(8,128)(2,1)S(1)} %get-tuple-element.72), channel_id=1, source_target_pairs={{0,1},{1,0},{2,3},{3,2},{4,5},{5,4},{6,7},{7,6},{8,9},{9,8},{10,11... | collective-permute-start | bytes 1671176 | tf_op jit(solution)/shard_map/ppermute | solution.py:302
  59.0 9.1 %collective-permute-start.24 = (bf16[64,2176]{1,0:T(8,128)(2,1)S(1)}, bf16[64,2176]{1,0:T(8,128)(2,1)S(1)}, u32[]{:S(2)}, u32[]{:S(2)}) collective-permute-start(bf16[64,2176]{1,0:T(8,128)(2,1)S(1)} %slice.98), channel_id=1, source_target_pairs={{0,4},{1,5},{2,6},{3,7},{4,0},{5,1},{6,2},{7,3},{8,12},{9,13},{10,... | collective-permute-start | bytes 835592 | tf_op jit(solution)/shard_map/ppermute | solution.py:302
  64.8 6.4 %collective-permute-start.18 = (bf16[128,4224]{1,0:T(8,128)(2,1)S(1)}, bf16[128,4224]{1,0:T(8,128)(2,1)S(1)}, u32[]{:S(2)}, u32[]{:S(2)}) collective-permute-start(bf16[128,4224]{1,0:T(8,128)(2,1)S(1)} %pad_maximum_fusion.3.mine.refs_9_), channel_id=1, source_target_pairs={{0,1},{1,0},{2,3},{3,2},{4,5},{5,4},{6,7},{7,6},{8,9},{9,8},{10,11... | collective-permute-start | bytes 3244040 | tf_op jit(solution)/shard_map/ppermute | solution.py:302
  68.3 8.3 %collective-permute-start.20 = (bf16[64,2176]{1,0:T(8,128)(2,1)S(1)}, bf16[64,2176]{1,0:T(8,128)(2,1)S(1)}, u32[]{:S(2)}, u32[]{:S(2)}) collective-permute-start(bf16[64,2176]{1,0:T(8,128)(2,1)S(1)} %slice.100), channel_id=1, source_target_pairs={{0,4},{1,5},{2,6},{3,7},{4,0},{5,1},{6,2},{7,3},{8,12},{9,13},{10,... | collective-permute-start | bytes 835592 | tf_op jit(solution)/shard_map/ppermute | solution.py:302
  70.0 16.3 %collective-permute-start.25 = (bf16[64,2176]{1,0:T(8,128)(2,1)S(1)}, bf16[64,2176]{1,0:T(8,128)(2,1)S(1)}, u32[]{:S(2)}, u32[]{:S(2)}) collective-permute-start(bf16[64,2176]{1,0:T(8,128)(2,1)S(1)} %fusion.2), channel_id=1, source_target_pairs={{0,8},{1,9},{2,10},{3,11},{4,12},{5,13},{6,14},{7,15},{8,24},{9,25... | collective-permute-start | bytes 835592 | tf_op jit(solution)/shard_map/ppermute | solution.py:302
  76.7 9.5 %collective-permute-start.23 = (bf16[64,2176]{1,0:T(8,128)(2,1)S(1)}, bf16[64,2176]{1,0:T(8,128)(2,1)S(1)}, u32[]{:S(2)}, u32[]{:S(2)}) collective-permute-start(bf16[64,2176]{1,0:T(8,128)(2,1)S(1)} %slice_add_fusion.2), channel_id=1, source_target_pairs={{0,16},{1,17},{2,18},{3,19},{4,20},{5,21},{6,22},{7,23},{8,0},{9,1... | collective-permute-start | bytes 835592 | tf_op jit(solution)/shard_map/ppermute | solution.py:302
  79.0 7.3 %collective-permute-start.22 = (bf16[64,2176]{1,0:T(8,128)(2,1)S(1)}, bf16[64,2176]{1,0:T(8,128)(2,1)S(1)}, u32[]{:S(2)}, u32[]{:S(2)}) collective-permute-start(bf16[64,2176]{1,0:T(8,128)(2,1)S(1)} %slice.99), channel_id=1, source_target_pairs={{0,4},{1,5},{2,6},{3,7},{4,0},{5,1},{6,2},{7,3},{8,12},{9,13},{10,... | collective-permute-start | bytes 835592 | tf_op jit(solution)/shard_map/ppermute | solution.py:302
  86.3 6.9 %collective-permute-start.26 = (bf16[64,2176]{1,0:T(8,128)(2,1)S(1)}, bf16[64,2176]{1,0:T(8,128)(2,1)S(1)}, u32[]{:S(2)}, u32[]{:S(2)}) collective-permute-start(bf16[64,2176]{1,0:T(8,128)(2,1)S(1)} %fusion.1), channel_id=1, source_target_pairs={{0,16},{1,17},{2,18},{3,19},{4,20},{5,21},{6,22},{7,23},{8,0},{9,1... | collective-permute-start | bytes 835592 | tf_op jit(solution)/shard_map/ppermute | solution.py:302
  93.3 7.2 %collective-permute-start.27 = (bf16[64,2176]{1,0:T(8,128)(2,1)S(1)}, bf16[64,2176]{1,0:T(8,128)(2,1)S(1)}, u32[]{:S(2)}, u32[]{:S(2)}) collective-permute-start(bf16[64,2176]{1,0:T(8,128)(2,1)S(1)} %fusion.5), channel_id=1, source_target_pairs={{0,2},{1,3},{2,0},{3,1},{4,6},{5,7},{6,4},{7,5},{8,10},{9,11},{10,... | collective-permute-start | bytes 835592 | tf_op jit(solution)/shard_map/ppermute | solution.py:302
  (26 other events, 134.4 us)

commit v4 on v3

--- a/solution.py
+++ b/solution.py
@@ -219,22 +219,28 @@
     )(*operands)
 
 
-def pack_kernel(
-    step, quarters, routes, probs, tokens, grad_out, *refs
-):
-    outs, (dense, sem) = refs[:4], refs[4:]
+def quarter_of(etp, i):
+    side, core = etp // 2, etp % 2
+    x = 1 - side if i % 2 else side
+    c = 1 - core if i // 2 else core
+    return 2 * x + c
+
+
+def pack_kernel(step, first, etp, routes, probs, tokens, grad_out, *refs):
+    outs, (dense, sem) = refs[:-2], refs[-2:]
     width = tokens.shape[1]
+    places = [
+        pl.ds(pl.multiple_of(quarter_of(etp[0], first + i) * step, step), step)
+        for i in range(len(outs))
+    ]
     copies = []
-    for i, out in enumerate(outs):
-        place = pl.ds(pl.multiple_of(quarters[i] * step, step), step)
-        copies.append(
-            pltpu.make_async_copy(tokens.at[place, :], out.at[:, pl.ds(0, width)], sem.at[2 * i])
-        )
-        copies.append(
-            pltpu.make_async_copy(
-                grad_out.at[place, :], out.at[:, pl.ds(width, width)], sem.at[2 * i + 1]
+    for i, (out, place) in enumerate(zip(outs, places)):
+        for j, rows in enumerate((tokens, grad_out)):
+            copies.append(
+                pltpu.make_async_copy(
+                    rows.at[place, :], out.at[:, pl.ds(j * width, width)], sem.at[2 * i + j]
+                )
             )
-        )
     for copy in copies:
         copy.start()
     named = routes[...]
@@ -245,26 +251,61 @@
     for k in range(named.shape[0]):
         spread = spread + jnp.where(ids == named[k : k + 1, :], given[k : k + 1, :], 0.0)
     dense[...] = spread.T
+    for out, place in zip(outs, places):
+        out[:, 2 * width :] = dense[place, :].astype(BF16)
     for copy in copies:
         copy.wait()
-    for i, out in enumerate(outs):
-        place = pl.ds(pl.multiple_of(quarters[i] * step, step), step)
-        out[:, 2 * width :] = dense[place, :].astype(BF16)
-
-
-def pack(quarters, routes, probs, tokens, grad_out, lanes):
+
+
+def pack(first, count, etp, routes, probs, tokens, grad_out, lanes):
     rows, width = tokens.shape
     step = rows // 4
     return pl.pallas_call(
-        functools.partial(pack_kernel, step),
-        out_shape=(jax.ShapeDtypeStruct((step, 2 * width + lanes), BF16),) * 4,
+        functools.partial(pack_kernel, step, first),
+        out_shape=(jax.ShapeDtypeStruct((step, 2 * width + lanes), BF16),) * count,
         in_specs=[pl.BlockSpec(memory_space=pltpu.SMEM)]
         + [pl.BlockSpec(memory_space=pltpu.VMEM)] * 2
         + [pl.BlockSpec(memory_space=pltpu.HBM)] * 2,
-        out_specs=(pl.BlockSpec(memory_space=pltpu.VMEM),) * 4,
-        scratch_shapes=[pltpu.VMEM((rows, lanes), F32), pltpu.SemaphoreType.DMA((8,))],
+        out_specs=(pl.BlockSpec(memory_space=pltpu.VMEM),) * count,
+        scratch_shapes=[
+            pltpu.VMEM((rows, lanes), F32),
+            pltpu.SemaphoreType.DMA((2 * count,)),
+        ],
         name="pack",
-    )(quarters, routes.T, probs.T, tokens, grad_out)
+    )(etp, routes.T, probs.T, tokens, grad_out)
+
+
+def unpack_kernel(etp, routes, near, far, rows, weights, found):
+    width = rows.shape[1]
+    step = near.shape[0] // 2
+    for i in range(4):
+        place = pl.ds(pl.multiple_of(quarter_of(etp[0], i) * step, step), step)
+        part = (near, far)[i // 2][(i % 2) * step : (i % 2 + 1) * step, :]
+        rows[place, :] = part[:, :width]
+        found[place, :] = part[:, width:].astype(F32)
+    flipped = found[...].T
+    named = routes[...]
+    ids = lax.broadcasted_iota(jnp.int32, flipped.shape, 0)
+    for k in range(named.shape[0]):
+        own = jnp.where(ids == named[k : k + 1, :], flipped, 0.0)
+        weights[k : k + 1, :] = jnp.sum(own, axis=0, keepdims=True).astype(BF16)
+
+
+def unpack(etp, routes, near, far, width):
+    rows, top_count = routes.shape
+    out, picked = pl.pallas_call(
+        unpack_kernel,
+        out_shape=(
+            jax.ShapeDtypeStruct((rows, width), BF16),
+            jax.ShapeDtypeStruct((top_count, rows), BF16),
+        ),
+        in_specs=[pl.BlockSpec(memory_space=pltpu.SMEM)]
+        + [pl.BlockSpec(memory_space=pltpu.VMEM)] * 3,
+        out_specs=(pl.BlockSpec(memory_space=pltpu.VMEM),) * 2,
+        scratch_shapes=[pltpu.VMEM((rows, near.shape[1] - width), F32)],
+        name="unpack",
+    )(etp, routes.T, near, far)
+    return out, picked.T
 
 
 def after(value, *others):
@@ -280,7 +321,6 @@
     tok_rows, top_count = routes.shape
     step = tok_rows // 4
     expert, etp = lax.axis_index("expert"), lax.axis_index("etp")
-    side, core = etp // 2, etp % 2
 
     order = (0, 2, 3, 1)
     places = [
@@ -302,12 +342,9 @@
         return lax.ppermute(value, axes, pairs)
 
     extra = -(-expert_count // LANES) * LANES
-    ids = jnp.arange(extra, dtype=jnp.int32)
-
-    quarters = jnp.stack(
-        [2 * x + c for x, c in ((side, core), (1 - side, core), (side, 1 - core), (1 - side, 1 - core))]
-    ).astype(jnp.int32)
-    here, near, *rest = pack(quarters, routes, probs, tokens, grad_out, extra)
+    place = etp.astype(jnp.int32).reshape(1)
+    (here,) = pack(0, 1, place, routes, probs, tokens, grad_out, extra)
+    near, *rest = pack(1, 3, place, routes, probs, tokens, grad_out, extra)
     gate_up = jnp.concatenate([w_gate.reshape(units, width), w_up.reshape(units, width)], axis=0)
     down = w_down.reshape(units, width)
     base = (expert * local_experts).astype(jnp.int32).reshape(1)
@@ -319,7 +356,8 @@
     line_x = {0: near, 1: move(line[1], over_x), 3: move(after(near, line[3]), along(-1))}
     other_x = {0: move(near, over_y)}
     ready, line_x[1], gate_up = lax.optimization_barrier((other[1], line_x[1], gate_up))
-    first = move(jnp.concatenate([ready, line[2]], axis=0), over_x)
+    other_x[1] = move(ready, over_x)
+    pair = move(jnp.concatenate([line[2], after(other[2], line[3])], axis=0), over_x)
     rows, grads, chips, fars, backs = {}, {}, {}, {}, {}
     sequence = list(range(lines))
     for s in sequence:
@@ -331,21 +369,23 @@
         else:
             theirs = move(mine, over_c)
         wait = [chips[s - 1]] if s > 1 else []
+        if s == 3:
+            wait += [fars[1]]
         keep, send, d_both, hid = stage(after(base, *wait), mine, theirs, gate_up, down, local_experts)
         rows[s], grads[s] = (mine, theirs), (d_both, hid)
         chips[s] = keep.astype(F32) + move(send, over_c).astype(F32)
-        fars[s] = move(chips[s][2 * step :].astype(BF16), over_y)
+        if s:
+            fars[s] = move(chips[s][2 * step :].astype(BF16), over_y)
         if s == 0:
-            _, pair, other[2], other[3], line_x[3] = lax.optimization_barrier(
-                (hid, first, other[2], other[3], line_x[3])
+            _, other_x[1], other[3], line_x[3] = lax.optimization_barrier(
+                (hid, other_x[1], other[3], line_x[3])
             )
-            other_x[1], line_x[2] = pair[:step], pair[step:]
-            second = move(jnp.concatenate([other[2], other[3]], axis=0), over_x)
+            other_x[3] = move(other[3], over_x)
         elif s == 1:
-            _, pair, fars[0] = lax.optimization_barrier((hid, second, fars[0]))
-            other_x[2], other_x[3] = pair[:step], pair[step:]
+            _, pair = lax.optimization_barrier((hid, pair))
+            line_x[2], other_x[2] = pair[:step], pair[step:]
         elif s == 2:
-            _, fars[1] = lax.optimization_barrier((hid, fars[1]))
+            _, other_x[3] = lax.optimization_barrier((hid, other_x[3]))
             backs[1] = move((chips[1][: 2 * step] + fars[1].astype(F32)).astype(BF16), along(-1))
         elif s == 3:
             _, fars[2] = lax.optimization_barrier((hid, fars[2]))
@@ -360,9 +400,10 @@
     )
     held = chips[3][: 2 * step] + fars[3].astype(F32) + passed.astype(F32)
     backs[3] = move(held.astype(BF16), along(1))
+    fars[0] = move(after(chips[0][2 * step :].astype(BF16), held), over_y)
     boths[-1] = boths[-1][:2] + (after(boths[-1][2], grad_down, held),)
     grad_gate = weight_grads(boths, 0, width, units)
-    grad_gate, backs[3] = lax.optimization_barrier((grad_gate, backs[3]))
+    grad_gate, backs[3], fars[0] = lax.optimization_barrier((grad_gate, backs[3], fars[0]))
     total = chips[0][: 2 * step] + fars[0].astype(F32)
     for back in backs.values():
         total = total + back.astype(F32)
@@ -376,14 +417,7 @@
     ).astype(BF16)
     beside = move(final, over_c)
 
-    pair = jnp.stack([final, beside]).reshape(2, 2, step, -1)
-    pair = jnp.where(core == 0, pair, pair[::-1])
-    pair = jnp.where(side == 0, pair, pair[:, ::-1])
-    whole = jnp.transpose(pair, (1, 0, 2, 3)).reshape(tok_rows, -1)
-    grad_tokens = whole[:, :width]
-    found = whole[:, None, width:]
-    named = routes[:, :, None] == ids
-    grad_probs = jnp.sum(jnp.where(named, found, 0).astype(F32), axis=2).astype(BF16)
+    grad_tokens, grad_probs = unpack(place, routes, final, beside, width)
     shape = w_gate.shape
     return (
         grad_tokens,

time: 105 us -> 97.1 us (0.925)
  waiting for transfers between devices: 30.8 us -> 21.2 us
  Pallas kernels: 31.8 us -> 35.9 us
  other arithmetic: 4.74 us -> 2.77 us
    ppermute x29 -> x30, waiting for transfers between devices: 30.8 us -> 21.2 us  [move(): return lax.ppermute(value, axes, pairs)]
    pallas_call x1 -> x3, Pallas kernels: 3.04 us -> 7.16 us  [the longest x2 5.24 us: pack(): pl.pallas_call(functools.partial(pack_kernel, step, first), out_shape=(ja...]
    unnamed x48 -> x52, local copies, waits for them, and re-layouts: 2.48 us -> 3.35 us
    ppermute x29 -> x30, starting transfers between devices: 32.2 us -> 31.8 us  [move(): return lax.ppermute(value, axes, pairs)]
  transfers between devices with their start and end apart: 29 -> 30, of which waited for: 13 -> 15; matrix products, arithmetic and copies ran while one was open for 4% -> 5% of each run, Pallas kernels for 27% -> 33%
where the time goes in v4:
time: 97.1 us; the launch traced here: 96.5 us
  Pallas kernels  35.9 us (37%)
  starting transfers between devices  31.8 us (33%)
  waiting for transfers between devices  21.2 us (22%)
  local copies, waits for them, and re-layouts  3.64 us (4%)
  other arithmetic  2.77 us (3%)
  between operations  1.19 us (1%)
    ppermute x30, starting transfers between devices, move(): return lax.ppermute(value, axes, pairs)  31.8 us
    ppermute x30, waiting for transfers between devices, move(): return lax.ppermute(value, axes, pairs)  21.2 us
    pallas_call x3, Pallas kernels, weight_grads(): pl.pallas_call(functools.partial(weights_kernel, len(parts)), grid=(tiles...  17.1 us
    pallas_call x4, Pallas kernels, stage(): pl.pallas_call(functools.partial(stage_kernel, local_experts), out_shape=...  11.7 us
    pallas_call x2, Pallas kernels, pack(): pl.pallas_call(functools.partial(pack_kernel, step, first), out_shape=(ja...  5.24 us
    unnamed x52, local copies, waits for them, and re-layouts  3.35 us
  transfers between devices with their start and end apart: 30, of which 15 were waited for; matrix products, arithmetic and copies ran while one was open for 5% of the time, Pallas kernels for 33%

profile of v4, /device:TPU:0, one launch (start us, length us, event | category | flops | bytes accessed | tf_op | source)
XLA Modules:
  0.0 96.5 jit_solution(7483381883955155554)
XLA Ops:
  0.6 2.4 %pack.2 = bf16[32,4224]{1,0:T(8,128)(2,1)} custom-call(s32[1]{0:T(128)} %bitcast.etp, s32[8,128]{1,0:T(8,128)} %bitcast.20, bf16[8,128]{1,0:T(8,128)(2,1)} %bitcast.23, bf16[128,2048]{1,0:T(8,128)(2,1)} %tokens.3, bf16[128,2048]{1,0:T(8,128)(2,1)} %grad_out.3), custom_call_target="tpu_custom_call" | custom-call | tf_op jit(solution)/shard_map/pack/pallas_call | solution.py:263
  3.1 4.1 %collective-permute-start.2 = (bf16[32,4224]{1,0:T(8,128)(2,1)}, bf16[32,4224]{1,0:T(8,128)(2,1)S(1)}, u32[]{:S(2)}, u32[]{:S(2)}) collective-permute-start(bf16[32,4224]{1,0:T(8,128)(2,1)} %pack.2), channel_id=1, source_target_pairs={{0,16},{1,17},{2,18},{3,19},{4,20},{5,21},{6,22},{7,23},{8,0},{9,1... | collective-permute-start | bytes 811016 | tf_op jit(solution)/shard_map/ppermute | solution.py:342
  7.1 1.5 %collective-permute-start = (bf16[32,4224]{1,0:T(8,128)(2,1)}, bf16[32,4224]{1,0:T(8,128)(2,1)S(1)}, u32[]{:S(2)}, u32[]{:S(2)}) collective-permute-start(bf16[32,4224]{1,0:T(8,128)(2,1)} %pack.2), channel_id=1, source_target_pairs={{0,4},{1,5},{2,6},{3,7},{4,0},{5,1},{6,2},{7,3},{8,12},{9,13},{10,... | collective-permute-start | bytes 811016 | tf_op jit(solution)/shard_map/ppermute | solution.py:342
  8.7 2.8 %pack.3 = (bf16[32,4224]{1,0:T(8,128)(2,1)}, bf16[32,4224]{1,0:T(8,128)(2,1)}, bf16[32,4224]{1,0:T(8,128)(2,1)}) custom-call(s32[1]{0:T(128)} %bitcast.etp, s32[8,128]{1,0:T(8,128)} %bitcast.21, bf16[8,128]{1,0:T(8,128)(2,1)} %bitcast.24, bf16[128,2048]{1,0:T(8,128)(2,1)} %tokens.3, bf16[128,2048]{1,0:T(8,128)(2,1)} %grad_out.3), custom_call_target="tpu_custom_call" | custom-call | tf_op jit(solution)/shard_map/pack/pallas_call | solution.py:263
  14.1 1.6 %pad_maximum_fusion.gate_up = bf16[768,2048]{1,0:T(8,128)(2,1)S(1)} fusion(bf16[384,2048]{1,0:T(8,128)(2,1)S(1)} %bitcast.15, bf16[384,2048]{1,0:T(8,128)(2,1)} %bitcast.16), kind=kLoop, calls=%fused_computation | loop fusion | flops 6291456 | bytes 6291456 | tf_op jit(solution)/shard_map/concatenate | solution.py:348
  15.7 1.6 %collective-permute-start.3 = (bf16[32,4224]{1,0:T(8,128)(2,1)S(1)}, bf16[32,4224]{1,0:T(8,128)(2,1)S(1)}, u32[]{:S(2)}, u32[]{:S(2)}) collective-permute-start(bf16[32,4224]{1,0:T(8,128)(2,1)S(1)} %collective-permute-done.2), channel_id=1, source_target_pairs={{0,16},{1,17},{2,18},{3,19},{4,20},{5,21},{6,22},{7,23},{8,0},{9,1... | collective-permute-start | bytes 811016 | tf_op jit(solution)/shard_map/ppermute | solution.py:342
  17.4 1.5 %collective-permute-start.5 = (bf16[32,4224]{1,0:T(8,128)(2,1)S(1)}, bf16[32,4224]{1,0:T(8,128)(2,1)S(1)}, u32[]{:S(2)}, u32[]{:S(2)}) collective-permute-start(bf16[32,4224]{1,0:T(8,128)(2,1)S(1)} %collective-permute-done.2), channel_id=1, source_target_pairs={{0,4},{1,5},{2,6},{3,7},{4,0},{5,1},{6,2},{7,3},{8,12},{9,13},{10,... | collective-permute-start | bytes 811016 | tf_op jit(solution)/shard_map/ppermute | solution.py:342
  20.4 2.1 %collective-permute-done.1 = bf16[32,4224]{1,0:T(8,128)(2,1)S(1)} collective-permute-done((bf16[32,4224]{1,0:T(8,128)(2,1)}, bf16[32,4224]{1,0:T(8,128)(2,1)S(1)}, u32[]{:S(2)}, u32[]{:S(2)}) %collective-permute-start.1) | collective-permute-done | bytes 270368 | tf_op jit(solution)/shard_map/ppermute | solution.py:342
  23.3 3.6 %collective-permute-done.5 = bf16[32,4224]{1,0:T(8,128)(2,1)S(1)} collective-permute-done((bf16[32,4224]{1,0:T(8,128)(2,1)S(1)}, bf16[32,4224]{1,0:T(8,128)(2,1)S(1)}, u32[]{:S(2)}, u32[]{:S(2)}) %collective-permute-start.5) | collective-permute-done | bytes 270368 | tf_op jit(solution)/shard_map/ppermute | solution.py:342
  26.9 1.6 %collective-permute-start.8 = (bf16[32,4224]{1,0:T(8,128)(2,1)S(1)}, bf16[32,4224]{1,0:T(8,128)(2,1)S(1)}, u32[]{:S(2)}, u32[]{:S(2)}) collective-permute-start(bf16[32,4224]{1,0:T(8,128)(2,1)S(1)} %collective-permute-done.5), channel_id=1, source_target_pairs={{0,2},{1,3},{2,0},{3,1},{4,6},{5,7},{6,4},{7,5},{8,10},{9,11},{10,... | collective-permute-start | bytes 811016 | tf_op jit(solution)/shard_map/ppermute | solution.py:342
  28.6 1.6 %collective-permute-start.13 = (bf16[32,4224]{1,0:T(8,128)(2,1)S(1)}, bf16[32,4224]{1,0:T(8,128)(2,1)S(1)}, u32[]{:S(2)}, u32[]{:S(2)}) collective-permute-start(bf16[32,4224]{1,0:T(8,128)(2,1)S(1)} %collective-permute-done.3), channel_id=1, source_target_pairs={{0,4},{1,5},{2,6},{3,7},{4,0},{5,1},{6,2},{7,3},{8,12},{9,13},{10,... | collective-permute-start | bytes 811016 | tf_op jit(solution)/shard_map/ppermute | solution.py:342
  30.2 4.6 %collective-permute-done.9 = bf16[32,4224]{1,0:T(8,128)(2,1)S(1)} collective-permute-done((bf16[32,4224]{1,0:T(8,128)(2,1)S(1)}, bf16[32,4224]{1,0:T(8,128)(2,1)S(1)}, u32[]{:S(2)}, u32[]{:S(2)}) %collective-permute-start.9) | collective-permute-done | bytes 270368 | tf_op jit(solution)/shard_map/ppermute | solution.py:342
  38.0 2.9 %stage.4 = (bf16[128,2176]{1,0:T(8,128)(2,1)S(1)}, bf16[128,2176]{1,0:T(8,128)(2,1)S(1)}, bf16[256,768]{1,0:T(8,128)(2,1)S(1)}, bf16[256,384]{1,0:T(8,128)(2,1)S(1)}) custom-call(s32[1]{0:T(128)} %bitcast.2.base_ref, bf16[128,4224]{1,0:T(8,128)(2,1)S(1)} %pad_maximum_fusion.1.mine.refs_0_, ...), custom_call_target="tpu_custom_call" | custom-call | flops 2013265920 | bytes 4325376 | tf_op jit(solution)/shard_map/stage/pallas_call | solution.py:166
  45.7 2.9 %stage.5 = (bf16[128,2176]{1,0:T(8,128)(2,1)S(1)}, bf16[128,2176]{1,0:T(8,128)(2,1)S(1)}, bf16[256,768]{1,0:T(8,128)(2,1)S(1)}, bf16[256,384]{1,0:T(8,128)(2,1)S(1)}) custom-call(s32[1]{0:T(128)} %bitcast.2.base_ref, bf16[128,4224]{1,0:T(8,128)(2,1)S(1)} %constant_dynamic-update-slice_fusion.3.mine.refs_3_, ...), custom_call_target="tpu_custom_call" | custom-call | flops 2013265920 | bytes 4325376 | tf_op jit(solution)/shard_map/stage/pallas_call | solution.py:166
  50.9 1.6 %collective-permute-start.20 = (bf16[64,2176]{1,0:T(8,128)(2,1)S(1)}, bf16[64,2176]{1,0:T(8,128)(2,1)S(1)}, u32[]{:S(2)}, u32[]{:S(2)}) collective-permute-start(bf16[64,2176]{1,0:T(8,128)(2,1)S(1)} %slice.83), channel_id=1, source_target_pairs={{0,4},{1,5},{2,6},{3,7},{4,0},{5,1},{6,2},{7,3},{8,12},{9,13},{10,... | collective-permute-start | bytes 835592 | tf_op jit(solution)/shard_map/ppermute | solution.py:342
  52.5 2.9 %stage.6 = (bf16[128,2176]{1,0:T(8,128)(2,1)S(1)}, bf16[128,2176]{1,0:T(8,128)(2,1)S(1)}, bf16[256,768]{1,0:T(8,128)(2,1)S(1)}, bf16[256,384]{1,0:T(8,128)(2,1)S(1)}) custom-call(s32[1]{0:T(128)} %bitcast.2.base_ref, bf16[128,4224]{1,0:T(8,128)(2,1)S(1)} %pad_maximum_fusion.2.mine.refs_6_, bf16[128,4224]{1,0:T(8,128)(2,1)S(1)} %collective-permute-done.15.theirs.refs_7_, ...), custom_call_target="tpu_custom_call" | custom-call | flops 2013265920 | bytes 4325376 | tf_op jit(solution)/shard_map/stage/pallas_call | solution.py:166
  59.7 2.2 %collective-permute-start.25 = (bf16[64,2176]{1,0:T(8,128)(2,1)S(1)}, bf16[64,2176]{1,0:T(8,128)(2,1)S(1)}, u32[]{:S(2)}, u32[]{:S(2)}) collective-permute-start(bf16[64,2176]{1,0:T(8,128)(2,1)S(1)} %fusion.1), channel_id=1, source_target_pairs={{0,8},{1,9},{2,10},{3,11},{4,12},{5,13},{6,14},{7,15},{8,24},{9,25... | collective-permute-start | bytes 835592 | tf_op jit(solution)/shard_map/ppermute | solution.py:342
  61.9 2.9 %stage.7 = (bf16[128,2176]{1,0:T(8,128)(2,1)S(1)}, bf16[128,2176]{1,0:T(8,128)(2,1)S(1)}, bf16[256,768]{1,0:T(8,128)(2,1)S(1)}, bf16[256,384]{1,0:T(8,128)(2,1)S(1)}) custom-call(s32[1]{0:T(128)} %bitcast.2.base_ref, bf16[128,4224]{1,0:T(8,128)(2,1)S(1)} %constant_dynamic-update-slice_fusion.7.mine.refs_9_, ...), custom_call_target="tpu_custom_call" | custom-call | flops 2013265920 | bytes 4325376 | tf_op jit(solution)/shard_map/stage/pallas_call | solution.py:166
  66.4 3.0 %collective-permute-start.24 = (bf16[64,2176]{1,0:T(8,128)(2,1)S(1)}, bf16[64,2176]{1,0:T(8,128)(2,1)S(1)}, u32[]{:S(2)}, u32[]{:S(2)}) collective-permute-start(bf16[64,2176]{1,0:T(8,128)(2,1)S(1)} %slice_add_fusion.2), channel_id=1, source_target_pairs={{0,16},{1,17},{2,18},{3,19},{4,20},{5,21},{6,22},{7,23},{8,0},{9,1... | collective-permute-start | bytes 835592 | tf_op jit(solution)/shard_map/ppermute | solution.py:342
  71.1 5.7 %weight_grads.3 = bf16[384,2048]{1,0:T(8,128)(2,1)} custom-call(bf16[128,4224]{1,0:T(8,128)(2,1)} %copy-done, bf16[128,4224]{1,0:T(8,128)(2,1)} %copy-done.3, bf16[256,384]{1,0:T(8,128)(2,1)} %copy-done.12, bf16[128,4224]{1,0:T(8,128)(2,1)} %copy-done.2, bf16[128,4224]{1,0:T(8,128)(2,1)} %copy-done.5, bf16[256,384]{1,0:T(8,128)(2,1)} %copy-done.13, ...), custom_call_target="tpu_custom_call" | custom-call | flops 1610612736 | bytes 5767168 | tf_op jit(solution)/shard_map/weight_grads/pallas_call | solution.py:206
  79.7 5.7 %weight_grads.4 = bf16[384,2048]{1,0:T(8,128)(2,1)} custom-call(bf16[128,4224]{1,0:T(8,128)(2,1)} %copy-done, bf16[128,4224]{1,0:T(8,128)(2,1)} %copy-done.3, bf16[256,768]{1,0:T(8,128)(2,1)} %copy-done.8, bf16[128,4224]{1,0:T(8,128)(2,1)} %copy-done.2, bf16[128,4224]{1,0:T(8,128)(2,1)} %copy-done.5, bf16[256,768]{1,0:T(8,128)(2,1)} %copy-done.9, ...), custom_call_target="tpu_custom_call" | custom-call | flops 1610612736 | bytes 5767168 | tf_op jit(solution)/shard_map/weight_grads/pallas_call | solution.py:206
  86.3 5.7 %weight_grads.5 = bf16[384,2048]{1,0:T(8,128)(2,1)} custom-call(bf16[128,4224]{1,0:T(8,128)(2,1)} %copy-done, bf16[128,4224]{1,0:T(8,128)(2,1)} %copy-done.3, bf16[256,768]{1,0:T(8,128)(2,1)} %copy-done.8, bf16[128,4224]{1,0:T(8,128)(2,1)} %copy-done.2, bf16[128,4224]{1,0:T(8,128)(2,1)} %copy-done.5, bf16[256,768]{1,0:T(8,128)(2,1)} %copy-done.9, ...), custom_call_target="tpu_custom_call" | custom-call | flops 1610612736 | bytes 5767168 | tf_op jit(solution)/shard_map/weight_grads/pallas_call | solution.py:206
  92.3 1.5 %collective-permute-done.29.far = bf16[64,2176]{1,0:T(8,128)(2,1)S(1)} collective-permute-done((bf16[64,2176]{1,0:T(8,128)(2,1)S(1)}, bf16[64,2176]{1,0:T(8,128)(2,1)S(1)}, u32[]{:S(2)}, u32[]{:S(2)}) %collective-permute-start.29) | collective-permute-done | bytes 278560 | tf_op jit(solution)/shard_map/ppermute | solution.py:342
  94.6 1.9 %unpack.1 = (bf16[128,2048]{1,0:T(8,128)(2,1)}, bf16[8,128]{1,0:T(8,128)(2,1)}) custom-call(s32[1]{0:T(128)} %bitcast.etp, s32[8,128]{1,0:T(8,128)} %bitcast.22, bf16[64,2176]{1,0:T(8,128)(2,1)} %copy-done.18, bf16[64,2176]{1,0:T(8,128)(2,1)} %copy-done.20), custom_call_target="tpu_custom_call" | custom-call | tf_op jit(solution)/shard_map/unpack/pallas_call | solution.py:296
  (121 shorter events, 27.2 us)
Async XLA Ops:
  3.1 12.7 %collective-permute-start.2 = (bf16[32,4224]{1,0:T(8,128)(2,1)}, bf16[32,4224]{1,0:T(8,128)(2,1)S(1)}, u32[]{:S(2)}, u32[]{:S(2)}) collective-permute-start(bf16[32,4224]{1,0:T(8,128)(2,1)} %pack.2), channel_id=1, source_target_pairs={{0,16},{1,17},{2,18},{3,19},{4,20},{5,21},{6,22},{7,23},{8,0},{9,1... | collective-permute-start | bytes 811016 | tf_op jit(solution)/shard_map/ppermute | solution.py:342
  7.1 16.0 %collective-permute-start = (bf16[32,4224]{1,0:T(8,128)(2,1)}, bf16[32,4224]{1,0:T(8,128)(2,1)S(1)}, u32[]{:S(2)}, u32[]{:S(2)}) collective-permute-start(bf16[32,4224]{1,0:T(8,128)(2,1)} %pack.2), channel_id=1, source_target_pairs={{0,4},{1,5},{2,6},{3,7},{4,0},{5,1},{6,2},{7,3},{8,12},{9,13},{10,... | collective-permute-start | bytes 811016 | tf_op jit(solution)/shard_map/ppermute | solution.py:342
  11.5 11.0 %collective-permute-start.1 = (bf16[32,4224]{1,0:T(8,128)(2,1)}, bf16[32,4224]{1,0:T(8,128)(2,1)S(1)}, u32[]{:S(2)}, u32[]{:S(2)}) collective-permute-start(bf16[32,4224]{1,0:T(8,128)(2,1)} %get-tuple-element.66), channel_id=1, source_target_pairs={{0,4},{1,5},{2,6},{3,7},{4,0},{5,1},{6,2},{7,3},{8,12},{9,13},{10,... | collective-permute-start | bytes 811016 | tf_op jit(solution)/shard_map/ppermute | solution.py:342
  15.7 7.4 %collective-permute-start.3 = (bf16[32,4224]{1,0:T(8,128)(2,1)S(1)}, bf16[32,4224]{1,0:T(8,128)(2,1)S(1)}, u32[]{:S(2)}, u32[]{:S(2)}) collective-permute-start(bf16[32,4224]{1,0:T(8,128)(2,1)S(1)} %collective-permute-done.2), channel_id=1, source_target_pairs={{0,16},{1,17},{2,18},{3,19},{4,20},{5,21},{6,22},{7,23},{8,0},{9,1... | collective-permute-start | bytes 811016 | tf_op jit(solution)/shard_map/ppermute | solution.py:342
  17.4 9.5 %collective-permute-start.5 = (bf16[32,4224]{1,0:T(8,128)(2,1)S(1)}, bf16[32,4224]{1,0:T(8,128)(2,1)S(1)}, u32[]{:S(2)}, u32[]{:S(2)}) collective-permute-start(bf16[32,4224]{1,0:T(8,128)(2,1)S(1)} %collective-permute-done.2), channel_id=1, source_target_pairs={{0,4},{1,5},{2,6},{3,7},{4,0},{5,1},{6,2},{7,3},{8,12},{9,13},{10,... | collective-permute-start | bytes 811016 | tf_op jit(solution)/shard_map/ppermute | solution.py:342
  18.9 8.0 %collective-permute-start.6 = (bf16[32,4224]{1,0:T(8,128)(2,1)S(1)}, bf16[32,4224]{1,0:T(8,128)(2,1)S(1)}, u32[]{:S(2)}, u32[]{:S(2)}) collective-permute-start(bf16[32,4224]{1,0:T(8,128)(2,1)S(1)} %collective-permute-done.2), channel_id=1, source_target_pairs={{0,2},{1,3},{2,0},{3,1},{4,6},{5,7},{6,4},{7,5},{8,10},{9,11},{10,... | collective-permute-start | bytes 811016 | tf_op jit(solution)/shard_map/ppermute | solution.py:342
  23.2 14.7 %collective-permute-start.4 = (bf16[64,4224]{1,0:T(8,128)(2,1)S(1)}, bf16[64,4224]{1,0:T(8,128)(2,1)S(1)}, u32[]{:S(2)}, u32[]{:S(2)}) collective-permute-start(bf16[64,4224]{1,0:T(8,128)(2,1)S(1)} %pad_maximum_fusion.3), channel_id=1, source_target_pairs={{0,1},{1,0},{2,3},{3,2},{4,5},{5,4},{6,7},{7,6},{8,9},{9,8},{10,11... | collective-permute-start | bytes 1622024 | tf_op jit(solution)/shard_map/ppermute | solution.py:342
  26.9 7.9 %collective-permute-start.9 = (bf16[32,4224]{1,0:T(8,128)(2,1)S(1)}, bf16[32,4224]{1,0:T(8,128)(2,1)S(1)}, u32[]{:S(2)}, u32[]{:S(2)}) collective-permute-start(bf16[32,4224]{1,0:T(8,128)(2,1)S(1)} %copy-done.19), channel_id=1, source_target_pairs={{0,8},{1,9},{2,10},{3,11},{4,12},{5,13},{6,14},{7,15},{8,24},{9,25... | collective-permute-start | bytes 811016 | tf_op jit(solution)/shard_map/ppermute | solution.py:342
  26.9 14.1 %collective-permute-start.8 = (bf16[32,4224]{1,0:T(8,128)(2,1)S(1)}, bf16[32,4224]{1,0:T(8,128)(2,1)S(1)}, u32[]{:S(2)}, u32[]{:S(2)}) collective-permute-start(bf16[32,4224]{1,0:T(8,128)(2,1)S(1)} %collective-permute-done.5), channel_id=1, source_target_pairs={{0,2},{1,3},{2,0},{3,1},{4,6},{5,7},{6,4},{7,5},{8,10},{9,11},{10,... | collective-permute-start | bytes 811016 | tf_op jit(solution)/shard_map/ppermute | solution.py:342
  28.6 6.8 %collective-permute-start.13 = (bf16[32,4224]{1,0:T(8,128)(2,1)S(1)}, bf16[32,4224]{1,0:T(8,128)(2,1)S(1)}, u32[]{:S(2)}, u32[]{:S(2)}) collective-permute-start(bf16[32,4224]{1,0:T(8,128)(2,1)S(1)} %collective-permute-done.3), channel_id=1, source_target_pairs={{0,4},{1,5},{2,6},{3,7},{4,0},{5,1},{6,2},{7,3},{8,12},{9,13},{10,... | collective-permute-start | bytes 811016 | tf_op jit(solution)/shard_map/ppermute | solution.py:342
  34.8 7.4 %collective-permute-start.11 = (bf16[32,4224]{1,0:T(8,128)(2,1)S(1)}, bf16[32,4224]{1,0:T(8,128)(2,1)S(1)}, u32[]{:S(2)}, u32[]{:S(2)}) collective-permute-start(bf16[32,4224]{1,0:T(8,128)(2,1)S(1)} %copy-done.21), channel_id=1, source_target_pairs={{0,8},{1,9},{2,10},{3,11},{4,12},{5,13},{6,14},{7,15},{8,24},{9,25... | collective-permute-start | bytes 811016 | tf_op jit(solution)/shard_map/ppermute | solution.py:342
  35.5 13.4 %collective-permute-start.14 = (bf16[64,4224]{1,0:T(8,128)(2,1)S(1)}, bf16[64,4224]{1,0:T(8,128)(2,1)S(1)}, u32[]{:S(2)}, u32[]{:S(2)}) collective-permute-start(bf16[64,4224]{1,0:T(8,128)(2,1)S(1)} %pad_maximum_fusion.4), channel_id=1, source_target_pairs={{0,2},{1,3},{2,0},{3,1},{4,6},{5,7},{6,4},{7,5},{8,10},{9,11},{10,... | collective-permute-start | bytes 1622024 | tf_op jit(solution)/shard_map/ppermute | solution.py:342
  36.4 6.5 %collective-permute-start.10 = (bf16[32,4224]{1,0:T(8,128)(2,1)S(1)}, bf16[32,4224]{1,0:T(8,128)(2,1)S(1)}, u32[]{:S(2)}, u32[]{:S(2)}) collective-permute-start(bf16[32,4224]{1,0:T(8,128)(2,1)S(1)} %collective-permute-done.9), channel_id=1, source_target_pairs={{0,4},{1,5},{2,6},{3,7},{4,0},{5,1},{6,2},{7,3},{8,12},{9,13},{10,... | collective-permute-start | bytes 811016 | tf_op jit(solution)/shard_map/ppermute | solution.py:342
  43.0 12.5 %collective-permute-start.17 = (bf16[32,4224]{1,0:T(8,128)(2,1)S(1)}, bf16[32,4224]{1,0:T(8,128)(2,1)S(1)}, u32[]{:S(2)}, u32[]{:S(2)}) collective-permute-start(bf16[32,4224]{1,0:T(8,128)(2,1)S(1)} %collective-permute-done.10), channel_id=1, source_target_pairs={{0,2},{1,3},{2,0},{3,1},{4,6},{5,7},{6,4},{7,5},{8,10},{9,11},{10,... | collective-permute-start | bytes 811016 | tf_op jit(solution)/shard_map/ppermute | solution.py:342
  44.2 26.8 %collective-permute-start.7 = (bf16[128,2176]{1,0:T(8,128)(2,1)S(1)}, bf16[128,2176]{1,0:T(8,128)(2,1)S(1)}, u32[]{:S(2)}, u32[]{:S(2)}) collective-permute-start(bf16[128,2176]{1,0:T(8,128)(2,1)S(1)} %get-tuple-element.60), channel_id=1, source_target_pairs={{0,1},{1,0},{2,3},{3,2},{4,5},{5,4},{6,7},{7,6},{8,9},{9,8},{10,11... | collective-permute-start | bytes 1671176 | tf_op jit(solution)/shard_map/ppermute | solution.py:342
  50.9 8.8 %collective-permute-start.20 = (bf16[64,2176]{1,0:T(8,128)(2,1)S(1)}, bf16[64,2176]{1,0:T(8,128)(2,1)S(1)}, u32[]{:S(2)}, u32[]{:S(2)}) collective-permute-start(bf16[64,2176]{1,0:T(8,128)(2,1)S(1)} %slice.83), channel_id=1, source_target_pairs={{0,4},{1,5},{2,6},{3,7},{4,0},{5,1},{6,2},{7,3},{8,12},{9,13},{10,... | collective-permute-start | bytes 835592 | tf_op jit(solution)/shard_map/ppermute | solution.py:342
  55.5 6.3 %collective-permute-start.18 = (bf16[128,4224]{1,0:T(8,128)(2,1)S(1)}, bf16[128,4224]{1,0:T(8,128)(2,1)S(1)}, u32[]{:S(2)}, u32[]{:S(2)}) collective-permute-start(bf16[128,4224]{1,0:T(8,128)(2,1)S(1)} %constant_dynamic-update-slice_fusion.7.mine.refs_9_), channel_id=1, source_target_pairs={{0,1},{1,0},{2,3},{3,2},{4,5},{5,4},{6,7},{7,6},{8,9},{9,8},{10,11... | collective-permute-start | bytes 3244040 | tf_op jit(solution)/shard_map/ppermute | solution.py:342
  57.6 8.8 %collective-permute-start.21 = (bf16[64,2176]{1,0:T(8,128)(2,1)S(1)}, bf16[64,2176]{1,0:T(8,128)(2,1)S(1)}, u32[]{:S(2)}, u32[]{:S(2)}) collective-permute-start(bf16[64,2176]{1,0:T(8,128)(2,1)S(1)} %slice.82), channel_id=1, source_target_pairs={{0,4},{1,5},{2,6},{3,7},{4,0},{5,1},{6,2},{7,3},{8,12},{9,13},{10,... | collective-permute-start | bytes 835592 | tf_op jit(solution)/shard_map/ppermute | solution.py:342
  59.7 17.1 %collective-permute-start.25 = (bf16[64,2176]{1,0:T(8,128)(2,1)S(1)}, bf16[64,2176]{1,0:T(8,128)(2,1)S(1)}, u32[]{:S(2)}, u32[]{:S(2)}) collective-permute-start(bf16[64,2176]{1,0:T(8,128)(2,1)S(1)} %fusion.1), channel_id=1, source_target_pairs={{0,8},{1,9},{2,10},{3,11},{4,12},{5,13},{6,14},{7,15},{8,24},{9,25... | collective-permute-start | bytes 835592 | tf_op jit(solution)/shard_map/ppermute | solution.py:342
  66.4 10.4 %collective-permute-start.24 = (bf16[64,2176]{1,0:T(8,128)(2,1)S(1)}, bf16[64,2176]{1,0:T(8,128)(2,1)S(1)}, u32[]{:S(2)}, u32[]{:S(2)}) collective-permute-start(bf16[64,2176]{1,0:T(8,128)(2,1)S(1)} %slice_add_fusion.2), channel_id=1, source_target_pairs={{0,16},{1,17},{2,18},{3,19},{4,20},{5,21},{6,22},{7,23},{8,0},{9,1... | collective-permute-start | bytes 835592 | tf_op jit(solution)/shard_map/ppermute | solution.py:342
  69.6 7.7 %collective-permute-start.23 = (bf16[64,2176]{1,0:T(8,128)(2,1)S(1)}, bf16[64,2176]{1,0:T(8,128)(2,1)S(1)}, u32[]{:S(2)}, u32[]{:S(2)}) collective-permute-start(bf16[64,2176]{1,0:T(8,128)(2,1)S(1)} %slice.81), channel_id=1, source_target_pairs={{0,4},{1,5},{2,6},{3,7},{4,0},{5,1},{6,2},{7,3},{8,12},{9,13},{10,... | collective-permute-start | bytes 835592 | tf_op jit(solution)/shard_map/ppermute | solution.py:342
  77.3 8.0 %collective-permute-start.27 = (bf16[64,2176]{1,0:T(8,128)(2,1)S(1)}, bf16[64,2176]{1,0:T(8,128)(2,1)S(1)}, u32[]{:S(2)}, u32[]{:S(2)}) collective-permute-start(bf16[64,2176]{1,0:T(8,128)(2,1)S(1)} %slice.80), channel_id=1, source_target_pairs={{0,4},{1,5},{2,6},{3,7},{4,0},{5,1},{6,2},{7,3},{8,12},{9,13},{10,... | collective-permute-start | bytes 835592 | tf_op jit(solution)/shard_map/ppermute | solution.py:342
  78.7 6.6 %collective-permute-start.26 = (bf16[64,2176]{1,0:T(8,128)(2,1)S(1)}, bf16[64,2176]{1,0:T(8,128)(2,1)S(1)}, u32[]{:S(2)}, u32[]{:S(2)}) collective-permute-start(bf16[64,2176]{1,0:T(8,128)(2,1)S(1)} %fusion), channel_id=1, source_target_pairs={{0,16},{1,17},{2,18},{3,19},{4,20},{5,21},{6,22},{7,23},{8,0},{9,1... | collective-permute-start | bytes 835592 | tf_op jit(solution)/shard_map/ppermute | solution.py:342
  85.5 6.6 %collective-permute-start.28 = (bf16[64,2176]{1,0:T(8,128)(2,1)S(1)}, bf16[64,2176]{1,0:T(8,128)(2,1)S(1)}, u32[]{:S(2)}, u32[]{:S(2)}) collective-permute-start(bf16[64,2176]{1,0:T(8,128)(2,1)S(1)} %fusion.4), channel_id=1, source_target_pairs={{0,2},{1,3},{2,0},{3,1},{4,6},{5,7},{6,4},{7,5},{8,10},{9,11},{10,... | collective-permute-start | bytes 835592 | tf_op jit(solution)/shard_map/ppermute | solution.py:342
  (28 other events, 119.6 us)

commit v5 on v4

--- a/solution.py
+++ b/solution.py
@@ -303,6 +303,7 @@
         + [pl.BlockSpec(memory_space=pltpu.VMEM)] * 3,
         out_specs=(pl.BlockSpec(memory_space=pltpu.VMEM),) * 2,
         scratch_shapes=[pltpu.VMEM((rows, near.shape[1] - width), F32)],
+        compiler_params=pltpu.CompilerParams(vmem_limit_bytes=VMEM_BYTES),
         name="unpack",
     )(etp, routes.T, near, far)
     return out, picked.T

time: 97.1 us -> 95.3 us (0.981)
  Pallas kernels: 35.9 us -> 34.9 us
    pallas_call x1, Pallas kernels: 1.92 us -> 0.86 us  [unpack(): pl.pallas_call(unpack_kernel, out_shape=(jax.ShapeDtypeStruct((rows, widt...]
    unnamed x52 -> x50, local copies, waits for them, and re-layouts: 3.35 us -> 2.63 us
where the time goes in v5:
time: 95.3 us; the launch traced here: 94.7 us
  Pallas kernels  34.9 us (37%)
  starting transfers between devices  31.8 us (33%)
  waiting for transfers between devices  21.2 us (22%)
  local copies, waits for them, and re-layouts  2.92 us (3%)
  other arithmetic  2.77 us (3%)
  between operations  1.18 us (1%)
    ppermute x30, starting transfers between devices, move(): return lax.ppermute(value, axes, pairs)  31.8 us
    ppermute x30, waiting for transfers between devices, move(): return lax.ppermute(value, axes, pairs)  21.2 us
    pallas_call x3, Pallas kernels, weight_grads(): pl.pallas_call(functools.partial(weights_kernel, len(parts)), grid=(tiles...  17.1 us
    pallas_call x4, Pallas kernels, stage(): pl.pallas_call(functools.partial(stage_kernel, local_experts), out_shape=...  11.7 us
    pallas_call x2, Pallas kernels, pack(): pl.pallas_call(functools.partial(pack_kernel, step, first), out_shape=(ja...  5.24 us
    unnamed x50, local copies, waits for them, and re-layouts  2.63 us
  transfers between devices with their start and end apart: 30, of which 15 were waited for; matrix products, arithmetic and copies ran while one was open for 5% of the time, Pallas kernels for 33%

profile of v5, /device:TPU:0, one launch (start us, length us, event | category | flops | bytes accessed | tf_op | source)
XLA Modules:
  0.0 94.7 jit_solution(18220560651459085800)
XLA Ops:
  0.6 2.4 %pack.2 = bf16[32,4224]{1,0:T(8,128)(2,1)} custom-call(s32[1]{0:T(128)} %bitcast.etp, s32[8,128]{1,0:T(8,128)} %bitcast.11, bf16[8,128]{1,0:T(8,128)(2,1)} %bitcast.23, bf16[128,2048]{1,0:T(8,128)(2,1)} %tokens.3, bf16[128,2048]{1,0:T(8,128)(2,1)} %grad_out.3), custom_call_target="tpu_custom_call" | custom-call | tf_op jit(solution)/shard_map/pack/pallas_call | solution.py:263
  3.1 4.1 %collective-permute-start.2 = (bf16[32,4224]{1,0:T(8,128)(2,1)}, bf16[32,4224]{1,0:T(8,128)(2,1)S(1)}, u32[]{:S(2)}, u32[]{:S(2)}) collective-permute-start(bf16[32,4224]{1,0:T(8,128)(2,1)} %pack.2), channel_id=1, source_target_pairs={{0,16},{1,17},{2,18},{3,19},{4,20},{5,21},{6,22},{7,23},{8,0},{9,1... | collective-permute-start | bytes 811016 | tf_op jit(solution)/shard_map/ppermute | solution.py:343
  7.1 1.5 %collective-permute-start = (bf16[32,4224]{1,0:T(8,128)(2,1)}, bf16[32,4224]{1,0:T(8,128)(2,1)S(1)}, u32[]{:S(2)}, u32[]{:S(2)}) collective-permute-start(bf16[32,4224]{1,0:T(8,128)(2,1)} %pack.2), channel_id=1, source_target_pairs={{0,4},{1,5},{2,6},{3,7},{4,0},{5,1},{6,2},{7,3},{8,12},{9,13},{10,... | collective-permute-start | bytes 811016 | tf_op jit(solution)/shard_map/ppermute | solution.py:343
  8.7 2.8 %pack.3 = (bf16[32,4224]{1,0:T(8,128)(2,1)}, bf16[32,4224]{1,0:T(8,128)(2,1)}, bf16[32,4224]{1,0:T(8,128)(2,1)}) custom-call(s32[1]{0:T(128)} %bitcast.etp, s32[8,128]{1,0:T(8,128)} %bitcast.12, bf16[8,128]{1,0:T(8,128)(2,1)} %bitcast.24, bf16[128,2048]{1,0:T(8,128)(2,1)} %tokens.3, bf16[128,2048]{1,0:T(8,128)(2,1)} %grad_out.3), custom_call_target="tpu_custom_call" | custom-call | tf_op jit(solution)/shard_map/pack/pallas_call | solution.py:263
  14.1 1.6 %pad_maximum_fusion.gate_up = bf16[768,2048]{1,0:T(8,128)(2,1)S(1)} fusion(bf16[384,2048]{1,0:T(8,128)(2,1)S(1)} %bitcast.18, bf16[384,2048]{1,0:T(8,128)(2,1)} %bitcast.19), kind=kLoop, calls=%fused_computation | loop fusion | flops 6291456 | bytes 6291456 | tf_op jit(solution)/shard_map/concatenate | solution.py:349
  15.7 1.6 %collective-permute-start.3 = (bf16[32,4224]{1,0:T(8,128)(2,1)S(1)}, bf16[32,4224]{1,0:T(8,128)(2,1)S(1)}, u32[]{:S(2)}, u32[]{:S(2)}) collective-permute-start(bf16[32,4224]{1,0:T(8,128)(2,1)S(1)} %collective-permute-done.2), channel_id=1, source_target_pairs={{0,16},{1,17},{2,18},{3,19},{4,20},{5,21},{6,22},{7,23},{8,0},{9,1... | collective-permute-start | bytes 811016 | tf_op jit(solution)/shard_map/ppermute | solution.py:343
  17.4 1.5 %collective-permute-start.5 = (bf16[32,4224]{1,0:T(8,128)(2,1)S(1)}, bf16[32,4224]{1,0:T(8,128)(2,1)S(1)}, u32[]{:S(2)}, u32[]{:S(2)}) collective-permute-start(bf16[32,4224]{1,0:T(8,128)(2,1)S(1)} %collective-permute-done.2), channel_id=1, source_target_pairs={{0,4},{1,5},{2,6},{3,7},{4,0},{5,1},{6,2},{7,3},{8,12},{9,13},{10,... | collective-permute-start | bytes 811016 | tf_op jit(solution)/shard_map/ppermute | solution.py:343
  20.4 2.1 %collective-permute-done.1 = bf16[32,4224]{1,0:T(8,128)(2,1)S(1)} collective-permute-done((bf16[32,4224]{1,0:T(8,128)(2,1)}, bf16[32,4224]{1,0:T(8,128)(2,1)S(1)}, u32[]{:S(2)}, u32[]{:S(2)}) %collective-permute-start.1) | collective-permute-done | bytes 270368 | tf_op jit(solution)/shard_map/ppermute | solution.py:343
  23.3 3.6 %collective-permute-done.5 = bf16[32,4224]{1,0:T(8,128)(2,1)S(1)} collective-permute-done((bf16[32,4224]{1,0:T(8,128)(2,1)S(1)}, bf16[32,4224]{1,0:T(8,128)(2,1)S(1)}, u32[]{:S(2)}, u32[]{:S(2)}) %collective-permute-start.5) | collective-permute-done | bytes 270368 | tf_op jit(solution)/shard_map/ppermute | solution.py:343
  26.9 1.6 %collective-permute-start.8 = (bf16[32,4224]{1,0:T(8,128)(2,1)S(1)}, bf16[32,4224]{1,0:T(8,128)(2,1)S(1)}, u32[]{:S(2)}, u32[]{:S(2)}) collective-permute-start(bf16[32,4224]{1,0:T(8,128)(2,1)S(1)} %collective-permute-done.5), channel_id=1, source_target_pairs={{0,2},{1,3},{2,0},{3,1},{4,6},{5,7},{6,4},{7,5},{8,10},{9,11},{10,... | collective-permute-start | bytes 811016 | tf_op jit(solution)/shard_map/ppermute | solution.py:343
  28.6 1.6 %collective-permute-start.13 = (bf16[32,4224]{1,0:T(8,128)(2,1)S(1)}, bf16[32,4224]{1,0:T(8,128)(2,1)S(1)}, u32[]{:S(2)}, u32[]{:S(2)}) collective-permute-start(bf16[32,4224]{1,0:T(8,128)(2,1)S(1)} %collective-permute-done.3), channel_id=1, source_target_pairs={{0,4},{1,5},{2,6},{3,7},{4,0},{5,1},{6,2},{7,3},{8,12},{9,13},{10,... | collective-permute-start | bytes 811016 | tf_op jit(solution)/shard_map/ppermute | solution.py:343
  30.2 4.6 %collective-permute-done.9 = bf16[32,4224]{1,0:T(8,128)(2,1)S(1)} collective-permute-done((bf16[32,4224]{1,0:T(8,128)(2,1)S(1)}, bf16[32,4224]{1,0:T(8,128)(2,1)S(1)}, u32[]{:S(2)}, u32[]{:S(2)}) %collective-permute-start.9) | collective-permute-done | bytes 270368 | tf_op jit(solution)/shard_map/ppermute | solution.py:343
  36.4 1.5 %collective-permute-start.10 = (bf16[32,4224]{1,0:T(8,128)(2,1)S(1)}, bf16[32,4224]{1,0:T(8,128)(2,1)S(1)}, u32[]{:S(2)}, u32[]{:S(2)}) collective-permute-start(bf16[32,4224]{1,0:T(8,128)(2,1)S(1)} %collective-permute-done.9), channel_id=1, source_target_pairs={{0,4},{1,5},{2,6},{3,7},{4,0},{5,1},{6,2},{7,3},{8,12},{9,13},{10,... | collective-permute-start | bytes 811016 | tf_op jit(solution)/shard_map/ppermute | solution.py:343
  38.0 2.9 %stage.4 = (bf16[128,2176]{1,0:T(8,128)(2,1)S(1)}, bf16[128,2176]{1,0:T(8,128)(2,1)S(1)}, bf16[256,768]{1,0:T(8,128)(2,1)S(1)}, bf16[256,384]{1,0:T(8,128)(2,1)S(1)}) custom-call(s32[1]{0:T(128)} %bitcast.2.base_ref, bf16[128,4224]{1,0:T(8,128)(2,1)S(1)} %pad_maximum_fusion.1.mine.refs_0_, ...), custom_call_target="tpu_custom_call" | custom-call | flops 2013265920 | bytes 4325376 | tf_op jit(solution)/shard_map/stage/pallas_call | solution.py:166
  45.7 2.9 %stage.5 = (bf16[128,2176]{1,0:T(8,128)(2,1)S(1)}, bf16[128,2176]{1,0:T(8,128)(2,1)S(1)}, bf16[256,768]{1,0:T(8,128)(2,1)S(1)}, bf16[256,384]{1,0:T(8,128)(2,1)S(1)}) custom-call(s32[1]{0:T(128)} %bitcast.2.base_ref, bf16[128,4224]{1,0:T(8,128)(2,1)S(1)} %constant_dynamic-update-slice_fusion.3.mine.refs_3_, ...), custom_call_target="tpu_custom_call" | custom-call | flops 2013265920 | bytes 4325376 | tf_op jit(solution)/shard_map/stage/pallas_call | solution.py:166
  50.9 1.6 %collective-permute-start.20 = (bf16[64,2176]{1,0:T(8,128)(2,1)S(1)}, bf16[64,2176]{1,0:T(8,128)(2,1)S(1)}, u32[]{:S(2)}, u32[]{:S(2)}) collective-permute-start(bf16[64,2176]{1,0:T(8,128)(2,1)S(1)} %slice.83), channel_id=1, source_target_pairs={{0,4},{1,5},{2,6},{3,7},{4,0},{5,1},{6,2},{7,3},{8,12},{9,13},{10,... | collective-permute-start | bytes 835592 | tf_op jit(solution)/shard_map/ppermute | solution.py:343
  52.5 2.9 %stage.6 = (bf16[128,2176]{1,0:T(8,128)(2,1)S(1)}, bf16[128,2176]{1,0:T(8,128)(2,1)S(1)}, bf16[256,768]{1,0:T(8,128)(2,1)S(1)}, bf16[256,384]{1,0:T(8,128)(2,1)S(1)}) custom-call(s32[1]{0:T(128)} %bitcast.2.base_ref, bf16[128,4224]{1,0:T(8,128)(2,1)S(1)} %pad_maximum_fusion.2.mine.refs_6_, bf16[128,4224]{1,0:T(8,128)(2,1)S(1)} %collective-permute-done.15.theirs.refs_7_, ...), custom_call_target="tpu_custom_call" | custom-call | flops 2013265920 | bytes 4325376 | tf_op jit(solution)/shard_map/stage/pallas_call | solution.py:166
  59.7 2.2 %collective-permute-start.25 = (bf16[64,2176]{1,0:T(8,128)(2,1)S(1)}, bf16[64,2176]{1,0:T(8,128)(2,1)S(1)}, u32[]{:S(2)}, u32[]{:S(2)}) collective-permute-start(bf16[64,2176]{1,0:T(8,128)(2,1)S(1)} %fusion.1), channel_id=1, source_target_pairs={{0,8},{1,9},{2,10},{3,11},{4,12},{5,13},{6,14},{7,15},{8,24},{9,25... | collective-permute-start | bytes 835592 | tf_op jit(solution)/shard_map/ppermute | solution.py:343
  61.9 2.9 %stage.7 = (bf16[128,2176]{1,0:T(8,128)(2,1)S(1)}, bf16[128,2176]{1,0:T(8,128)(2,1)S(1)}, bf16[256,768]{1,0:T(8,128)(2,1)S(1)}, bf16[256,384]{1,0:T(8,128)(2,1)S(1)}) custom-call(s32[1]{0:T(128)} %bitcast.2.base_ref, bf16[128,4224]{1,0:T(8,128)(2,1)S(1)} %constant_dynamic-update-slice_fusion.7.mine.refs_9_, ...), custom_call_target="tpu_custom_call" | custom-call | flops 2013265920 | bytes 4325376 | tf_op jit(solution)/shard_map/stage/pallas_call | solution.py:166
  66.4 3.0 %collective-permute-start.24 = (bf16[64,2176]{1,0:T(8,128)(2,1)S(1)}, bf16[64,2176]{1,0:T(8,128)(2,1)S(1)}, u32[]{:S(2)}, u32[]{:S(2)}) collective-permute-start(bf16[64,2176]{1,0:T(8,128)(2,1)S(1)} %slice_add_fusion.2), channel_id=1, source_target_pairs={{0,16},{1,17},{2,18},{3,19},{4,20},{5,21},{6,22},{7,23},{8,0},{9,1... | collective-permute-start | bytes 835592 | tf_op jit(solution)/shard_map/ppermute | solution.py:343
  71.1 5.7 %weight_grads.3 = bf16[384,2048]{1,0:T(8,128)(2,1)} custom-call(bf16[128,4224]{1,0:T(8,128)(2,1)} %copy-done, bf16[128,4224]{1,0:T(8,128)(2,1)} %copy-done.3, bf16[256,384]{1,0:T(8,128)(2,1)} %copy-done.12, bf16[128,4224]{1,0:T(8,128)(2,1)} %copy-done.2, bf16[128,4224]{1,0:T(8,128)(2,1)} %copy-done.5, bf16[256,384]{1,0:T(8,128)(2,1)} %copy-done.13, ...), custom_call_target="tpu_custom_call" | custom-call | flops 1610612736 | bytes 5767168 | tf_op jit(solution)/shard_map/weight_grads/pallas_call | solution.py:206
  79.7 5.7 %weight_grads.4 = bf16[384,2048]{1,0:T(8,128)(2,1)} custom-call(bf16[128,4224]{1,0:T(8,128)(2,1)} %copy-done, bf16[128,4224]{1,0:T(8,128)(2,1)} %copy-done.3, bf16[256,768]{1,0:T(8,128)(2,1)} %copy-done.8, bf16[128,4224]{1,0:T(8,128)(2,1)} %copy-done.2, bf16[128,4224]{1,0:T(8,128)(2,1)} %copy-done.5, bf16[256,768]{1,0:T(8,128)(2,1)} %copy-done.9, ...), custom_call_target="tpu_custom_call" | custom-call | flops 1610612736 | bytes 5767168 | tf_op jit(solution)/shard_map/weight_grads/pallas_call | solution.py:206
  86.3 5.7 %weight_grads.5 = bf16[384,2048]{1,0:T(8,128)(2,1)} custom-call(bf16[128,4224]{1,0:T(8,128)(2,1)} %copy-done, bf16[128,4224]{1,0:T(8,128)(2,1)} %copy-done.3, bf16[256,768]{1,0:T(8,128)(2,1)} %copy-done.8, bf16[128,4224]{1,0:T(8,128)(2,1)} %copy-done.2, bf16[128,4224]{1,0:T(8,128)(2,1)} %copy-done.5, bf16[256,768]{1,0:T(8,128)(2,1)} %copy-done.9, ...), custom_call_target="tpu_custom_call" | custom-call | flops 1610612736 | bytes 5767168 | tf_op jit(solution)/shard_map/weight_grads/pallas_call | solution.py:206
  92.3 1.5 %collective-permute-done.29.far = bf16[64,2176]{1,0:T(8,128)(2,1)S(1)} collective-permute-done((bf16[64,2176]{1,0:T(8,128)(2,1)S(1)}, bf16[64,2176]{1,0:T(8,128)(2,1)S(1)}, u32[]{:S(2)}, u32[]{:S(2)}) %collective-permute-start.29) | collective-permute-done | bytes 278560 | tf_op jit(solution)/shard_map/ppermute | solution.py:343
  (119 shorter events, 25.9 us)
Async XLA Ops:
  3.1 12.7 %collective-permute-start.2 = (bf16[32,4224]{1,0:T(8,128)(2,1)}, bf16[32,4224]{1,0:T(8,128)(2,1)S(1)}, u32[]{:S(2)}, u32[]{:S(2)}) collective-permute-start(bf16[32,4224]{1,0:T(8,128)(2,1)} %pack.2), channel_id=1, source_target_pairs={{0,16},{1,17},{2,18},{3,19},{4,20},{5,21},{6,22},{7,23},{8,0},{9,1... | collective-permute-start | bytes 811016 | tf_op jit(solution)/shard_map/ppermute | solution.py:343
  7.1 16.0 %collective-permute-start = (bf16[32,4224]{1,0:T(8,128)(2,1)}, bf16[32,4224]{1,0:T(8,128)(2,1)S(1)}, u32[]{:S(2)}, u32[]{:S(2)}) collective-permute-start(bf16[32,4224]{1,0:T(8,128)(2,1)} %pack.2), channel_id=1, source_target_pairs={{0,4},{1,5},{2,6},{3,7},{4,0},{5,1},{6,2},{7,3},{8,12},{9,13},{10,... | collective-permute-start | bytes 811016 | tf_op jit(solution)/shard_map/ppermute | solution.py:343
  11.5 11.0 %collective-permute-start.1 = (bf16[32,4224]{1,0:T(8,128)(2,1)}, bf16[32,4224]{1,0:T(8,128)(2,1)S(1)}, u32[]{:S(2)}, u32[]{:S(2)}) collective-permute-start(bf16[32,4224]{1,0:T(8,128)(2,1)} %get-tuple-element.66), channel_id=1, source_target_pairs={{0,4},{1,5},{2,6},{3,7},{4,0},{5,1},{6,2},{7,3},{8,12},{9,13},{10,... | collective-permute-start | bytes 811016 | tf_op jit(solution)/shard_map/ppermute | solution.py:343
  15.7 7.4 %collective-permute-start.3 = (bf16[32,4224]{1,0:T(8,128)(2,1)S(1)}, bf16[32,4224]{1,0:T(8,128)(2,1)S(1)}, u32[]{:S(2)}, u32[]{:S(2)}) collective-permute-start(bf16[32,4224]{1,0:T(8,128)(2,1)S(1)} %collective-permute-done.2), channel_id=1, source_target_pairs={{0,16},{1,17},{2,18},{3,19},{4,20},{5,21},{6,22},{7,23},{8,0},{9,1... | collective-permute-start | bytes 811016 | tf_op jit(solution)/shard_map/ppermute | solution.py:343
  17.4 9.5 %collective-permute-start.5 = (bf16[32,4224]{1,0:T(8,128)(2,1)S(1)}, bf16[32,4224]{1,0:T(8,128)(2,1)S(1)}, u32[]{:S(2)}, u32[]{:S(2)}) collective-permute-start(bf16[32,4224]{1,0:T(8,128)(2,1)S(1)} %collective-permute-done.2), channel_id=1, source_target_pairs={{0,4},{1,5},{2,6},{3,7},{4,0},{5,1},{6,2},{7,3},{8,12},{9,13},{10,... | collective-permute-start | bytes 811016 | tf_op jit(solution)/shard_map/ppermute | solution.py:343
  18.9 8.0 %collective-permute-start.6 = (bf16[32,4224]{1,0:T(8,128)(2,1)S(1)}, bf16[32,4224]{1,0:T(8,128)(2,1)S(1)}, u32[]{:S(2)}, u32[]{:S(2)}) collective-permute-start(bf16[32,4224]{1,0:T(8,128)(2,1)S(1)} %collective-permute-done.2), channel_id=1, source_target_pairs={{0,2},{1,3},{2,0},{3,1},{4,6},{5,7},{6,4},{7,5},{8,10},{9,11},{10,... | collective-permute-start | bytes 811016 | tf_op jit(solution)/shard_map/ppermute | solution.py:343
  23.2 14.7 %collective-permute-start.4 = (bf16[64,4224]{1,0:T(8,128)(2,1)S(1)}, bf16[64,4224]{1,0:T(8,128)(2,1)S(1)}, u32[]{:S(2)}, u32[]{:S(2)}) collective-permute-start(bf16[64,4224]{1,0:T(8,128)(2,1)S(1)} %pad_maximum_fusion.3), channel_id=1, source_target_pairs={{0,1},{1,0},{2,3},{3,2},{4,5},{5,4},{6,7},{7,6},{8,9},{9,8},{10,11... | collective-permute-start | bytes 1622024 | tf_op jit(solution)/shard_map/ppermute | solution.py:343
  26.9 7.9 %collective-permute-start.9 = (bf16[32,4224]{1,0:T(8,128)(2,1)S(1)}, bf16[32,4224]{1,0:T(8,128)(2,1)S(1)}, u32[]{:S(2)}, u32[]{:S(2)}) collective-permute-start(bf16[32,4224]{1,0:T(8,128)(2,1)S(1)} %copy-done.19), channel_id=1, source_target_pairs={{0,8},{1,9},{2,10},{3,11},{4,12},{5,13},{6,14},{7,15},{8,24},{9,25... | collective-permute-start | bytes 811016 | tf_op jit(solution)/shard_map/ppermute | solution.py:343
  26.9 14.1 %collective-permute-start.8 = (bf16[32,4224]{1,0:T(8,128)(2,1)S(1)}, bf16[32,4224]{1,0:T(8,128)(2,1)S(1)}, u32[]{:S(2)}, u32[]{:S(2)}) collective-permute-start(bf16[32,4224]{1,0:T(8,128)(2,1)S(1)} %collective-permute-done.5), channel_id=1, source_target_pairs={{0,2},{1,3},{2,0},{3,1},{4,6},{5,7},{6,4},{7,5},{8,10},{9,11},{10,... | collective-permute-start | bytes 811016 | tf_op jit(solution)/shard_map/ppermute | solution.py:343
  28.6 6.8 %collective-permute-start.13 = (bf16[32,4224]{1,0:T(8,128)(2,1)S(1)}, bf16[32,4224]{1,0:T(8,128)(2,1)S(1)}, u32[]{:S(2)}, u32[]{:S(2)}) collective-permute-start(bf16[32,4224]{1,0:T(8,128)(2,1)S(1)} %collective-permute-done.3), channel_id=1, source_target_pairs={{0,4},{1,5},{2,6},{3,7},{4,0},{5,1},{6,2},{7,3},{8,12},{9,13},{10,... | collective-permute-start | bytes 811016 | tf_op jit(solution)/shard_map/ppermute | solution.py:343
  34.8 7.4 %collective-permute-start.11 = (bf16[32,4224]{1,0:T(8,128)(2,1)S(1)}, bf16[32,4224]{1,0:T(8,128)(2,1)S(1)}, u32[]{:S(2)}, u32[]{:S(2)}) collective-permute-start(bf16[32,4224]{1,0:T(8,128)(2,1)S(1)} %copy-done.20), channel_id=1, source_target_pairs={{0,8},{1,9},{2,10},{3,11},{4,12},{5,13},{6,14},{7,15},{8,24},{9,25... | collective-permute-start | bytes 811016 | tf_op jit(solution)/shard_map/ppermute | solution.py:343
  35.5 13.4 %collective-permute-start.14 = (bf16[64,4224]{1,0:T(8,128)(2,1)S(1)}, bf16[64,4224]{1,0:T(8,128)(2,1)S(1)}, u32[]{:S(2)}, u32[]{:S(2)}) collective-permute-start(bf16[64,4224]{1,0:T(8,128)(2,1)S(1)} %pad_maximum_fusion.4), channel_id=1, source_target_pairs={{0,2},{1,3},{2,0},{3,1},{4,6},{5,7},{6,4},{7,5},{8,10},{9,11},{10,... | collective-permute-start | bytes 1622024 | tf_op jit(solution)/shard_map/ppermute | solution.py:343
  36.4 6.5 %collective-permute-start.10 = (bf16[32,4224]{1,0:T(8,128)(2,1)S(1)}, bf16[32,4224]{1,0:T(8,128)(2,1)S(1)}, u32[]{:S(2)}, u32[]{:S(2)}) collective-permute-start(bf16[32,4224]{1,0:T(8,128)(2,1)S(1)} %collective-permute-done.9), channel_id=1, source_target_pairs={{0,4},{1,5},{2,6},{3,7},{4,0},{5,1},{6,2},{7,3},{8,12},{9,13},{10,... | collective-permute-start | bytes 811016 | tf_op jit(solution)/shard_map/ppermute | solution.py:343
  43.0 12.5 %collective-permute-start.17 = (bf16[32,4224]{1,0:T(8,128)(2,1)S(1)}, bf16[32,4224]{1,0:T(8,128)(2,1)S(1)}, u32[]{:S(2)}, u32[]{:S(2)}) collective-permute-start(bf16[32,4224]{1,0:T(8,128)(2,1)S(1)} %collective-permute-done.10), channel_id=1, source_target_pairs={{0,2},{1,3},{2,0},{3,1},{4,6},{5,7},{6,4},{7,5},{8,10},{9,11},{10,... | collective-permute-start | bytes 811016 | tf_op jit(solution)/shard_map/ppermute | solution.py:343
  44.2 26.8 %collective-permute-start.7 = (bf16[128,2176]{1,0:T(8,128)(2,1)S(1)}, bf16[128,2176]{1,0:T(8,128)(2,1)S(1)}, u32[]{:S(2)}, u32[]{:S(2)}) collective-permute-start(bf16[128,2176]{1,0:T(8,128)(2,1)S(1)} %get-tuple-element.60), channel_id=1, source_target_pairs={{0,1},{1,0},{2,3},{3,2},{4,5},{5,4},{6,7},{7,6},{8,9},{9,8},{10,11... | collective-permute-start | bytes 1671176 | tf_op jit(solution)/shard_map/ppermute | solution.py:343
  50.9 8.8 %collective-permute-start.20 = (bf16[64,2176]{1,0:T(8,128)(2,1)S(1)}, bf16[64,2176]{1,0:T(8,128)(2,1)S(1)}, u32[]{:S(2)}, u32[]{:S(2)}) collective-permute-start(bf16[64,2176]{1,0:T(8,128)(2,1)S(1)} %slice.83), channel_id=1, source_target_pairs={{0,4},{1,5},{2,6},{3,7},{4,0},{5,1},{6,2},{7,3},{8,12},{9,13},{10,... | collective-permute-start | bytes 835592 | tf_op jit(solution)/shard_map/ppermute | solution.py:343
  55.5 6.3 %collective-permute-start.18 = (bf16[128,4224]{1,0:T(8,128)(2,1)S(1)}, bf16[128,4224]{1,0:T(8,128)(2,1)S(1)}, u32[]{:S(2)}, u32[]{:S(2)}) collective-permute-start(bf16[128,4224]{1,0:T(8,128)(2,1)S(1)} %constant_dynamic-update-slice_fusion.7.mine.refs_9_), channel_id=1, source_target_pairs={{0,1},{1,0},{2,3},{3,2},{4,5},{5,4},{6,7},{7,6},{8,9},{9,8},{10,11... | collective-permute-start | bytes 3244040 | tf_op jit(solution)/shard_map/ppermute | solution.py:343
  57.6 8.8 %collective-permute-start.21 = (bf16[64,2176]{1,0:T(8,128)(2,1)S(1)}, bf16[64,2176]{1,0:T(8,128)(2,1)S(1)}, u32[]{:S(2)}, u32[]{:S(2)}) collective-permute-start(bf16[64,2176]{1,0:T(8,128)(2,1)S(1)} %slice.82), channel_id=1, source_target_pairs={{0,4},{1,5},{2,6},{3,7},{4,0},{5,1},{6,2},{7,3},{8,12},{9,13},{10,... | collective-permute-start | bytes 835592 | tf_op jit(solution)/shard_map/ppermute | solution.py:343
  59.7 17.1 %collective-permute-start.25 = (bf16[64,2176]{1,0:T(8,128)(2,1)S(1)}, bf16[64,2176]{1,0:T(8,128)(2,1)S(1)}, u32[]{:S(2)}, u32[]{:S(2)}) collective-permute-start(bf16[64,2176]{1,0:T(8,128)(2,1)S(1)} %fusion.1), channel_id=1, source_target_pairs={{0,8},{1,9},{2,10},{3,11},{4,12},{5,13},{6,14},{7,15},{8,24},{9,25... | collective-permute-start | bytes 835592 | tf_op jit(solution)/shard_map/ppermute | solution.py:343
  66.4 10.4 %collective-permute-start.24 = (bf16[64,2176]{1,0:T(8,128)(2,1)S(1)}, bf16[64,2176]{1,0:T(8,128)(2,1)S(1)}, u32[]{:S(2)}, u32[]{:S(2)}) collective-permute-start(bf16[64,2176]{1,0:T(8,128)(2,1)S(1)} %slice_add_fusion.2), channel_id=1, source_target_pairs={{0,16},{1,17},{2,18},{3,19},{4,20},{5,21},{6,22},{7,23},{8,0},{9,1... | collective-permute-start | bytes 835592 | tf_op jit(solution)/shard_map/ppermute | solution.py:343
  69.6 7.7 %collective-permute-start.23 = (bf16[64,2176]{1,0:T(8,128)(2,1)S(1)}, bf16[64,2176]{1,0:T(8,128)(2,1)S(1)}, u32[]{:S(2)}, u32[]{:S(2)}) collective-permute-start(bf16[64,2176]{1,0:T(8,128)(2,1)S(1)} %slice.81), channel_id=1, source_target_pairs={{0,4},{1,5},{2,6},{3,7},{4,0},{5,1},{6,2},{7,3},{8,12},{9,13},{10,... | collective-permute-start | bytes 835592 | tf_op jit(solution)/shard_map/ppermute | solution.py:343
  77.3 8.0 %collective-permute-start.27 = (bf16[64,2176]{1,0:T(8,128)(2,1)S(1)}, bf16[64,2176]{1,0:T(8,128)(2,1)S(1)}, u32[]{:S(2)}, u32[]{:S(2)}) collective-permute-start(bf16[64,2176]{1,0:T(8,128)(2,1)S(1)} %slice.80), channel_id=1, source_target_pairs={{0,4},{1,5},{2,6},{3,7},{4,0},{5,1},{6,2},{7,3},{8,12},{9,13},{10,... | collective-permute-start | bytes 835592 | tf_op jit(solution)/shard_map/ppermute | solution.py:343
  78.7 6.6 %collective-permute-start.26 = (bf16[64,2176]{1,0:T(8,128)(2,1)S(1)}, bf16[64,2176]{1,0:T(8,128)(2,1)S(1)}, u32[]{:S(2)}, u32[]{:S(2)}) collective-permute-start(bf16[64,2176]{1,0:T(8,128)(2,1)S(1)} %fusion), channel_id=1, source_target_pairs={{0,16},{1,17},{2,18},{3,19},{4,20},{5,21},{6,22},{7,23},{8,0},{9,1... | collective-permute-start | bytes 835592 | tf_op jit(solution)/shard_map/ppermute | solution.py:343
  85.5 6.6 %collective-permute-start.28 = (bf16[64,2176]{1,0:T(8,128)(2,1)S(1)}, bf16[64,2176]{1,0:T(8,128)(2,1)S(1)}, u32[]{:S(2)}, u32[]{:S(2)}) collective-permute-start(bf16[64,2176]{1,0:T(8,128)(2,1)S(1)} %fusion.4), channel_id=1, source_target_pairs={{0,2},{1,3},{2,0},{3,1},{4,6},{5,7},{6,4},{7,5},{8,10},{9,11},{10,... | collective-permute-start | bytes 835592 | tf_op jit(solution)/shard_map/ppermute | solution.py:343
  (27 other events, 119.1 us)

commit v6 on v5

--- a/solution.py
+++ b/solution.py
@@ -355,7 +355,7 @@
     line[3] = move(after(here, line[2]), along(-1))
     other = {s: move(line[s], over_y) for s in range(lines)}
     line_x = {0: near, 1: move(line[1], over_x), 3: move(after(near, line[3]), along(-1))}
-    other_x = {0: move(near, over_y)}
+    other_x = {0: move(after(near, other[1]), over_y)}
     ready, line_x[1], gate_up = lax.optimization_barrier((other[1], line_x[1], gate_up))
     other_x[1] = move(ready, over_x)
     pair = move(jnp.concatenate([line[2], after(other[2], line[3])], axis=0), over_x)

time: 95.3 us -> 95 us (level)
  starting transfers between devices: 31.8 us -> 26.7 us
  waiting for transfers between devices: 21.2 us -> 23.9 us
  local copies, waits for them, and re-layouts: 2.92 us -> 4.94 us
    ppermute x30, starting transfers between devices: 31.8 us -> 26.7 us  [move(): return lax.ppermute(value, axes, pairs)]
    ppermute x30, waiting for transfers between devices: 21.2 us -> 23.9 us  [move(): return lax.ppermute(value, axes, pairs)]
    unnamed x50, local copies, waits for them, and re-layouts: 2.63 us -> 4.64 us
  transfers between devices with their start and end apart: 30 -> 30, of which waited for: 15 -> 13; matrix products, arithmetic and copies ran while one was open for 5% -> 5% of each run, Pallas kernels for 33% -> 33%
where the time goes in v6:
time: 95 us; the launch traced here: 94.4 us
  Pallas kernels  34.8 us (37%)
  starting transfers between devices  26.7 us (28%)
  waiting for transfers between devices  23.9 us (25%)
  local copies, waits for them, and re-layouts  4.94 us (5%)
  other arithmetic  2.82 us (3%)
  between operations  1.17 us (1%)
    ppermute x30, starting transfers between devices, move(): return lax.ppermute(value, axes, pairs)  26.7 us
    ppermute x30, waiting for transfers between devices, move(): return lax.ppermute(value, axes, pairs)  23.9 us
    pallas_call x3, Pallas kernels, weight_grads(): pl.pallas_call(functools.partial(weights_kernel, len(parts)), grid=(tiles...  17 us
    pallas_call x4, Pallas kernels, stage(): pl.pallas_call(functools.partial(stage_kernel, local_experts), out_shape=...  11.7 us
    pallas_call x2, Pallas kernels, pack(): pl.pallas_call(functools.partial(pack_kernel, step, first), out_shape=(ja...  5.24 us
    unnamed x50, local copies, waits for them, and re-layouts  4.64 us
  transfers between devices with their start and end apart: 30, of which 13 were waited for; matrix products, arithmetic and copies ran while one was open for 5% of the time, Pallas kernels for 33%

profile of v6, /device:TPU:0, one launch (start us, length us, event | category | flops | bytes accessed | tf_op | source)
XLA Modules:
  0.0 94.4 jit_solution(7402320960212307274)
XLA Ops:
  0.6 2.4 %pack.2 = bf16[32,4224]{1,0:T(8,128)(2,1)} custom-call(s32[1]{0:T(128)} %bitcast.etp, s32[8,128]{1,0:T(8,128)} %bitcast.11, bf16[8,128]{1,0:T(8,128)(2,1)} %bitcast.23, bf16[128,2048]{1,0:T(8,128)(2,1)} %tokens.3, bf16[128,2048]{1,0:T(8,128)(2,1)} %grad_out.3), custom_call_target="tpu_custom_call" | custom-call | tf_op jit(solution)/shard_map/pack/pallas_call | solution.py:263
  3.1 4.1 %collective-permute-start.1 = (bf16[32,4224]{1,0:T(8,128)(2,1)}, bf16[32,4224]{1,0:T(8,128)(2,1)S(1)}, u32[]{:S(2)}, u32[]{:S(2)}) collective-permute-start(bf16[32,4224]{1,0:T(8,128)(2,1)} %pack.2), channel_id=1, source_target_pairs={{0,16},{1,17},{2,18},{3,19},{4,20},{5,21},{6,22},{7,23},{8,0},{9,1... | collective-permute-start | bytes 811016 | tf_op jit(solution)/shard_map/ppermute | solution.py:343
  7.1 1.5 %collective-permute-start = (bf16[32,4224]{1,0:T(8,128)(2,1)}, bf16[32,4224]{1,0:T(8,128)(2,1)S(1)}, u32[]{:S(2)}, u32[]{:S(2)}) collective-permute-start(bf16[32,4224]{1,0:T(8,128)(2,1)} %pack.2), channel_id=1, source_target_pairs={{0,4},{1,5},{2,6},{3,7},{4,0},{5,1},{6,2},{7,3},{8,12},{9,13},{10,... | collective-permute-start | bytes 811016 | tf_op jit(solution)/shard_map/ppermute | solution.py:343
  8.7 2.8 %pack.3 = (bf16[32,4224]{1,0:T(8,128)(2,1)}, bf16[32,4224]{1,0:T(8,128)(2,1)}, bf16[32,4224]{1,0:T(8,128)(2,1)}) custom-call(s32[1]{0:T(128)} %bitcast.etp, s32[8,128]{1,0:T(8,128)} %bitcast.12, bf16[8,128]{1,0:T(8,128)(2,1)} %bitcast.24, bf16[128,2048]{1,0:T(8,128)(2,1)} %tokens.3, bf16[128,2048]{1,0:T(8,128)(2,1)} %grad_out.3), custom_call_target="tpu_custom_call" | custom-call | tf_op jit(solution)/shard_map/pack/pallas_call | solution.py:263
  13.5 1.7 %pad_maximum_fusion.gate_up = bf16[768,2048]{1,0:T(8,128)(2,1)S(1)} fusion(bf16[384,2048]{1,0:T(8,128)(2,1)S(1)} %bitcast.18, bf16[384,2048]{1,0:T(8,128)(2,1)} %bitcast.19), kind=kLoop, calls=%fused_computation | loop fusion | flops 6291456 | bytes 6291456 | tf_op jit(solution)/shard_map/concatenate | solution.py:349
  15.8 2.2 %collective-permute-start.4 = (bf16[32,4224]{1,0:T(8,128)(2,1)S(1)}, bf16[32,4224]{1,0:T(8,128)(2,1)S(1)}, u32[]{:S(2)}, u32[]{:S(2)}) collective-permute-start(bf16[32,4224]{1,0:T(8,128)(2,1)S(1)} %collective-permute-done.1), channel_id=1, source_target_pairs={{0,16},{1,17},{2,18},{3,19},{4,20},{5,21},{6,22},{7,23},{8,0},{9,1... | collective-permute-start | bytes 811016 | tf_op jit(solution)/shard_map/ppermute | solution.py:343
  19.5 3.4 %collective-permute-done.2 = bf16[32,4224]{1,0:T(8,128)(2,1)S(1)} collective-permute-done((bf16[32,4224]{1,0:T(8,128)(2,1)S(1)}, bf16[32,4224]{1,0:T(8,128)(2,1)S(1)}, u32[]{:S(2)}, u32[]{:S(2)}) %collective-permute-start.2) | collective-permute-done | bytes 270368 | tf_op jit(solution)/shard_map/ppermute | solution.py:343
  26.5 1.6 %collective-permute-start.13 = (bf16[32,4224]{1,0:T(8,128)(2,1)S(1)}, bf16[32,4224]{1,0:T(8,128)(2,1)S(1)}, u32[]{:S(2)}, u32[]{:S(2)}) collective-permute-start(bf16[32,4224]{1,0:T(8,128)(2,1)S(1)} %collective-permute-done.4), channel_id=1, source_target_pairs={{0,4},{1,5},{2,6},{3,7},{4,0},{5,1},{6,2},{7,3},{8,12},{9,13},{10,... | collective-permute-start | bytes 811016 | tf_op jit(solution)/shard_map/ppermute | solution.py:343
  28.1 4.3 %collective-permute-done.3 = bf16[32,4224]{1,0:T(8,128)(2,1)S(1)} collective-permute-done((bf16[32,4224]{1,0:T(8,128)(2,1)S(1)}, bf16[32,4224]{1,0:T(8,128)(2,1)S(1)}, u32[]{:S(2)}, u32[]{:S(2)}) %collective-permute-start.3) | collective-permute-done | bytes 270368 | tf_op jit(solution)/shard_map/ppermute | solution.py:343
  32.6 2.9 %collective-permute-done.13 = bf16[32,4224]{1,0:T(8,128)(2,1)S(1)} collective-permute-done((bf16[32,4224]{1,0:T(8,128)(2,1)S(1)}, bf16[32,4224]{1,0:T(8,128)(2,1)S(1)}, u32[]{:S(2)}, u32[]{:S(2)}) %collective-permute-start.13) | collective-permute-done | bytes 270368 | tf_op jit(solution)/shard_map/ppermute | solution.py:343
  35.5 1.6 %collective-permute-start.14 = (bf16[64,4224]{1,0:T(8,128)(2,1)S(1)}, bf16[64,4224]{1,0:T(8,128)(2,1)S(1)}, u32[]{:S(2)}, u32[]{:S(2)}) collective-permute-start(bf16[64,4224]{1,0:T(8,128)(2,1)S(1)} %pad_maximum_fusion.4), channel_id=1, source_target_pairs={{0,2},{1,3},{2,0},{3,1},{4,6},{5,7},{6,4},{7,5},{8,10},{9,11},{10,... | collective-permute-start | bytes 1622024 | tf_op jit(solution)/shard_map/ppermute | solution.py:343
  37.8 2.0 %copy-done.17 = bf16[2,192,2048]{2,1,0:T(8,128)(2,1)S(1)} copy-done((bf16[2,192,2048]{2,1,0:T(8,128)(2,1)S(1)}, bf16[2,192,2048]{2,1,0:T(8,128)(2,1)}, u32[]{:S(2)}) %copy-start.17) | copy-done | bytes 1572888
  39.8 2.9 %stage.4 = (bf16[128,2176]{1,0:T(8,128)(2,1)S(1)}, bf16[128,2176]{1,0:T(8,128)(2,1)S(1)}, bf16[256,768]{1,0:T(8,128)(2,1)S(1)}, bf16[256,384]{1,0:T(8,128)(2,1)S(1)}) custom-call(s32[1]{0:T(128)} %bitcast.2.base_ref, bf16[128,4224]{1,0:T(8,128)(2,1)S(1)} %pad_maximum_fusion.1.mine.refs_0_, ...), custom_call_target="tpu_custom_call" | custom-call | flops 2013265920 | bytes 4325376 | tf_op jit(solution)/shard_map/stage/pallas_call | solution.py:166
  44.5 1.8 %collective-permute-done.12.theirs.refs_4_ = bf16[128,4224]{1,0:T(8,128)(2,1)S(1)} collective-permute-done((bf16[128,4224]{1,0:T(8,128)(2,1)S(1)}, bf16[128,4224]{1,0:T(8,128)(2,1)S(1)}, u32[]{:S(2)}, u32[]{:S(2)}) %collective-permute-start.12) | collective-permute-done | bytes 1081376 | tf_op jit(solution)/shard_map/ppermute | solution.py:343
  46.4 2.9 %stage.5 = (bf16[128,2176]{1,0:T(8,128)(2,1)S(1)}, bf16[128,2176]{1,0:T(8,128)(2,1)S(1)}, bf16[256,768]{1,0:T(8,128)(2,1)S(1)}, bf16[256,384]{1,0:T(8,128)(2,1)S(1)}) custom-call(s32[1]{0:T(128)} %bitcast.2.base_ref, bf16[128,4224]{1,0:T(8,128)(2,1)S(1)} %constant_dynamic-update-slice_fusion.3.mine.refs_3_, ...), custom_call_target="tpu_custom_call" | custom-call | flops 2013265920 | bytes 4325376 | tf_op jit(solution)/shard_map/stage/pallas_call | solution.py:166
  52.9 2.9 %stage.6 = (bf16[128,2176]{1,0:T(8,128)(2,1)S(1)}, bf16[128,2176]{1,0:T(8,128)(2,1)S(1)}, bf16[256,768]{1,0:T(8,128)(2,1)S(1)}, bf16[256,384]{1,0:T(8,128)(2,1)S(1)}) custom-call(s32[1]{0:T(128)} %bitcast.2.base_ref, bf16[128,4224]{1,0:T(8,128)(2,1)S(1)} %pad_maximum_fusion.2.mine.refs_6_, bf16[128,4224]{1,0:T(8,128)(2,1)S(1)} %collective-permute-done.15.theirs.refs_7_, ...), custom_call_target="tpu_custom_call" | custom-call | flops 2013265920 | bytes 4325376 | tf_op jit(solution)/shard_map/stage/pallas_call | solution.py:166
  61.4 2.9 %stage.7 = (bf16[128,2176]{1,0:T(8,128)(2,1)S(1)}, bf16[128,2176]{1,0:T(8,128)(2,1)S(1)}, bf16[256,768]{1,0:T(8,128)(2,1)S(1)}, bf16[256,384]{1,0:T(8,128)(2,1)S(1)}) custom-call(s32[1]{0:T(128)} %bitcast.2.base_ref, bf16[128,4224]{1,0:T(8,128)(2,1)S(1)} %constant_dynamic-update-slice_fusion.7.mine.refs_9_, ...), custom_call_target="tpu_custom_call" | custom-call | flops 2013265920 | bytes 4325376 | tf_op jit(solution)/shard_map/stage/pallas_call | solution.py:166
  64.4 2.4 %collective-permute-done.21 = bf16[64,2176]{1,0:T(8,128)(2,1)S(1)} collective-permute-done((bf16[64,2176]{1,0:T(8,128)(2,1)S(1)}, bf16[64,2176]{1,0:T(8,128)(2,1)S(1)}, u32[]{:S(2)}, u32[]{:S(2)}) %collective-permute-start.21) | collective-permute-done | bytes 278560 | tf_op jit(solution)/shard_map/ppermute | solution.py:343
  66.9 1.9 %collective-permute-start.24 = (bf16[64,2176]{1,0:T(8,128)(2,1)S(1)}, bf16[64,2176]{1,0:T(8,128)(2,1)S(1)}, u32[]{:S(2)}, u32[]{:S(2)}) collective-permute-start(bf16[64,2176]{1,0:T(8,128)(2,1)S(1)} %slice_add_fusion.2), channel_id=1, source_target_pairs={{0,16},{1,17},{2,18},{3,19},{4,20},{5,21},{6,22},{7,23},{8,0},{9,1... | collective-permute-start | bytes 835592 | tf_op jit(solution)/shard_map/ppermute | solution.py:343
  69.9 5.7 %weight_grads.3 = bf16[384,2048]{1,0:T(8,128)(2,1)} custom-call(bf16[128,4224]{1,0:T(8,128)(2,1)} %copy-done, bf16[128,4224]{1,0:T(8,128)(2,1)} %copy-done.3, bf16[256,384]{1,0:T(8,128)(2,1)} %copy-done.12, bf16[128,4224]{1,0:T(8,128)(2,1)} %copy-done.2, bf16[128,4224]{1,0:T(8,128)(2,1)} %copy-done.5, bf16[256,384]{1,0:T(8,128)(2,1)} %copy-done.13, ...), custom_call_target="tpu_custom_call" | custom-call | flops 1610612736 | bytes 5767168 | tf_op jit(solution)/shard_map/weight_grads/pallas_call | solution.py:206
  78.4 5.7 %weight_grads.4 = bf16[384,2048]{1,0:T(8,128)(2,1)} custom-call(bf16[128,4224]{1,0:T(8,128)(2,1)} %copy-done, bf16[128,4224]{1,0:T(8,128)(2,1)} %copy-done.3, bf16[256,768]{1,0:T(8,128)(2,1)} %copy-done.8, bf16[128,4224]{1,0:T(8,128)(2,1)} %copy-done.2, bf16[128,4224]{1,0:T(8,128)(2,1)} %copy-done.5, bf16[256,768]{1,0:T(8,128)(2,1)} %copy-done.9, ...), custom_call_target="tpu_custom_call" | custom-call | flops 1610612736 | bytes 5767168 | tf_op jit(solution)/shard_map/weight_grads/pallas_call | solution.py:206
  84.3 1.9 %collective-permute-start.28 = (bf16[64,2176]{1,0:T(8,128)(2,1)S(1)}, bf16[64,2176]{1,0:T(8,128)(2,1)S(1)}, u32[]{:S(2)}, u32[]{:S(2)}) collective-permute-start(bf16[64,2176]{1,0:T(8,128)(2,1)S(1)} %fusion.4), channel_id=1, source_target_pairs={{0,2},{1,3},{2,0},{3,1},{4,6},{5,7},{6,4},{7,5},{8,10},{9,11},{10,... | collective-permute-start | bytes 835592 | tf_op jit(solution)/shard_map/ppermute | solution.py:343
  86.1 5.7 %weight_grads.5 = bf16[384,2048]{1,0:T(8,128)(2,1)} custom-call(bf16[128,4224]{1,0:T(8,128)(2,1)} %copy-done, bf16[128,4224]{1,0:T(8,128)(2,1)} %copy-done.3, bf16[256,768]{1,0:T(8,128)(2,1)} %copy-done.8, bf16[128,4224]{1,0:T(8,128)(2,1)} %copy-done.2, bf16[128,4224]{1,0:T(8,128)(2,1)} %copy-done.5, bf16[256,768]{1,0:T(8,128)(2,1)} %copy-done.9, ...), custom_call_target="tpu_custom_call" | custom-call | flops 1610612736 | bytes 5767168 | tf_op jit(solution)/shard_map/weight_grads/pallas_call | solution.py:206
  92.0 1.5 %collective-permute-done.29.far = bf16[64,2176]{1,0:T(8,128)(2,1)S(1)} collective-permute-done((bf16[64,2176]{1,0:T(8,128)(2,1)S(1)}, bf16[64,2176]{1,0:T(8,128)(2,1)S(1)}, u32[]{:S(2)}, u32[]{:S(2)}) %collective-permute-start.29) | collective-permute-done | bytes 278560 | tf_op jit(solution)/shard_map/ppermute | solution.py:343
  (119 shorter events, 24.5 us)
Async XLA Ops:
  3.1 12.2 %collective-permute-start.1 = (bf16[32,4224]{1,0:T(8,128)(2,1)}, bf16[32,4224]{1,0:T(8,128)(2,1)S(1)}, u32[]{:S(2)}, u32[]{:S(2)}) collective-permute-start(bf16[32,4224]{1,0:T(8,128)(2,1)} %pack.2), channel_id=1, source_target_pairs={{0,16},{1,17},{2,18},{3,19},{4,20},{5,21},{6,22},{7,23},{8,0},{9,1... | collective-permute-start | bytes 811016 | tf_op jit(solution)/shard_map/ppermute | solution.py:343
  7.1 25.2 %collective-permute-start = (bf16[32,4224]{1,0:T(8,128)(2,1)}, bf16[32,4224]{1,0:T(8,128)(2,1)S(1)}, u32[]{:S(2)}, u32[]{:S(2)}) collective-permute-start(bf16[32,4224]{1,0:T(8,128)(2,1)} %pack.2), channel_id=1, source_target_pairs={{0,4},{1,5},{2,6},{3,7},{4,0},{5,1},{6,2},{7,3},{8,12},{9,13},{10,... | collective-permute-start | bytes 811016 | tf_op jit(solution)/shard_map/ppermute | solution.py:343
  15.2 7.7 %collective-permute-start.2 = (bf16[32,4224]{1,0:T(8,128)(2,1)S(1)}, bf16[32,4224]{1,0:T(8,128)(2,1)S(1)}, u32[]{:S(2)}, u32[]{:S(2)}) collective-permute-start(bf16[32,4224]{1,0:T(8,128)(2,1)S(1)} %collective-permute-done.1), channel_id=1, source_target_pairs={{0,4},{1,5},{2,6},{3,7},{4,0},{5,1},{6,2},{7,3},{8,12},{9,13},{10,... | collective-permute-start | bytes 811016 | tf_op jit(solution)/shard_map/ppermute | solution.py:343
  15.8 9.0 %collective-permute-start.4 = (bf16[32,4224]{1,0:T(8,128)(2,1)S(1)}, bf16[32,4224]{1,0:T(8,128)(2,1)S(1)}, u32[]{:S(2)}, u32[]{:S(2)}) collective-permute-start(bf16[32,4224]{1,0:T(8,128)(2,1)S(1)} %collective-permute-done.1), channel_id=1, source_target_pairs={{0,16},{1,17},{2,18},{3,19},{4,20},{5,21},{6,22},{7,23},{8,0},{9,1... | collective-permute-start | bytes 811016 | tf_op jit(solution)/shard_map/ppermute | solution.py:343
  18.0 6.8 %collective-permute-start.6 = (bf16[32,4224]{1,0:T(8,128)(2,1)S(1)}, bf16[32,4224]{1,0:T(8,128)(2,1)S(1)}, u32[]{:S(2)}, u32[]{:S(2)}) collective-permute-start(bf16[32,4224]{1,0:T(8,128)(2,1)S(1)} %collective-permute-done.1), channel_id=1, source_target_pairs={{0,2},{1,3},{2,0},{3,1},{4,6},{5,7},{6,4},{7,5},{8,10},{9,11},{10,... | collective-permute-start | bytes 811016 | tf_op jit(solution)/shard_map/ppermute | solution.py:343
  23.0 9.4 %collective-permute-start.3 = (bf16[32,4224]{1,0:T(8,128)(2,1)S(1)}, bf16[32,4224]{1,0:T(8,128)(2,1)S(1)}, u32[]{:S(2)}, u32[]{:S(2)}) collective-permute-start(bf16[32,4224]{1,0:T(8,128)(2,1)S(1)} %copy-done.20), channel_id=1, source_target_pairs={{0,4},{1,5},{2,6},{3,7},{4,0},{5,1},{6,2},{7,3},{8,12},{9,13},{10,... | collective-permute-start | bytes 811016 | tf_op jit(solution)/shard_map/ppermute | solution.py:343
  24.8 7.7 %collective-permute-start.9 = (bf16[32,4224]{1,0:T(8,128)(2,1)S(1)}, bf16[32,4224]{1,0:T(8,128)(2,1)S(1)}, u32[]{:S(2)}, u32[]{:S(2)}) collective-permute-start(bf16[32,4224]{1,0:T(8,128)(2,1)S(1)} %copy-done.19), channel_id=1, source_target_pairs={{0,8},{1,9},{2,10},{3,11},{4,12},{5,13},{6,14},{7,15},{8,24},{9,25... | collective-permute-start | bytes 811016 | tf_op jit(solution)/shard_map/ppermute | solution.py:343
  25.0 17.8 %collective-permute-start.8 = (bf16[32,4224]{1,0:T(8,128)(2,1)S(1)}, bf16[32,4224]{1,0:T(8,128)(2,1)S(1)}, u32[]{:S(2)}, u32[]{:S(2)}) collective-permute-start(bf16[32,4224]{1,0:T(8,128)(2,1)S(1)} %collective-permute-done.2), channel_id=1, source_target_pairs={{0,2},{1,3},{2,0},{3,1},{4,6},{5,7},{6,4},{7,5},{8,10},{9,11},{10,... | collective-permute-start | bytes 811016 | tf_op jit(solution)/shard_map/ppermute | solution.py:343
  26.5 9.0 %collective-permute-start.13 = (bf16[32,4224]{1,0:T(8,128)(2,1)S(1)}, bf16[32,4224]{1,0:T(8,128)(2,1)S(1)}, u32[]{:S(2)}, u32[]{:S(2)}) collective-permute-start(bf16[32,4224]{1,0:T(8,128)(2,1)S(1)} %collective-permute-done.4), channel_id=1, source_target_pairs={{0,4},{1,5},{2,6},{3,7},{4,0},{5,1},{6,2},{7,3},{8,12},{9,13},{10,... | collective-permute-start | bytes 811016 | tf_op jit(solution)/shard_map/ppermute | solution.py:343
  32.4 5.3 %collective-permute-start.5 = (bf16[64,4224]{1,0:T(8,128)(2,1)S(1)}, bf16[64,4224]{1,0:T(8,128)(2,1)S(1)}, u32[]{:S(2)}, u32[]{:S(2)}) collective-permute-start(bf16[64,4224]{1,0:T(8,128)(2,1)S(1)} %pad_maximum_fusion.3), channel_id=1, source_target_pairs={{0,1},{1,0},{2,3},{3,2},{4,5},{5,4},{6,7},{7,6},{8,9},{9,8},{10,11... | collective-permute-start | bytes 1622024 | tf_op jit(solution)/shard_map/ppermute | solution.py:343
  32.5 10.3 %collective-permute-start.11 = (bf16[32,4224]{1,0:T(8,128)(2,1)S(1)}, bf16[32,4224]{1,0:T(8,128)(2,1)S(1)}, u32[]{:S(2)}, u32[]{:S(2)}) collective-permute-start(bf16[32,4224]{1,0:T(8,128)(2,1)S(1)} %copy-done.20), channel_id=1, source_target_pairs={{0,8},{1,9},{2,10},{3,11},{4,12},{5,13},{6,14},{7,15},{8,24},{9,25... | collective-permute-start | bytes 811016 | tf_op jit(solution)/shard_map/ppermute | solution.py:343
  35.5 14.0 %collective-permute-start.14 = (bf16[64,4224]{1,0:T(8,128)(2,1)S(1)}, bf16[64,4224]{1,0:T(8,128)(2,1)S(1)}, u32[]{:S(2)}, u32[]{:S(2)}) collective-permute-start(bf16[64,4224]{1,0:T(8,128)(2,1)S(1)} %pad_maximum_fusion.4), channel_id=1, source_target_pairs={{0,2},{1,3},{2,0},{3,1},{4,6},{5,7},{6,4},{7,5},{8,10},{9,11},{10,... | collective-permute-start | bytes 1622024 | tf_op jit(solution)/shard_map/ppermute | solution.py:343
  37.1 6.5 %collective-permute-start.10 = (bf16[32,4224]{1,0:T(8,128)(2,1)S(1)}, bf16[32,4224]{1,0:T(8,128)(2,1)S(1)}, u32[]{:S(2)}, u32[]{:S(2)}) collective-permute-start(bf16[32,4224]{1,0:T(8,128)(2,1)S(1)} %collective-permute-done.9), channel_id=1, source_target_pairs={{0,4},{1,5},{2,6},{3,7},{4,0},{5,1},{6,2},{7,3},{8,12},{9,13},{10,... | collective-permute-start | bytes 811016 | tf_op jit(solution)/shard_map/ppermute | solution.py:343
  43.7 12.4 %collective-permute-start.17 = (bf16[32,4224]{1,0:T(8,128)(2,1)S(1)}, bf16[32,4224]{1,0:T(8,128)(2,1)S(1)}, u32[]{:S(2)}, u32[]{:S(2)}) collective-permute-start(bf16[32,4224]{1,0:T(8,128)(2,1)S(1)} %collective-permute-done.10), channel_id=1, source_target_pairs={{0,2},{1,3},{2,0},{3,1},{4,6},{5,7},{6,4},{7,5},{8,10},{9,11},{10,... | collective-permute-start | bytes 811016 | tf_op jit(solution)/shard_map/ppermute | solution.py:343
  44.3 25.4 %collective-permute-start.7 = (bf16[128,2176]{1,0:T(8,128)(2,1)S(1)}, bf16[128,2176]{1,0:T(8,128)(2,1)S(1)}, u32[]{:S(2)}, u32[]{:S(2)}) collective-permute-start(bf16[128,2176]{1,0:T(8,128)(2,1)S(1)} %get-tuple-element.62), channel_id=1, source_target_pairs={{0,1},{1,0},{2,3},{3,2},{4,5},{5,4},{6,7},{7,6},{8,9},{9,8},{10,11... | collective-permute-start | bytes 1671176 | tf_op jit(solution)/shard_map/ppermute | solution.py:343
  51.5 8.8 %collective-permute-start.20 = (bf16[64,2176]{1,0:T(8,128)(2,1)S(1)}, bf16[64,2176]{1,0:T(8,128)(2,1)S(1)}, u32[]{:S(2)}, u32[]{:S(2)}) collective-permute-start(bf16[64,2176]{1,0:T(8,128)(2,1)S(1)} %slice.83), channel_id=1, source_target_pairs={{0,4},{1,5},{2,6},{3,7},{4,0},{5,1},{6,2},{7,3},{8,12},{9,13},{10,... | collective-permute-start | bytes 835592 | tf_op jit(solution)/shard_map/ppermute | solution.py:343
  56.1 5.3 %collective-permute-start.18 = (bf16[128,4224]{1,0:T(8,128)(2,1)S(1)}, bf16[128,4224]{1,0:T(8,128)(2,1)S(1)}, u32[]{:S(2)}, u32[]{:S(2)}) collective-permute-start(bf16[128,4224]{1,0:T(8,128)(2,1)S(1)} %constant_dynamic-update-slice_fusion.7.mine.refs_9_), channel_id=1, source_target_pairs={{0,1},{1,0},{2,3},{3,2},{4,5},{5,4},{6,7},{7,6},{8,9},{9,8},{10,11... | collective-permute-start | bytes 3244040 | tf_op jit(solution)/shard_map/ppermute | solution.py:343
  58.1 8.8 %collective-permute-start.21 = (bf16[64,2176]{1,0:T(8,128)(2,1)S(1)}, bf16[64,2176]{1,0:T(8,128)(2,1)S(1)}, u32[]{:S(2)}, u32[]{:S(2)}) collective-permute-start(bf16[64,2176]{1,0:T(8,128)(2,1)S(1)} %slice.82), channel_id=1, source_target_pairs={{0,4},{1,5},{2,6},{3,7},{4,0},{5,1},{6,2},{7,3},{8,12},{9,13},{10,... | collective-permute-start | bytes 835592 | tf_op jit(solution)/shard_map/ppermute | solution.py:343
  60.3 15.2 %collective-permute-start.25 = (bf16[64,2176]{1,0:T(8,128)(2,1)S(1)}, bf16[64,2176]{1,0:T(8,128)(2,1)S(1)}, u32[]{:S(2)}, u32[]{:S(2)}) collective-permute-start(bf16[64,2176]{1,0:T(8,128)(2,1)S(1)} %fusion.1), channel_id=1, source_target_pairs={{0,8},{1,9},{2,10},{3,11},{4,12},{5,13},{6,14},{7,15},{8,24},{9,25... | collective-permute-start | bytes 835592 | tf_op jit(solution)/shard_map/ppermute | solution.py:343
  66.9 8.7 %collective-permute-start.24 = (bf16[64,2176]{1,0:T(8,128)(2,1)S(1)}, bf16[64,2176]{1,0:T(8,128)(2,1)S(1)}, u32[]{:S(2)}, u32[]{:S(2)}) collective-permute-start(bf16[64,2176]{1,0:T(8,128)(2,1)S(1)} %slice_add_fusion.2), channel_id=1, source_target_pairs={{0,16},{1,17},{2,18},{3,19},{4,20},{5,21},{6,22},{7,23},{8,0},{9,1... | collective-permute-start | bytes 835592 | tf_op jit(solution)/shard_map/ppermute | solution.py:343
  68.9 7.7 %collective-permute-start.23 = (bf16[64,2176]{1,0:T(8,128)(2,1)S(1)}, bf16[64,2176]{1,0:T(8,128)(2,1)S(1)}, u32[]{:S(2)}, u32[]{:S(2)}) collective-permute-start(bf16[64,2176]{1,0:T(8,128)(2,1)S(1)} %slice.81), channel_id=1, source_target_pairs={{0,4},{1,5},{2,6},{3,7},{4,0},{5,1},{6,2},{7,3},{8,12},{9,13},{10,... | collective-permute-start | bytes 835592 | tf_op jit(solution)/shard_map/ppermute | solution.py:343
  76.7 7.4 %collective-permute-start.27 = (bf16[64,2176]{1,0:T(8,128)(2,1)S(1)}, bf16[64,2176]{1,0:T(8,128)(2,1)S(1)}, u32[]{:S(2)}, u32[]{:S(2)}) collective-permute-start(bf16[64,2176]{1,0:T(8,128)(2,1)S(1)} %slice.80), channel_id=1, source_target_pairs={{0,4},{1,5},{2,6},{3,7},{4,0},{5,1},{6,2},{7,3},{8,12},{9,13},{10,... | collective-permute-start | bytes 835592 | tf_op jit(solution)/shard_map/ppermute | solution.py:343
  77.5 6.6 %collective-permute-start.26 = (bf16[64,2176]{1,0:T(8,128)(2,1)S(1)}, bf16[64,2176]{1,0:T(8,128)(2,1)S(1)}, u32[]{:S(2)}, u32[]{:S(2)}) collective-permute-start(bf16[64,2176]{1,0:T(8,128)(2,1)S(1)} %fusion), channel_id=1, source_target_pairs={{0,16},{1,17},{2,18},{3,19},{4,20},{5,21},{6,22},{7,23},{8,0},{9,1... | collective-permute-start | bytes 835592 | tf_op jit(solution)/shard_map/ppermute | solution.py:343
  84.3 7.6 %collective-permute-start.28 = (bf16[64,2176]{1,0:T(8,128)(2,1)S(1)}, bf16[64,2176]{1,0:T(8,128)(2,1)S(1)}, u32[]{:S(2)}, u32[]{:S(2)}) collective-permute-start(bf16[64,2176]{1,0:T(8,128)(2,1)S(1)} %fusion.4), channel_id=1, source_target_pairs={{0,2},{1,3},{2,0},{3,1},{4,6},{5,7},{6,4},{7,5},{8,10},{9,11},{10,... | collective-permute-start | bytes 835592 | tf_op jit(solution)/shard_map/ppermute | solution.py:343
  (27 other events, 101.9 us)
